TPU v7x, 256 devices: a whole 4x4x8 slice. The times are simulated.
256 devices in a mesh: dp: 32 (over x, y, core), tensor: 8 (over z).
Axes of the slice: x: 4, y: 4, z: 8, core: 2. Of those that a mesh axis runs over, the one named last changes fastest.
Arguments:
- gradients: bfloat16 [32, 2, 320, 14336], P('dp', None, None, 'tensor'), may hold values from -6 to 6
- feedback: float32 [32, 2, 320, 14336], P('dp', None, None, 'tensor'), may hold values from -4 to 4
- seed_value: int32 [1], replicated, may hold values from 0 to 29999
Outputs:
- new_feedback: float32 [32, 2, 320, 14336], P('dp', None, None, 'tensor')
- left_basis: float32 [2, 320, 128], replicated
- right_factor: float32 [2, 14336, 128], P(None, 'tensor')
All inputs are finite; a program needn't handle non-finite values.
Results may differ from a plain program's by a relative error of at most 0.0003.
Values sent between devices are 32-bit elements; how exact they have to be, the bound alone decides.
No kernel may reach another device: no remote copies, remote signals or barrier semaphores. Data moves between devices by JAX's collectives and lax.ppermute only.
A program may use at most 64 MiB of HBM per device.

v0:
```python
import jax
import jax.numpy as jnp
from jax import lax
from jax.sharding import PartitionSpec as P

RANK = 128


unit_scale = 3.4641016


def start_factor(seed_scalar, col_start, columns, rank_count):
    col_ids = col_start + jnp.arange(columns, dtype=jnp.int32)[:, None]
    rank_ids = jnp.arange(rank_count, dtype=jnp.int32)[None, :]
    hashed = (col_ids * 131 + rank_ids * 977 + seed_scalar) % 32749
    hashed = (hashed * hashed + rank_ids * 17 + 7) % 32749
    hashed = (hashed * hashed + col_ids) % 32749
    return (hashed.astype(jnp.float32) / 32749.0 - 0.5) * unit_scale


def solve_basis(left_rows, factor_low):
    return lax.linalg.triangular_solve(
        factor_low, left_rows, left_side=False, lower=True, transpose_a=True
    )


def on_device(gradients, feedback, seed_value):
    highest = lax.Precision.HIGHEST
    columns = gradients.shape[3]
    replicas = lax.axis_size("dp")
    col_start = lax.axis_index("tensor") * columns
    start_right = start_factor(seed_value[0], col_start, columns, RANK)
    summed_in = gradients[0].astype(jnp.float32) + feedback[0]
    left_part = jnp.einsum("mrc,ck->mrk", summed_in, start_right, precision=highest)
    left_sum = lax.psum(left_part, ("dp", "tensor")) / replicas
    gram_sums = jnp.einsum("mrk,mrj->mkj", left_sum, left_sum, precision=highest)
    factor_low = jnp.linalg.cholesky(gram_sums)
    left_basis = solve_basis(left_sum, factor_low)
    right_local = jnp.einsum("mrc,mrk->mck", summed_in, left_basis, precision=highest)
    right_factor = lax.psum(right_local, "dp") / replicas
    rebuilt = jnp.einsum("mrk,mck->mrc", left_basis, right_factor, precision=highest)
    new_feedback = summed_in - rebuilt
    return (new_feedback[None], left_basis, right_factor)


def solution(mesh):
    placed = (P("dp", None, None, "tensor"), P("dp", None, None, "tensor"), P())
    return jax.shard_map(
        on_device,
        mesh=mesh,
        in_specs=placed,
        out_specs=(P("dp", None, None, "tensor"), P(), P(None, "tensor", None)),
        check_vma=False,
    )
```

profile of v0, /device:TPU:1, one launch (start us, length us, event | category | flops | bytes accessed | tf_op | source)
XLA Modules:
  0.0 456.4 jit_solution(10966978682709938940)
XLA Ops:
  7.2 0.0 all-reduce.3.cloned.1.call-start
  7.9 0.0 copy-start
  7.9 9.6 %fusion.2 = f32[2,320,128]{2,1,0:T(8,128)} fusion(f32[1,2,320,1792]{3,2,1,0:T(8,128)} %param.4, bf16[1,2,320,1792]{3,2,1,0:T(8,128)(2,1)} %param.3, s32[1792]{0:T(1024)S(1)} %get-tuple-element.3, s32[128]{0:T(128)S(1)} %get-tuple-element.5, s32[]{:T(128)} %bitcast.26, s32[128]{0:T(128)S(1)} %get-tuple-element.6, s32[1792]{0:T(1024)S(1)} %get-tuple-element.4), kind=kOutput, calls=%fused_computation.3 | convolution fusion | flops 1770553344 | bytes 7224324 | tf_op jit(solution)/shard_map/mrc,ck->mrk/dot_general | solution.py:34
  17.5 0.0 all-reduce.3.cloned.1.call-update
  17.5 0.0 all-reduce.5.cloned.1.call-start
  17.6 249.8 %all-reduce.3.cloned.1.call-done = f32[2,320,128]{2,1,0:T(8,128)} async-done(((f32[2,320,128]{2,1,0:T(8,128)}), f32[2,320,128]{2,1,0:T(8,128)}) %all-reduce.3.cloned.1.call-update) | async-done | bytes 327696 | tf_op jit(solution)/shard_map/psum | solution.py:35
  267.5 1.9 fusion.42
  269.4 0.1 copy.8
  269.5 23.6 %custom-call.7 = f32[2,128,128]{2,1,0:T(8,128)S(1)} custom-call(f32[2,128,128]{2,1,0:T(8,128)S(1)} %fusion.47), custom_call_target="Cholesky" | custom-call | tf_op jit(solution)/shard_map/jit(cholesky)/cholesky | solution.py:37
  293.2 0.1 compare_reduce_fusion
  293.3 0.1 select_bitcast_fusion
  293.4 19.7 %custom-call.8 = f32[2,1,128,128]{2,3,1,0:T(8,128)S(1)} custom-call(f32[2,1,128,128]{3,2,1,0:T(8,128)S(1)} %select_bitcast_fusion), custom_call_target="InvertDiagBlocksLowerTriangular" | custom-call | tf_op jit(solution)/shard_map/triangular_solve | solution.py:22
  313.1 1.4 fusion.40
  314.5 0.0 copy-done
  314.5 0.0 copy-start.2
  314.5 11.7 %fusion = f32[2,1792,128]{2,1,0:T(8,128)} fusion(f32[2,320,128]{2,1,0:T(8,128)S(1)} %fusion.40, f32[1,2,320,1792]{3,2,1,0:T(8,128)} %param.4, bf16[1,2,320,1792]{3,2,1,0:T(8,128)(2,1)S(1)} %copy-done), kind=kOutput, calls=%fused_computation.1 | convolution fusion | flops 1763901440 | bytes 9043968 | tf_op jit(solution)/shard_map/mrc,mrk->mck/dot_general | solution.py:39
  326.3 0.0 all-reduce.5.cloned.1.call-update
  326.3 113.9 %all-reduce.5.cloned.1.call-done = f32[2,1792,128]{2,1,0:T(8,128)} async-done(((f32[2,1792,128]{2,1,0:T(8,128)}), f32[2,1792,128]{2,1,0:T(8,128)}) %all-reduce.5.cloned.1.call-update) | async-done | bytes 1835024 | tf_op jit(solution)/shard_map/psum | solution.py:40
  440.2 1.6 broadcast_multiply_fusion
  441.8 0.0 copy-done.2
  441.8 0.0 copy-start.1
  441.8 7.7 %fusion.4 = f32[1,2,320,1792]{3,2,1,0:T(8,128)} fusion(f32[2,320,128]{2,1,0:T(8,128)S(1)} %fusion.40, f32[2,1792,128]{2,1,0:T(8,128)S(1)} %broadcast_multiply_fusion, f32[1,2,320,1792]{3,2,1,0:T(8,128)} %param.4, bf16[1,2,320,1792]{3,2,1,0:T(8,128)(2,1)S(1)} %copy-done), kind=kOutput, calls=%fused_computation.5 | convolution fusion | flops 1765048320 | bytes 13631488 | tf_op jit(solution)/shard_map/mrk,mck->mrc/dot_general | solution.py:41
  449.5 0.0 copy-done.1
  (6 shorter events, 0.1 us)
Async XLA Ops:
  7.2 260.3 %all-reduce.3.cloned.1.call-start = ((), (), s32[]{:S(2)}) async-start(), calls=%async_computation | async-start | bytes 655360 | tf_op jit(solution)/shard_map/psum | solution.py:35
  7.9 306.6 %copy-start = (bf16[1,2,320,1792]{3,2,1,0:T(8,128)(2,1)S(1)}, bf16[1,2,320,1792]{3,2,1,0:T(8,128)(2,1)}, u32[]{:S(2)}) copy-start(bf16[1,2,320,1792]{3,2,1,0:T(8,128)(2,1)} %param.3) | copy-start | bytes 6881284
  17.5 422.6 %all-reduce.5.cloned.1.call-start = ((), (), s32[]{:S(2)}) async-start(), calls=%async_computation.1 | async-start | bytes 3670016 | tf_op jit(solution)/shard_map/psum | solution.py:40
  314.5 127.3 %copy-start.2 = (f32[2,320,128]{2,1,0:T(8,128)}, f32[2,320,128]{2,1,0:T(8,128)S(1)}, u32[]{:S(2)}) copy-start(f32[2,320,128]{2,1,0:T(8,128)S(1)} %fusion.40) | copy-start | bytes 983044
  441.8 7.7 %copy-start.1 = (f32[2,1792,128]{2,1,0:T(8,128)}, f32[2,1792,128]{2,1,0:T(8,128)S(1)}, u32[]{:S(2)}) copy-start(f32[2,1792,128]{2,1,0:T(8,128)S(1)} %broadcast_multiply_fusion) | copy-start | bytes 5505028
Sparse Core Ops, SparseCore 0:
  17.7 249.7 all-reduce.2
  326.4 113.7 all-reduce.4
where the time goes:
time: 457 us; the launch traced here: 456 us
  waiting for transfers between devices  364 us (80%)
  other arithmetic  45.2 us (10%)
  matrix products  32.4 us (7%)
  between operations  14.8 us (3%)
    psum x1, waiting for transfers between devices, on_device(): left_sum = lax.psum(left_part, ('dp', 'tensor')) / replicas  250 us
    psum x1, waiting for transfers between devices, on_device(): right_factor = lax.psum(right_local, 'dp') / replicas  114 us
    another operation x4, other arithmetic, on_device(): factor_low = jnp.linalg.cholesky(gram_sums)  23.8 us
    another operation x3, other arithmetic, solve_basis(): lax.linalg.triangular_solve(factor_low, left_rows, left_side=False, lower...  19.8 us
    dot_general x1, matrix products, on_device(): jnp.einsum('mrc,mrk->mck', summed_in, left_basis, precision=highest)  11.7 us
    dot_general x1, matrix products, on_device(): jnp.einsum('mrc,ck->mrk', summed_in, start_right, precision=highest)  9.61 us
  transfers between devices with their start and end apart: 2, of which 2 were waited for; matrix products, arithmetic and copies ran while one was open for 0% of the time, Pallas kernels for 0%

commit v1 on v0

v1 whole, which is shorter than its diff:
```python
import functools

import jax
import jax.numpy as jnp
from jax import lax
from jax.experimental import pallas as pl
from jax.experimental.pallas import tpu as pltpu
from jax.sharding import Mesh, PartitionSpec as P

RANK = 128
PRIME = 32749
SIDE = 4
CORES = 2
CHUNK = 256

unit_scale = 3.4641016
f32 = jnp.float32
bf16 = jnp.bfloat16


def split(x):
    high = x.astype(bf16)
    return high, (x - high.astype(f32)).astype(bf16)


def dot(a, b, contract=((1,), (0,))):
    return lax.dot_general(a, b, (contract, ((), ())), preferred_element_type=f32)


def exact_dot(a, b, contract):
    return lax.dot_general(
        a, b, (contract, ((), ())), precision=lax.Precision.HIGHEST, preferred_element_type=f32
    )


def modulo(x):
    quotient = (x.astype(f32) * (0.999999 / PRIME)).astype(jnp.int32)
    rest = x - quotient * PRIME
    return jnp.where(rest >= PRIME, rest - PRIME, rest)


def start_block(seed, first, columns):
    col = first + lax.broadcasted_iota(jnp.int32, (columns, RANK), 0)
    rank = lax.broadcasted_iota(jnp.int32, (columns, RANK), 1)
    hashed = modulo(col * 131 + rank * 977 + seed)
    hashed = modulo(hashed * hashed + rank * 17 + 7)
    hashed = modulo(hashed * hashed + col)
    return (hashed.astype(f32) * (1.0 / PRIME) - 0.5) * unit_scale


def left_kernel(where_ref, grad_ref, feed_ref, out_ref):
    step = pl.program_id(0)
    seed, first, core = where_ref[0], where_ref[1], where_ref[2]
    start = start_block(seed, first + step * CHUNK, CHUNK)
    high, low = split(start)
    both = jnp.concatenate([high, low], axis=1)
    for m in range(2):
        s_high, s_low = split(grad_ref[m].astype(f32) + feed_ref[m])
        wide = dot(s_high, both)
        part = wide[:, :RANK] + wide[:, RANK:] + dot(s_low, high)
        slot = m ^ core

        @pl.when(step == 0)
        def _():
            out_ref[slot] = part

        @pl.when(step > 0)
        def _():
            out_ref[slot] += part


def basis_kernel(left_ref, basis_ref):
    left = left_ref[...] * (1.0 / 32)
    gram = exact_dot(left, left, ((0,), (0,)))
    lane = lax.broadcasted_iota(jnp.int32, (1, RANK), 1)
    rows8 = lax.broadcasted_iota(jnp.int32, (8, RANK), 0)
    blocks = [gram[8 * b : 8 * b + 8, :] for b in range(RANK // 8)]
    pivots = []
    for j in range(RANK):
        at = lane == j
        bj, sj = j // 8, j % 8
        row = blocks[bj][sj : sj + 1, :]
        pivot = jnp.broadcast_to(row[:, j : j + 1], (1, RANK))
        pivots.append(pivot)
        inverse = 1.0 / pivot
        row = jnp.where(at, 1.0, row)
        for b in range(bj, RANK // 8):
            block = blocks[b]
            factor = jnp.broadcast_to(block[:, j : j + 1], (8, RANK)) * inverse
            kept = jnp.where(at, 0.0, block)
            if b == bj:
                if sj == 7:
                    continue
                blocks[b] = jnp.where(rows8 > sj, kept - factor * row, block)
            else:
                blocks[b] = kept - factor * row
    lower = jnp.concatenate(blocks, axis=0)
    i = lax.broadcasted_iota(jnp.int32, (RANK, RANK), 0)
    j = lax.broadcasted_iota(jnp.int32, (RANK, RANK), 1)
    scale = lax.rsqrt(jnp.concatenate(pivots, axis=0))
    inverse = jnp.where(i > j, lower, jnp.where(i == j, 1.0, 0.0)) * scale
    basis_ref[...] = exact_dot(left, inverse, ((1,), (1,)))


def right_kernel(where_ref, mine_ref, other_ref, grad_ref, feed_ref, out_ref, basis_ref, wide_ref):
    core = where_ref[2]

    @pl.when(pl.program_id(0) == 0)
    def _():
        for m in range(2):
            basis = jnp.where(core == m, mine_ref[...], other_ref[...])
            basis_ref[m] = basis
            flipped = basis.T
            high, low = split(flipped)
            wide_ref[m, :RANK, :] = high
            wide_ref[m, RANK:, :] = low

    for m in range(2):
        s_high, s_low = split(grad_ref[m].astype(f32) + feed_ref[m])
        wide = dot(wide_ref[m], s_high)
        part = wide[:RANK] + wide[RANK:] + dot(wide_ref[m, :RANK, :], s_low)
        out_ref[m ^ core] = part


def update_kernel(where_ref, basis_ref, mine_ref, other_ref, grad_ref, feed_ref, out_ref, right_ref, wide_ref):
    core = where_ref[2]

    @pl.when(pl.program_id(0) == 0)
    def _():
        for m in range(2):
            high, low = split(basis_ref[m])
            wide_ref[m, :, :RANK] = high
            wide_ref[m, :, RANK:] = low

    for m in range(2):
        right = jnp.where(core == m, mine_ref[...], other_ref[...])
        right_ref[m] = right.T
        high, low = split(right)
        rebuilt = dot(wide_ref[m], jnp.concatenate([high, high], axis=0)) + dot(wide_ref[m, :, :RANK], low)
        out_ref[m] = grad_ref[m].astype(f32) + feed_ref[m] - rebuilt


def params(**more):
    return pltpu.CompilerParams(dimension_semantics=("arbitrary",), vmem_limit_bytes=40 * 1024 * 1024)


def whole(*shape):
    return pl.BlockSpec(shape, lambda i: (0,) * len(shape))


def spread(x, axes, count):
    return lax.all_to_all(jnp.broadcast_to(x[None], (count,) + x.shape), axes, 0, 0)


def swap(x):
    return lax.ppermute(x, "core", [(0, 1), (1, 0)])


def on_device(gradients, feedback, seed_value):
    gradients, feedback = gradients[0], feedback[0]
    mats, rows, columns = gradients.shape
    chips = SIDE * SIDE
    depth = lax.axis_size("z")
    core = lax.axis_index("core")
    where = jnp.stack([seed_value[0], lax.axis_index("z") * columns, core]).astype(jnp.int32)
    steps = columns // CHUNK
    smem = pl.BlockSpec(memory_space=pltpu.SMEM)
    wide_spec = pl.BlockSpec((mats, rows, CHUNK), lambda i: (0, 0, i))

    left_part = pl.pallas_call(
        left_kernel,
        grid=(steps,),
        in_specs=[smem, wide_spec, wide_spec],
        out_specs=whole(mats, rows, RANK),
        out_shape=jax.ShapeDtypeStruct((mats, rows, RANK), f32),
        compiler_params=params(),
        name="left_part",
    )(where, gradients, feedback)

    left = left_part[0] + swap(left_part[1])
    left = lax.all_to_all(left.reshape(chips, rows // chips, RANK), ("x", "y"), 0, 0).sum(0)
    left = spread(left, "z", depth).sum(0)
    left = spread(left, ("x", "y"), chips).reshape(rows, RANK)

    basis_mine = pl.pallas_call(
        basis_kernel,
        out_shape=jax.ShapeDtypeStruct((rows, RANK), f32),
        compiler_params=pltpu.CompilerParams(vmem_limit_bytes=40 * 1024 * 1024),
        name="basis",
    )(left)
    basis_other = swap(basis_mine)

    right_part, left_basis = pl.pallas_call(
        right_kernel,
        grid=(steps,),
        in_specs=[smem, whole(rows, RANK), whole(rows, RANK), wide_spec, wide_spec],
        out_specs=[pl.BlockSpec((mats, RANK, CHUNK), lambda i: (0, 0, i)), whole(mats, rows, RANK)],
        out_shape=[
            jax.ShapeDtypeStruct((mats, RANK, columns), f32),
            jax.ShapeDtypeStruct((mats, rows, RANK), f32),
        ],
        scratch_shapes=[pltpu.VMEM((mats, 2 * RANK, rows), bf16)],
        compiler_params=params(),
        name="right_part",
    )(where, basis_mine, basis_other, gradients, feedback)

    right = right_part[0] + swap(right_part[1])
    right = lax.all_to_all(right.reshape(chips, RANK // chips, columns), ("x", "y"), 0, 0).sum(0) * (1.0 / 32)
    right_mine = spread(right, ("x", "y"), chips).reshape(RANK, columns)
    right_other = swap(right_mine)

    flat_spec = pl.BlockSpec((RANK, CHUNK), lambda i: (0, i))
    new_feedback, right_factor = pl.pallas_call(
        update_kernel,
        grid=(steps,),
        in_specs=[smem, whole(mats, rows, RANK), flat_spec, flat_spec, wide_spec, wide_spec],
        out_specs=[wide_spec, pl.BlockSpec((mats, CHUNK, RANK), lambda i: (0, i, 0))],
        out_shape=[
            jax.ShapeDtypeStruct((mats, rows, columns), f32),
            jax.ShapeDtypeStruct((mats, columns, RANK), f32),
        ],
        scratch_shapes=[pltpu.VMEM((mats, rows, 2 * RANK), bf16)],
        compiler_params=params(),
        name="update",
    )(where, left_basis, right_mine, right_other, gradients, feedback)
    return new_feedback[None], left_basis, right_factor


def solution(mesh):
    fine = Mesh(mesh.devices.reshape(SIDE, SIDE, CORES, -1), ("x", "y", "core", "z"))
    dp = ("x", "y", "core")
    placed = (P(dp, None, None, "z"), P(dp, None, None, "z"), P())
    return jax.shard_map(
        on_device,
        mesh=fine,
        in_specs=placed,
        out_specs=(P(dp, None, None, "z"), P(), P(None, "z", None)),
        check_vma=False,
    )
```

time: 457 us -> 131 us (0.29)
  waiting for transfers between devices: 364 us -> 6.26 us
  blocking collectives: 0 us -> 72 us
  other arithmetic: 45.2 us -> 1.72 us
  matrix products: 32.4 us -> 0 us
  Pallas kernels: 0 us -> 28.4 us
  between operations: 14.8 us -> 1.37 us
  starting transfers between devices: 0.08 us -> 11.7 us
  local copies, waits for them, and re-layouts: 0.11 us -> 8.74 us
    psum x2 -> x0, waiting for transfers between devices: 364 us -> none  [the longest x1 250 us: on_device(): left_sum = lax.psum(left_part, ('dp', 'tensor')) / replicas]
    all_to_all x0 -> x5, blocking collectives: none -> 72 us  [the longest x3 42.8 us: spread(): lax.all_to_all(jnp.broadcast_to(x[None], (count,) + x.shape), axes, 0, 0)]
    another operation x7 -> x1, other arithmetic: 43.6 us -> 0.08 us  [on_device(): jnp.stack([seed_value[0], lax.axis_index('z') * columns, core])]
    dot_general x4 -> x0, matrix products: 31 us -> none  [the longest x1 11.7 us: on_device(): jnp.einsum('mrc,mrk->mck', summed_in, left_basis, precision=highest)]
    pallas_call x0 -> x4, Pallas kernels: none -> 28.4 us  [the longest x1 11.4 us: on_device(): pl.pallas_call(basis_kernel, out_shape=jax.ShapeDtypeStruct((rows, RANK),...]
    ppermute x0 -> x4, starting transfers between devices: none -> 11.7 us  [swap(): return lax.ppermute(x, 'core', [(0, 1), (1, 0)])]
    unnamed x6 -> x12, local copies, waits for them, and re-layouts: 0.02 us -> 8.56 us
    ppermute x0 -> x4, waiting for transfers between devices: none -> 6.26 us  [swap(): return lax.ppermute(x, 'core', [(0, 1), (1, 0)])]
  transfers between devices with their start and end apart: 2 -> 4, of which waited for: 2 -> 4; matrix products, arithmetic and copies ran while one was open for 0% -> 0% of each run, Pallas kernels for 0% -> 0%
where the time goes in v1:
time: 131 us; the launch traced here: 130 us
  blocking collectives  72 us (55%)
  Pallas kernels  28.4 us (22%)
  starting transfers between devices  11.7 us (9%)
  local copies, waits for them, and re-layouts  8.74 us (7%)
  waiting for transfers between devices  6.26 us (5%)
  other arithmetic  1.72 us (1%)
  between operations  1.37 us (1%)
    all_to_all x3, blocking collectives, spread(): lax.all_to_all(jnp.broadcast_to(x[None], (count,) + x.shape), axes, 0, 0)  42.8 us
    all_to_all x1, blocking collectives, on_device(): lax.all_to_all(right.reshape(chips, RANK // chips, columns), ('x', 'y'),...  17.3 us
    all_to_all x1, blocking collectives, on_device(): lax.all_to_all(left.reshape(chips, rows // chips, RANK), ('x', 'y'), 0, 0)  11.9 us
    ppermute x4, starting transfers between devices, swap(): return lax.ppermute(x, 'core', [(0, 1), (1, 0)])  11.7 us
    pallas_call x1, Pallas kernels, on_device(): pl.pallas_call(basis_kernel, out_shape=jax.ShapeDtypeStruct((rows, RANK),...  11.4 us
    unnamed x12, local copies, waits for them, and re-layouts  8.56 us
    ppermute x4, waiting for transfers between devices, swap(): return lax.ppermute(x, 'core', [(0, 1), (1, 0)])  6.26 us
    pallas_call x1, Pallas kernels, on_device(): pl.pallas_call(left_kernel, grid=(steps,), in_specs=[smem, wide_spec, wid...  6.06 us
  transfers between devices with their start and end apart: 4, of which 4 were waited for; matrix products, arithmetic and copies ran while one was open for 0% of the time, Pallas kernels for 0%

profile of v1, /device:TPU:1, one launch (start us, length us, event | category | flops | bytes accessed | tf_op | source)
XLA Modules:
  0.0 130.2 jit_solution(3623609007355369222)
XLA Ops:
  1.3 0.1 pad_add_fusion.where_ref
  1.4 0.0 copy-start
  1.4 2.3 %copy-done = f32[1,2,320,1792]{3,2,1,0:T(8,128)S(1)} copy-done((f32[1,2,320,1792]{3,2,1,0:T(8,128)S(1)}, f32[1,2,320,1792]{3,2,1,0:T(8,128)}, u32[]{:S(2)}) %copy-start) | copy-done | bytes 4587544
  3.7 0.0 copy-start.3
  3.7 1.6 %copy-done.3 = bf16[1,2,320,1792]{3,2,1,0:T(8,128)(2,1)S(1)} copy-done((bf16[1,2,320,1792]{3,2,1,0:T(8,128)(2,1)S(1)}, bf16[1,2,320,1792]{3,2,1,0:T(8,128)(2,1)}, u32[]{:S(2)}) %copy-start.3) | copy-done | bytes 2293784
  5.3 6.1 %left_part.1 = f32[2,320,128]{2,1,0:T(8,128)S(1)} custom-call(s32[3]{0:T(128)S(1)} %pad_add_fusion.where_ref, bf16[2,320,1792]{2,1,0:T(8,128)(2,1)S(1)} %bitcast.23, f32[2,320,1792]{2,1,0:T(8,128)S(1)} %bitcast.20), custom_call_target="tpu_custom_call" | custom-call | tf_op jit(solution)/shard_map/left_part/pallas_call | solution.py:170
  11.4 0.0 copy-start.4
  11.4 3.3 %collective-permute-start = (f32[320,128]{1,0:T(8,128)S(1)}, f32[320,128]{1,0:T(8,128)S(1)}, u32[]{:S(2)}, u32[]{:S(2)}) collective-permute-start(f32[320,128]{1,0:T(8,128)S(1)} %slice_bitcast_fusion.1), channel_id=1, source_target_pairs={{0,8},{8,0},{1,9},{9,1},{2,10},{10,2},{3,11},{11,3},{4,12},{12,4},... | collective-permute-start | bytes 491528 | tf_op jit(solution)/shard_map/ppermute | solution.py:156
  14.7 1.0 collective-permute-done
  15.8 11.9 %all_to_all.25 = f32[16,20,128]{2,1,0:T(8,128)S(1)} all-to-all(f32[16,20,128]{2,1,0:T(8,128)S(1)} %reshape.23), channel_id=1, replica_groups=mesh['x'=4,'y'=4,'core'=2,'z'=8] {'x','y'}, dimensions={0} | all-to-all | bytes 327680 | tf_op jit(solution)/shard_map/all_to_all | solution.py:181
  27.7 15.7 %all_to_all.26 = f32[8,20,128]{2,1,0:T(8,128)S(1)} all-to-all(f32[8,20,128]{2,1,0:T(8,128)S(1)} %broadcast_in_dim.8), channel_id=1, replica_groups=mesh['x'=4,'y'=4,'core'=2,'z'=8] {'z'}, dimensions={0} | all-to-all | bytes 163840 | tf_op jit(solution)/shard_map/all_to_all | solution.py:152
  43.4 10.3 %all_to_all.27 = f32[16,20,128]{2,1,0:T(8,128)S(1)} all-to-all(f32[16,20,128]{2,1,0:T(8,128)S(1)} %broadcast_in_dim.9), channel_id=1, replica_groups=mesh['x'=4,'y'=4,'core'=2,'z'=8] {'x','y'}, dimensions={0} | all-to-all | bytes 327680 | tf_op jit(solution)/shard_map/all_to_all | solution.py:152
  53.7 11.4 %basis.1.mine_ref = f32[320,128]{1,0:T(8,128)S(1)} custom-call(f32[320,128]{1,0:T(8,128)S(1)} %reshape.24.left_ref), custom_call_target="tpu_custom_call" | custom-call | tf_op jit(solution)/shard_map/basis/pallas_call | solution.py:185
  65.2 4.4 %collective-permute-start.1 = (f32[320,128]{1,0:T(8,128)S(1)}, f32[320,128]{1,0:T(8,128)S(1)}, u32[]{:S(2)}, u32[]{:S(2)}) collective-permute-start(f32[320,128]{1,0:T(8,128)S(1)} %basis.1.mine_ref), channel_id=1, source_target_pairs={{0,8},{8,0},{1,9},{9,1},{2,10},{10,2},{3,11},{11,3},{4,12},{12,4},... | collective-permute-start | bytes 491528 | tf_op jit(solution)/shard_map/ppermute | solution.py:156
  69.6 1.0 collective-permute-done.1.other_ref
  70.6 0.0 copy-done.4
  70.6 0.0 copy-start.1
  70.6 2.3 %copy-done.1 = f32[1,2,320,1792]{3,2,1,0:T(8,128)S(1)} copy-done((f32[1,2,320,1792]{3,2,1,0:T(8,128)S(1)}, f32[1,2,320,1792]{3,2,1,0:T(8,128)}, u32[]{:S(2)}) %copy-start.1) | copy-done | bytes 4587544
  72.9 5.0 %right_part.1 = (f32[2,128,1792]{2,1,0:T(8,128)S(1)}, f32[2,320,128]{2,1,0:T(8,128)}) custom-call(s32[3]{0:T(128)S(1)} %pad_add_fusion.where_ref, f32[320,128]{1,0:T(8,128)S(1)} %basis.1.mine_ref, f32[320,128]{1,0:T(8,128)S(1)} %collective-permute-done.1.other_ref, bf16[2,320,1792]{2,1,0:T(8,128)(2,1)S(1)} %bitcast.24, f32[2,320,1792]{2,1,0:T(8,128)S(1)} %bitcast.21), custom_call_target="tpu_custom_call" | custom-call | tf_op jit(solution)/shard_map/right_part/pallas_call | solution.py:193
  77.9 0.1 slice_bitcast_fusion
  77.9 0.5 collective-permute-start.2
  78.4 2.1 %collective-permute-done.2 = f32[128,1792]{1,0:T(8,128)S(1)} collective-permute-done((f32[128,1792]{1,0:T(8,128)S(1)}, f32[128,1792]{1,0:T(8,128)S(1)}, u32[]{:S(2)}, u32[]{:S(2)}) %collective-permute-start.2) | collective-permute-done | bytes 917536 | tf_op jit(solution)/shard_map/ppermute | solution.py:156
  80.5 0.1 fusion
  80.6 17.3 %all_to_all.28 = f32[16,8,1792]{2,1,0:T(8,128)S(1)} all-to-all(f32[16,8,1792]{2,1,0:T(8,128)S(1)} %fusion), channel_id=1, replica_groups=mesh['x'=4,'y'=4,'core'=2,'z'=8] {'x','y'}, dimensions={0} | all-to-all | bytes 1835008 | tf_op jit(solution)/shard_map/all_to_all | solution.py:208
  97.9 0.0 copy-start.5
  97.9 0.7 reduce_sum.29
  98.6 0.8 broadcast_multiply_fusion
  99.4 0.1 broadcast_in_dim.10
  99.5 16.9 %all_to_all.29 = f32[16,8,1792]{2,1,0:T(8,128)S(1)} all-to-all(f32[16,8,1792]{2,1,0:T(8,128)S(1)} %broadcast_in_dim.10), channel_id=1, replica_groups=mesh['x'=4,'y'=4,'core'=2,'z'=8] {'x','y'}, dimensions={0} | all-to-all | bytes 1835008 | tf_op jit(solution)/shard_map/all_to_all | solution.py:152
  116.4 3.5 %collective-permute-start.3 = (f32[128,1792]{1,0:T(8,128)S(1)}, f32[128,1792]{1,0:T(8,128)S(1)}, u32[]{:S(2)}, u32[]{:S(2)}) collective-permute-start(f32[128,1792]{1,0:T(8,128)S(1)} %bitcast.26), channel_id=1, source_target_pairs={{0,8},{8,0},{1,9},{9,1},{2,10},{10,2},{3,11},{11,3},{4,12},{12,4},... | collective-permute-start | bytes 2752520 | tf_op jit(solution)/shard_map/ppermute | solution.py:156
  119.9 2.1 %collective-permute-done.3.other_ref = f32[128,1792]{1,0:T(8,128)S(1)} collective-permute-done((f32[128,1792]{1,0:T(8,128)S(1)}, f32[128,1792]{1,0:T(8,128)S(1)}, u32[]{:S(2)}, u32[]{:S(2)}) %collective-permute-start.3) | collective-permute-done | bytes 917536 | tf_op jit(solution)/shard_map/ppermute | solution.py:156
  122.0 0.0 copy-done.5
  122.0 0.0 copy-start.2
  122.0 2.3 %copy-done.2 = f32[1,2,320,1792]{3,2,1,0:T(8,128)S(1)} copy-done((f32[1,2,320,1792]{3,2,1,0:T(8,128)S(1)}, f32[1,2,320,1792]{3,2,1,0:T(8,128)}, u32[]{:S(2)}) %copy-start.2) | copy-done | bytes 4587544
  124.3 5.9 %update.1 = (f32[2,320,1792]{2,1,0:T(8,128)}, f32[2,1792,128]{2,1,0:T(8,128)}) custom-call(s32[3]{0:T(128)S(1)} %pad_add_fusion.where_ref, f32[2,320,128]{2,1,0:T(8,128)S(1)} %copy-done.5, f32[128,1792]{1,0:T(8,128)S(1)} %bitcast.27, f32[128,1792]{1,0:T(8,128)S(1)} %collective-permute-done.3.other_ref, bf16[2,320,1792]{2,1,0:T(8,128)(2,1)S(1)} %bitcast.25, ...), custom_call_target="tpu_custom_call" | custom-call | tf_op jit(solution)/shard_map/update/pallas_call | solution.py:213
  (8 shorter events, 0.1 us)
Async XLA Ops:
  1.4 2.3 %copy-start = (f32[1,2,320,1792]{3,2,1,0:T(8,128)S(1)}, f32[1,2,320,1792]{3,2,1,0:T(8,128)}, u32[]{:S(2)}) copy-start(f32[1,2,320,1792]{3,2,1,0:T(8,128)} %param.4) | copy-start | bytes 13762564
  3.7 1.6 %copy-start.3 = (bf16[1,2,320,1792]{3,2,1,0:T(8,128)(2,1)S(1)}, bf16[1,2,320,1792]{3,2,1,0:T(8,128)(2,1)}, u32[]{:S(2)}) copy-start(bf16[1,2,320,1792]{3,2,1,0:T(8,128)(2,1)} %param.3) | copy-start | bytes 6881284
  11.4 59.2 %copy-start.4 = (bf16[1,2,320,1792]{3,2,1,0:T(8,128)(2,1)S(1)}, bf16[1,2,320,1792]{3,2,1,0:T(8,128)(2,1)}, u32[]{:S(2)}) copy-start(bf16[1,2,320,1792]{3,2,1,0:T(8,128)(2,1)} %param.3) | copy-start | bytes 6881284
  11.4 4.4 %collective-permute-start = (f32[320,128]{1,0:T(8,128)S(1)}, f32[320,128]{1,0:T(8,128)S(1)}, u32[]{:S(2)}, u32[]{:S(2)}) collective-permute-start(f32[320,128]{1,0:T(8,128)S(1)} %slice_bitcast_fusion.1), channel_id=1, source_target_pairs={{0,8},{8,0},{1,9},{9,1},{2,10},{10,2},{3,11},{11,3},{4,12},{12,4},... | collective-permute-start | bytes 491528 | tf_op jit(solution)/shard_map/ppermute | solution.py:156
  65.2 5.4 %collective-permute-start.1 = (f32[320,128]{1,0:T(8,128)S(1)}, f32[320,128]{1,0:T(8,128)S(1)}, u32[]{:S(2)}, u32[]{:S(2)}) collective-permute-start(f32[320,128]{1,0:T(8,128)S(1)} %basis.1.mine_ref), channel_id=1, source_target_pairs={{0,8},{8,0},{1,9},{9,1},{2,10},{10,2},{3,11},{11,3},{4,12},{12,4},... | collective-permute-start | bytes 491528 | tf_op jit(solution)/shard_map/ppermute | solution.py:156
  70.6 2.3 %copy-start.1 = (f32[1,2,320,1792]{3,2,1,0:T(8,128)S(1)}, f32[1,2,320,1792]{3,2,1,0:T(8,128)}, u32[]{:S(2)}) copy-start(f32[1,2,320,1792]{3,2,1,0:T(8,128)} %param.4) | copy-start | bytes 13762564
  77.9 2.6 %collective-permute-start.2 = (f32[128,1792]{1,0:T(8,128)S(1)}, f32[128,1792]{1,0:T(8,128)S(1)}, u32[]{:S(2)}, u32[]{:S(2)}) collective-permute-start(f32[128,1792]{1,0:T(8,128)S(1)} %slice_bitcast_fusion), channel_id=1, source_target_pairs={{0,8},{8,0},{1,9},{9,1},{2,10},{10,2},{3,11},{11,3},{4,12},{12,4},... | collective-permute-start | bytes 2752520 | tf_op jit(solution)/shard_map/ppermute | solution.py:156
  97.9 24.1 %copy-start.5 = (f32[2,320,128]{2,1,0:T(8,128)S(1)}, f32[2,320,128]{2,1,0:T(8,128)}, u32[]{:S(2)}) copy-start(f32[2,320,128]{2,1,0:T(8,128)} %get-tuple-element.5.basis_ref) | copy-start | bytes 983044
  116.4 5.6 %collective-permute-start.3 = (f32[128,1792]{1,0:T(8,128)S(1)}, f32[128,1792]{1,0:T(8,128)S(1)}, u32[]{:S(2)}, u32[]{:S(2)}) collective-permute-start(f32[128,1792]{1,0:T(8,128)S(1)} %bitcast.26), channel_id=1, source_target_pairs={{0,8},{8,0},{1,9},{9,1},{2,10},{10,2},{3,11},{11,3},{4,12},{12,4},... | collective-permute-start | bytes 2752520 | tf_op jit(solution)/shard_map/ppermute | solution.py:156
  122.0 2.3 %copy-start.2 = (f32[1,2,320,1792]{3,2,1,0:T(8,128)S(1)}, f32[1,2,320,1792]{3,2,1,0:T(8,128)}, u32[]{:S(2)}) copy-start(f32[1,2,320,1792]{3,2,1,0:T(8,128)} %param.4) | copy-start | bytes 13762564

commit v2 on v0

v2 whole, which is shorter than its diff:
```python
import functools

import jax
import jax.numpy as jnp
from jax import lax
from jax.experimental import pallas as pl
from jax.experimental.pallas import tpu as pltpu
from jax.sharding import Mesh, PartitionSpec as P

RANK = 128
PRIME = 32749
SIDE = 4
CORES = 2
CHUNK = 256
GROUP = 8
MIB = 1024 * 1024

unit_scale = 3.4641016
f32 = jnp.float32
bf16 = jnp.bfloat16

smem = pl.BlockSpec(memory_space=pltpu.SMEM)
hbm = pl.BlockSpec(memory_space=pltpu.HBM)
vmem = pl.BlockSpec(memory_space=pltpu.VMEM)


def split(x):
    high = x.astype(bf16)
    return high, (x - high.astype(f32)).astype(bf16)


def dot(a, b, contract=((1,), (0,))):
    return lax.dot_general(a, b, (contract, ((), ())), preferred_element_type=f32)


def exact_dot(a, b, contract):
    return lax.dot_general(
        a, b, (contract, ((), ())), precision=lax.Precision.HIGHEST, preferred_element_type=f32
    )


def cols(j):
    return pl.ds(j * CHUNK, CHUNK)


def centred(x):
    quotient = (x.astype(f32) * (1.0 / PRIME) + 0.5).astype(jnp.int32)
    return x - quotient * PRIME


def start_block(seed, first, columns):
    col = first + lax.broadcasted_iota(jnp.int32, (columns, RANK), 0)
    rank = lax.broadcasted_iota(jnp.int32, (columns, RANK), 1)
    hashed = centred(col * 131 + rank * 977 + seed)
    hashed = centred(hashed * hashed + rank * 17 + 7)
    hashed = centred(hashed * hashed + col)
    hashed = jnp.where(hashed < 0, hashed + PRIME, hashed)
    return (hashed.astype(f32) * (1.0 / PRIME) - 0.5) * unit_scale


def left_kernel(where_ref, grad_hbm, feed_hbm, out_ref, grad_ref, feed_ref, start_ref, sems):
    seed, first, core = where_ref[0], where_ref[1], where_ref[2]
    steps = grad_ref.shape[2] // CHUNK
    copies = []
    for j in range(steps):
        pair = (
            pltpu.make_async_copy(grad_hbm.at[:, :, cols(j)], grad_ref.at[:, :, cols(j)], sems.at[j, 0]),
            pltpu.make_async_copy(feed_hbm.at[:, :, cols(j)], feed_ref.at[:, :, cols(j)], sems.at[j, 1]),
        )
        for copy in pair:
            copy.start()
        copies.append(pair)
    for j in range(steps):
        high, low = split(start_block(seed, first + j * CHUNK, CHUNK))
        start_ref[cols(j), :RANK] = high
        start_ref[cols(j), RANK:] = low
    for j in range(steps):
        for copy in copies[j]:
            copy.wait()
        both = start_ref[cols(j), :]
        for m in range(2):
            s_high, s_low = split(grad_ref[m, :, cols(j)].astype(f32) + feed_ref[m, :, cols(j)])
            wide = dot(s_high, both)
            part = wide[:, :RANK] + wide[:, RANK:] + dot(s_low, both[:, :RANK])
            if j == 0:
                out_ref[m ^ core] = part
            else:
                out_ref[m ^ core] += part


def eliminate(gram):
    lane = lax.broadcasted_iota(jnp.int32, (1, RANK), 1)
    count = RANK // GROUP
    blocks = [gram[GROUP * b : GROUP * (b + 1), :] for b in range(count)]
    sub = lax.broadcasted_iota(jnp.int32, (GROUP, RANK), 0)
    pivots = []
    for b in range(count):
        start = GROUP * b
        panel = blocks[b]
        spread_cols = [jnp.broadcast_to(panel[:, start + t : start + t + 1], (GROUP, RANK)) for t in range(GROUP)]
        a = [[spread_cols[t][s : s + 1, :] for t in range(GROUP)] for s in range(GROUP)]
        factors = [[None] * GROUP for _ in range(GROUP)]
        inverses = []
        for t in range(GROUP):
            pivots.append(a[t][t])
            inverses.append(1.0 / a[t][t])
            for s in range(t + 1, GROUP):
                factors[s][t] = a[s][t] * inverses[t]
                for u in range(t + 1, GROUP):
                    a[s][u] = a[s][u] - factors[s][t] * a[t][u]
        rows, sources = [], []
        for s in range(GROUP):
            row = panel[s : s + 1, :]
            for t in range(s):
                row = jnp.where(lane == start + t, 0.0, row) - factors[s][t] * sources[t]
            rows.append(row)
            sources.append(jnp.where(lane == start + s, 1.0, row))
        for s in range(GROUP):
            panel = jnp.where(sub == s, rows[s], panel)
        blocks[b] = panel
        for later in range(b + 1, count):
            block = blocks[later]
            heads = [jnp.broadcast_to(block[:, start + t : start + t + 1], (GROUP, RANK)) for t in range(GROUP)]
            for t in range(GROUP):
                factor = heads[t] * inverses[t]
                for u in range(t + 1, GROUP):
                    heads[u] = heads[u] - factor * a[t][u]
                block = jnp.where(lane == start + t, 0.0, block) - factor * sources[t]
            blocks[later] = block
    return jnp.concatenate(blocks, axis=0), jnp.concatenate(pivots, axis=0)


def basis_kernel(left_ref, basis_ref, inverse_ref):
    left = left_ref[...] * (1.0 / 32)
    lower, pivots = eliminate(exact_dot(left, left, ((0,), (0,))))
    i = lax.broadcasted_iota(jnp.int32, (RANK, RANK), 0)
    j = lax.broadcasted_iota(jnp.int32, (RANK, RANK), 1)
    inverse = jnp.where(i > j, lower, jnp.where(i == j, 1.0, 0.0)) * lax.rsqrt(pivots)
    inverse_ref[...] = inverse
    basis_ref[...] = exact_dot(left, inverse, ((1,), (1,)))


def right_kernel(where_ref, mine_ref, other_ref, grad_ref, feed_ref, out_ref):
    core = where_ref[2]
    for m in range(2):
        high, low = split(jnp.where(core == m, mine_ref[...], other_ref[...]) * (1.0 / 32))
        first = jnp.concatenate([high, low], axis=1)
        second = jnp.concatenate([high, jnp.zeros_like(low)], axis=1)
        stack = jnp.concatenate([first, second], axis=0)
        for j in range(grad_ref.shape[2] // CHUNK):
            s_high, s_low = split(grad_ref[m, :, cols(j)].astype(f32) + feed_ref[m, :, cols(j)])
            wide = dot(jnp.concatenate([s_high, s_low], axis=0), stack, ((0,), (0,)))
            out_ref[m ^ core, cols(j), :] = wide[:, :RANK] + wide[:, RANK:]


def finish_kernel(part_ref, inverse_ref, out_ref):
    total = part_ref[0]
    for i in range(1, part_ref.shape[0]):
        total = total + part_ref[i]
    done = exact_dot(total * (1.0 / 32), inverse_ref[...], ((1,), (1,)))
    for i in range(part_ref.shape[0]):
        out_ref[i] = done


def update_kernel(slot, where_ref, basis_ref, right_ref, grad_ref, feed_ref, *rest):
    out_hbm, right_hbm, out_ref, sems = rest[2 * slot :]
    m = where_ref[2] ^ slot
    copies = [pltpu.make_async_copy(right_ref, right_hbm.at[m], sems.at[0])]
    copies[0].start()
    high, low = split(basis_ref[...])
    wide = jnp.concatenate([high, low], axis=1)
    for j in range(right_ref.shape[0] // CHUNK):
        r_high, r_low = split(right_ref[cols(j), :])
        rebuilt = dot(wide, jnp.concatenate([r_high, r_high], axis=1), ((1,), (1,)))
        rebuilt = rebuilt + dot(high, r_low, ((1,), (1,)))
        out_ref[:, cols(j)] = grad_ref[m, :, cols(j)].astype(f32) + feed_ref[m, :, cols(j)] - rebuilt
        copy = pltpu.make_async_copy(out_ref.at[:, cols(j)], out_hbm.at[m, :, cols(j)], sems.at[1 + j])
        copy.start()
        copies.append(copy)
    for copy in copies:
        copy.wait()


def update(slot, where, basis, right, gradients, feedback, previous=()):
    mats, rows, columns = gradients.shape
    return pl.pallas_call(
        functools.partial(update_kernel, slot),
        in_specs=[smem, vmem, vmem, vmem, vmem] + [hbm] * len(previous),
        out_specs=[hbm, hbm],
        out_shape=[
            jax.ShapeDtypeStruct((mats, rows, columns), f32),
            jax.ShapeDtypeStruct((mats, columns, RANK), f32),
        ],
        scratch_shapes=[
            pltpu.VMEM((rows, columns), f32),
            pltpu.SemaphoreType.DMA((1 + columns // CHUNK,)),
        ],
        input_output_aliases={5: 0, 6: 1} if previous else {},
        cost_estimate=pl.CostEstimate(flops=6 * rows * columns * RANK, bytes_accessed=8 * rows * columns, transcendentals=0),
        compiler_params=pltpu.CompilerParams(vmem_limit_bytes=8 * MIB),
        name=("update_mine", "update_other")[slot],
    )(where, basis, right, gradients, feedback, *previous)


def spread(x, axes, count):
    return lax.all_to_all(jnp.broadcast_to(x[None], (count,) + x.shape), axes, 0, 0)


def swap(x):
    return lax.ppermute(x, "core", [(0, 1), (1, 0)])


def on_device(gradients, feedback, seed_value):
    gradients, feedback = gradients[0], feedback[0]
    mats, rows, columns = gradients.shape
    chips = SIDE * SIDE
    depth = lax.axis_size("z")
    core = lax.axis_index("core")
    where = jnp.stack([seed_value[0], lax.axis_index("z") * columns, core]).astype(jnp.int32)

    left_part = pl.pallas_call(
        left_kernel,
        in_specs=[smem, hbm, hbm],
        out_specs=vmem,
        out_shape=jax.ShapeDtypeStruct((mats, rows, RANK), f32),
        scratch_shapes=[
            pltpu.VMEM((mats, rows, columns), bf16),
            pltpu.VMEM((mats, rows, columns), f32),
            pltpu.VMEM((columns, 2 * RANK), bf16),
            pltpu.SemaphoreType.DMA((columns // CHUNK, 2)),
        ],
        compiler_params=pltpu.CompilerParams(vmem_limit_bytes=62 * MIB),
        name="left_part",
    )(where, gradients, feedback)

    left = left_part[0] + swap(left_part[1])
    left = lax.all_to_all(left.reshape(chips, rows // chips, RANK), ("x", "y"), 0, 0).sum(0)
    left = spread(left, "z", depth).sum(0)
    left_mine = spread(left, ("x", "y"), chips).reshape(rows, RANK)
    left_other = swap(left_mine)

    right_part = pl.pallas_call(
        right_kernel,
        in_specs=[smem, vmem, vmem, vmem, vmem],
        out_specs=vmem,
        out_shape=jax.ShapeDtypeStruct((mats, columns, RANK), f32),
        cost_estimate=pl.CostEstimate(
            flops=12 * rows * columns * RANK, bytes_accessed=12 * rows * columns, transcendentals=0
        ),
        compiler_params=pltpu.CompilerParams(vmem_limit_bytes=8 * MIB),
        name="right_part",
    )(where, left_mine, left_other, gradients, feedback)

    basis_mine, inverse = pl.pallas_call(
        basis_kernel,
        in_specs=[vmem],
        out_specs=[vmem, vmem],
        out_shape=[jax.ShapeDtypeStruct((rows, RANK), f32), jax.ShapeDtypeStruct((RANK, RANK), f32)],
        cost_estimate=pl.CostEstimate(flops=6_000_000_000, bytes_accessed=400_000, transcendentals=0),
        compiler_params=pltpu.CompilerParams(vmem_limit_bytes=8 * MIB),
        name="basis",
    )(left_mine)
    basis_other = swap(basis_mine)
    mine_first = jnp.where(core == 0, basis_mine, basis_other)
    mine_last = jnp.where(core == 0, basis_other, basis_mine)
    left_basis = jnp.stack([mine_first, mine_last])

    right = right_part[0] + swap(right_part[1])
    right = lax.all_to_all(right.reshape(chips, columns // chips, RANK), ("x", "y"), 0, 0)
    right = pl.pallas_call(
        finish_kernel,
        in_specs=[vmem, vmem],
        out_specs=vmem,
        out_shape=jax.ShapeDtypeStruct(right.shape, f32),
        compiler_params=pltpu.CompilerParams(vmem_limit_bytes=8 * MIB),
        name="finish",
    )(right, inverse)
    right_mine = lax.all_to_all(right, ("x", "y"), 0, 0).reshape(columns, RANK)
    right_other = swap(right_mine)

    outs = update(0, where, basis_mine, right_mine, gradients, feedback)
    new_feedback, right_factor = update(1, where, basis_other, right_other, gradients, feedback, outs)
    return new_feedback[None], left_basis, right_factor


def solution(mesh):
    fine = Mesh(mesh.devices.reshape(SIDE, SIDE, CORES, -1), ("x", "y", "core", "z"))
    dp = ("x", "y", "core")
    placed = (P(dp, None, None, "z"), P(dp, None, None, "z"), P())
    return jax.shard_map(
        on_device,
        mesh=fine,
        in_specs=placed,
        out_specs=(P(dp, None, None, "z"), P(), P(None, "z", None)),
        check_vma=False,
    )
```

time: 457 us -> 116 us (0.25)
  waiting for transfers between devices: 364 us -> 15 us
  blocking collectives: 0 us -> 55 us
  other arithmetic: 45.2 us -> 3.34 us
  matrix products: 32.4 us -> 0 us
  Pallas kernels: 0 us -> 18 us
  starting transfers between devices: 0.08 us -> 15.5 us
  between operations: 14.8 us -> 1.58 us
  local copies, waits for them, and re-layouts: 0.11 us -> 7.27 us
    psum x2 -> x0, waiting for transfers between devices: 364 us -> none  [the longest x1 250 us: on_device(): left_sum = lax.psum(left_part, ('dp', 'tensor')) / replicas]
    all_to_all x0 -> x4, blocking collectives: none -> 55 us  [the longest x2 25.9 us: spread(): lax.all_to_all(jnp.broadcast_to(x[None], (count,) + x.shape), axes, 0, 0)]
    another operation x7 -> x3, other arithmetic: 43.6 us -> 1.36 us  [the longest x2 0.77 us: on_device(): left_basis = jnp.stack([mine_first, mine_last])]
    dot_general x4 -> x0, matrix products: 31 us -> none  [the longest x1 11.7 us: on_device(): jnp.einsum('mrc,mrk->mck', summed_in, left_basis, precision=highest)]
    pallas_call x0 -> x6, Pallas kernels: none -> 18 us  [the longest x2 5.48 us: update(): pl.pallas_call(functools.partial(update_kernel, slot), in_specs=[smem, vm...]
    ppermute x0 -> x5, starting transfers between devices: none -> 11.7 us  [swap(): return lax.ppermute(x, 'core', [(0, 1), (1, 0)])]
    all_to_all x0 -> x1, waiting for transfers between devices: none -> 8.69 us  [on_device(): lax.all_to_all(right.reshape(chips, columns // chips, RANK), ('x', 'y'),...]
    ppermute x0 -> x5, waiting for transfers between devices: none -> 6.36 us  [swap(): return lax.ppermute(x, 'core', [(0, 1), (1, 0)])]
  transfers between devices with their start and end apart: 2 -> 6, of which waited for: 2 -> 5; matrix products, arithmetic and copies ran while one was open for 0% -> 1% of each run, Pallas kernels for 0% -> 6%
where the time goes in v2:
time: 116 us
  blocking collectives  55 us (47%)
  Pallas kernels  18 us (16%)
  starting transfers between devices  15.5 us (13%)
  waiting for transfers between devices  15 us (13%)
  local copies, waits for them, and re-layouts  7.27 us (6%)
  other arithmetic  3.34 us (3%)
  between operations  1.58 us (1%)
    all_to_all x2, blocking collectives, spread(): lax.all_to_all(jnp.broadcast_to(x[None], (count,) + x.shape), axes, 0, 0)  25.9 us
    all_to_all x1, blocking collectives, on_device(): right_mine = lax.all_to_all(right, ('x', 'y'), 0, 0).reshape(columns, RANK)  17.1 us
    all_to_all x1, blocking collectives, on_device(): lax.all_to_all(left.reshape(chips, rows // chips, RANK), ('x', 'y'), 0, 0)  11.9 us
    ppermute x5, starting transfers between devices, swap(): return lax.ppermute(x, 'core', [(0, 1), (1, 0)])  11.7 us
    all_to_all x1, waiting for transfers between devices, on_device(): lax.all_to_all(right.reshape(chips, columns // chips, RANK), ('x', 'y'),...  8.69 us
    ppermute x5, waiting for transfers between devices, swap(): return lax.ppermute(x, 'core', [(0, 1), (1, 0)])  6.36 us
    unnamed x12, local copies, waits for them, and re-layouts  6.08 us
    pallas_call x2, Pallas kernels, update(): pl.pallas_call(functools.partial(update_kernel, slot), in_specs=[smem, vm...  5.48 us
  transfers between devices with their start and end apart: 6, of which 5 were waited for; matrix products, arithmetic and copies ran while one was open for 1% of the time, Pallas kernels for 6%

profile of v2, /device:TPU:1, one launch (start us, length us, event | category | flops | bytes accessed | tf_op | source)
XLA Modules:
  0.0 115.7 jit_solution(7040159299038495583)
XLA Ops:
  1.3 0.6 pad_add_fusion.where_ref
  1.9 5.3 %left_part.1 = f32[2,320,128]{2,1,0:T(8,128)} custom-call(s32[3]{0:T(128)} %pad_add_fusion.where_ref, bf16[2,320,1792]{2,1,0:T(8,128)(2,1)} %bitcast.27, f32[2,320,1792]{2,1,0:T(8,128)} %bitcast.23), custom_call_target="tpu_custom_call" | custom-call | tf_op jit(solution)/shard_map/left_part/pallas_call | solution.py:221
  7.1 0.0 copy-start.2
  7.2 0.0 copy-start.5
  7.2 1.1 slice_bitcast_fusion.2
  8.2 3.3 %collective-permute-start = (f32[320,128]{1,0:T(8,128)S(1)}, f32[320,128]{1,0:T(8,128)S(1)}, u32[]{:S(2)}, u32[]{:S(2)}) collective-permute-start(f32[320,128]{1,0:T(8,128)S(1)} %slice_bitcast_fusion.2), channel_id=1, source_target_pairs={{0,8},{8,0},{1,9},{9,1},{2,10},{10,2},{3,11},{11,3},{4,12},{12,4},... | collective-permute-start | bytes 491528 | tf_op jit(solution)/shard_map/ppermute | solution.py:210
  11.6 1.0 collective-permute-done
  12.6 0.9 fusion.1
  13.6 11.9 %all_to_all.25 = f32[16,20,128]{2,1,0:T(8,128)S(1)} all-to-all(f32[16,20,128]{2,1,0:T(8,128)S(1)} %reshape.20), channel_id=1, replica_groups=mesh['x'=4,'y'=4,'core'=2,'z'=8] {'x','y'}, dimensions={0} | all-to-all | bytes 327680 | tf_op jit(solution)/shard_map/all_to_all | solution.py:237
  25.5 15.7 %all_to_all.26 = f32[8,20,128]{2,1,0:T(8,128)S(1)} all-to-all(f32[8,20,128]{2,1,0:T(8,128)S(1)} %broadcast_in_dim.6), channel_id=1, replica_groups=mesh['x'=4,'y'=4,'core'=2,'z'=8] {'z'}, dimensions={0} | all-to-all | bytes 163840 | tf_op jit(solution)/shard_map/all_to_all | solution.py:206
  41.2 10.3 %all_to_all.27 = f32[16,20,128]{2,1,0:T(8,128)S(1)} all-to-all(f32[16,20,128]{2,1,0:T(8,128)S(1)} %broadcast_in_dim.7), channel_id=1, replica_groups=mesh['x'=4,'y'=4,'core'=2,'z'=8] {'x','y'}, dimensions={0} | all-to-all | bytes 327680 | tf_op jit(solution)/shard_map/all_to_all | solution.py:206
  51.5 4.4 %collective-permute-start.2 = (f32[320,128]{1,0:T(8,128)S(1)}, f32[320,128]{1,0:T(8,128)S(1)}, u32[]{:S(2)}, u32[]{:S(2)}) collective-permute-start(f32[320,128]{1,0:T(8,128)S(1)} %reshape.21.left_ref.mine_ref), channel_id=1, source_target_pairs={{0,8},{8,0},{1,9},{9,1},{2,10},{10,2},{3,11},{11,3},{4,12},{12,4},... | collective-permute-start | bytes 491528 | tf_op jit(solution)/shard_map/ppermute | solution.py:210
  55.9 1.0 collective-permute-done.2.other_ref
  56.9 0.0 copy-done.2
  56.9 0.0 copy-done.5
  56.9 0.0 copy-start
  56.9 2.3 %copy-done = f32[1,2,320,1792]{3,2,1,0:T(8,128)S(1)} copy-done((f32[1,2,320,1792]{3,2,1,0:T(8,128)S(1)}, f32[1,2,320,1792]{3,2,1,0:T(8,128)}, u32[]{:S(2)}) %copy-start) | copy-done | bytes 4587544
  59.2 2.1 %right_part.1 = f32[2,1792,128]{2,1,0:T(8,128)S(1)} custom-call(s32[3]{0:T(128)S(1)} %copy-done.5, f32[320,128]{1,0:T(8,128)S(1)} %reshape.21.left_ref.mine_ref, f32[320,128]{1,0:T(8,128)S(1)} %collective-permute-done.2.other_ref, bf16[2,320,1792]{2,1,0:T(8,128)(2,1)S(1)} %bitcast.28, f32[2,320,1792]{2,1,0:T(8,128)S(1)} %bitcast.24), custom_call_target="tpu_custom_call" | custom-call | flops 880803840 | bytes 6881280 | tf_op jit(solution)/shard_map/right_part/pallas_call | solution.py:242
  61.3 0.1 slice_bitcast_fusion
  61.4 0.5 collective-permute-start.3
  61.8 2.1 %collective-permute-done.3 = f32[1792,128]{1,0:T(8,128)S(1)} collective-permute-done((f32[1792,128]{1,0:T(8,128)S(1)}, f32[1792,128]{1,0:T(8,128)S(1)}, u32[]{:S(2)}, u32[]{:S(2)}) %collective-permute-start.3) | collective-permute-done | bytes 917536 | tf_op jit(solution)/shard_map/ppermute | solution.py:210
  64.0 1.0 fusion
  65.0 3.8 %all-to-all-start.3 = ((f32[16,112,128]{2,1,0:T(8,128)}), f32[16,112,128]{2,1,0:T(8,128)S(1)}, u32[]{:S(2)}, u32[]{:S(2)}) async-start(f32[16,112,128]{2,1,0:T(8,128)} %bitcast.34), calls=%async_computation.3 | async-start | bytes 1835008 | tf_op jit(solution)/shard_map/all_to_all | solution.py:269
  68.8 4.9 %basis.1 = (f32[320,128]{1,0:T(8,128)S(1)}, f32[128,128]{1,0:T(8,128)S(1)}) custom-call(f32[320,128]{1,0:T(8,128)S(1)} %reshape.21.left_ref.mine_ref), custom_call_target="tpu_custom_call" | custom-call | flops 6000000000 | bytes 400000 | tf_op jit(solution)/shard_map/basis/pallas_call | solution.py:254
  73.7 0.0 copy-start.3
  73.7 0.6 copy-done.3
  74.3 8.7 %all-to-all-done.3.part_ref = f32[16,112,128]{2,1,0:T(8,128)S(1)} async-done(((f32[16,112,128]{2,1,0:T(8,128)}), f32[16,112,128]{2,1,0:T(8,128)S(1)}, u32[]{:S(2)}, u32[]{:S(2)}) %all-to-all-start.3) | async-done | bytes 917536 | tf_op jit(solution)/shard_map/all_to_all | solution.py:269
  83.0 0.0 copy-start.4
  83.0 0.8 copy-done.4
  83.8 0.3 finish.1
  84.1 17.1 %all_to_all.28 = f32[16,112,128]{2,1,0:T(8,128)S(1)} all-to-all(f32[16,112,128]{2,1,0:T(8,128)S(1)} %finish.1), channel_id=1, replica_groups=mesh['x'=4,'y'=4,'core'=2,'z'=8] {'x','y'}, dimensions={0} | all-to-all | bytes 1835008 | tf_op jit(solution)/shard_map/all_to_all | solution.py:278
  101.3 3.5 %collective-permute-start.4 = (f32[1792,128]{1,0:T(8,128)S(1)}, f32[1792,128]{1,0:T(8,128)}, u32[]{:S(2)}, u32[]{:S(2)}) collective-permute-start(f32[1792,128]{1,0:T(8,128)S(1)} %bitcast.31), channel_id=1, source_target_pairs={{0,8},{8,0},{1,9},{9,1},{2,10},{10,2},{3,11},{11,3},{4,12},{12,4},... | collective-permute-start | bytes 2752520 | tf_op jit(solution)/shard_map/ppermute | solution.py:210
  104.8 0.0 collective-permute-start.1
  104.8 2.2 %collective-permute-done.1.basis_ref = f32[320,128]{1,0:T(8,128)S(1)} collective-permute-done((f32[320,128]{1,0:T(8,128)S(1)}, f32[320,128]{1,0:T(8,128)S(1)}, u32[]{:S(2)}, u32[]{:S(2)}) %collective-permute-start.1) | collective-permute-done | bytes 163872 | tf_op jit(solution)/shard_map/ppermute | solution.py:210
  107.0 0.7 pad_maximum_fusion
  107.8 0.0 copy-start.1
  107.8 2.3 %copy-done.1 = f32[1,2,320,1792]{3,2,1,0:T(8,128)S(1)} copy-done((f32[1,2,320,1792]{3,2,1,0:T(8,128)S(1)}, f32[1,2,320,1792]{3,2,1,0:T(8,128)}, u32[]{:S(2)}) %copy-start.1) | copy-done | bytes 4587544
  110.1 2.4 %update_mine.1 = (f32[2,320,1792]{2,1,0:T(8,128)}, f32[2,1792,128]{2,1,0:T(8,128)}) custom-call(s32[3]{0:T(128)S(1)} %copy-done.5, f32[320,128]{1,0:T(8,128)S(1)} %get-tuple-element.9.basis_ref, f32[1792,128]{1,0:T(8,128)S(1)} %bitcast.32, bf16[2,320,1792]{2,1,0:T(8,128)(2,1)S(1)} %bitcast.29, f32[2,320,1792]{2,1,0:T(8,128)S(1)} %bitcast.25), custom_call_target="tpu_custom_call" | custom-call | flops 440401920 | bytes 4587520 | tf_op jit(solution)/shard_map/update_mine/pallas_call | solution.py:186
  112.5 0.0 collective-permute-done.4.right_ref
  112.5 3.1 %update_other.1 = (f32[2,320,1792]{2,1,0:T(8,128)}, f32[2,1792,128]{2,1,0:T(8,128)}) custom-call(s32[3]{0:T(128)S(1)} %copy-done.5, f32[320,128]{1,0:T(8,128)S(1)} %collective-permute-done.1.basis_ref, f32[1792,128]{1,0:T(8,128)} %collective-permute-done.4.right_ref, ...), custom_call_target="tpu_custom_call", output_to_operand_aliasing={{0}: (5, {}), {1}: (6, {})} | custom-call | flops 440401920 | bytes 4587520 | tf_op jit(solution)/shard_map/update_other/pallas_call | solution.py:186
  (7 shorter events, 0.1 us)
Async XLA Ops:
  7.1 49.8 %copy-start.2 = (bf16[1,2,320,1792]{3,2,1,0:T(8,128)(2,1)S(1)}, bf16[1,2,320,1792]{3,2,1,0:T(8,128)(2,1)}, u32[]{:S(2)}) copy-start(bf16[1,2,320,1792]{3,2,1,0:T(8,128)(2,1)} %param.3) | copy-start | bytes 6881284
  7.2 49.8 %copy-start.5 = (s32[3]{0:T(128)S(1)}, s32[3]{0:T(128)}, u32[]{:S(2)}) copy-start(s32[3]{0:T(128)} %pad_add_fusion.where_ref) | copy-start | bytes 40
  8.2 4.4 %collective-permute-start = (f32[320,128]{1,0:T(8,128)S(1)}, f32[320,128]{1,0:T(8,128)S(1)}, u32[]{:S(2)}, u32[]{:S(2)}) collective-permute-start(f32[320,128]{1,0:T(8,128)S(1)} %slice_bitcast_fusion.2), channel_id=1, source_target_pairs={{0,8},{8,0},{1,9},{9,1},{2,10},{10,2},{3,11},{11,3},{4,12},{12,4},... | collective-permute-start | bytes 491528 | tf_op jit(solution)/shard_map/ppermute | solution.py:210
  51.5 5.4 %collective-permute-start.2 = (f32[320,128]{1,0:T(8,128)S(1)}, f32[320,128]{1,0:T(8,128)S(1)}, u32[]{:S(2)}, u32[]{:S(2)}) collective-permute-start(f32[320,128]{1,0:T(8,128)S(1)} %reshape.21.left_ref.mine_ref), channel_id=1, source_target_pairs={{0,8},{8,0},{1,9},{9,1},{2,10},{10,2},{3,11},{11,3},{4,12},{12,4},... | collective-permute-start | bytes 491528 | tf_op jit(solution)/shard_map/ppermute | solution.py:210
  56.9 2.3 %copy-start = (f32[1,2,320,1792]{3,2,1,0:T(8,128)S(1)}, f32[1,2,320,1792]{3,2,1,0:T(8,128)}, u32[]{:S(2)}) copy-start(f32[1,2,320,1792]{3,2,1,0:T(8,128)} %param.4) | copy-start | bytes 13762564
  61.4 2.6 %collective-permute-start.3 = (f32[1792,128]{1,0:T(8,128)S(1)}, f32[1792,128]{1,0:T(8,128)S(1)}, u32[]{:S(2)}, u32[]{:S(2)}) collective-permute-start(f32[1792,128]{1,0:T(8,128)S(1)} %slice_bitcast_fusion), channel_id=1, source_target_pairs={{0,8},{8,0},{1,9},{9,1},{2,10},{10,2},{3,11},{11,3},{4,12},{12,4},... | collective-permute-start | bytes 2752520 | tf_op jit(solution)/shard_map/ppermute | solution.py:210
  65.0 18.0 %all-to-all-start.3 = ((f32[16,112,128]{2,1,0:T(8,128)}), f32[16,112,128]{2,1,0:T(8,128)S(1)}, u32[]{:S(2)}, u32[]{:S(2)}) async-start(f32[16,112,128]{2,1,0:T(8,128)} %bitcast.34), calls=%async_computation.3 | async-start | bytes 1835008 | tf_op jit(solution)/shard_map/all_to_all | solution.py:269
  73.7 0.6 copy-start.3
  83.0 0.8 copy-start.4
  101.3 11.2 %collective-permute-start.4 = (f32[1792,128]{1,0:T(8,128)S(1)}, f32[1792,128]{1,0:T(8,128)}, u32[]{:S(2)}, u32[]{:S(2)}) collective-permute-start(f32[1792,128]{1,0:T(8,128)S(1)} %bitcast.31), channel_id=1, source_target_pairs={{0,8},{8,0},{1,9},{9,1},{2,10},{10,2},{3,11},{11,3},{4,12},{12,4},... | collective-permute-start | bytes 2752520 | tf_op jit(solution)/shard_map/ppermute | solution.py:210
  104.8 2.2 %collective-permute-start.1 = (f32[320,128]{1,0:T(8,128)S(1)}, f32[320,128]{1,0:T(8,128)S(1)}, u32[]{:S(2)}, u32[]{:S(2)}) collective-permute-start(f32[320,128]{1,0:T(8,128)S(1)} %get-tuple-element.9.basis_ref), channel_id=1, source_target_pairs={{0,8},{8,0},{1,9},{9,1},{2,10},{10,2},{3,11},{11,3},{4,12},{12,4},... | collective-permute-start | bytes 491528 | tf_op jit(solution)/shard_map/ppermute | solution.py:210
  107.8 2.3 %copy-start.1 = (f32[1,2,320,1792]{3,2,1,0:T(8,128)S(1)}, f32[1,2,320,1792]{3,2,1,0:T(8,128)}, u32[]{:S(2)}) copy-start(f32[1,2,320,1792]{3,2,1,0:T(8,128)} %param.4) | copy-start | bytes 13762564

commit v3 on v2

v3 whole, which is shorter than its diff:
```python
import functools

import jax
import jax.numpy as jnp
from jax import lax
from jax.experimental import pallas as pl
from jax.experimental.pallas import tpu as pltpu
from jax.sharding import Mesh, PartitionSpec as P

RANK = 128
PRIME = 32749
SIDE = 4
CORES = 2
CHUNK = 256
GROUP = 8
MIB = 1024 * 1024

unit_scale = 3.4641016
f32 = jnp.float32
bf16 = jnp.bfloat16

smem = pl.BlockSpec(memory_space=pltpu.SMEM)
hbm = pl.BlockSpec(memory_space=pltpu.HBM)
vmem = pl.BlockSpec(memory_space=pltpu.VMEM)


def split(x):
    high = x.astype(bf16)
    return high, (x - high.astype(f32)).astype(bf16)


def dot(a, b, contract=((1,), (0,))):
    return lax.dot_general(a, b, (contract, ((), ())), preferred_element_type=f32)


def exact_dot(a, b, contract):
    return lax.dot_general(
        a, b, (contract, ((), ())), precision=lax.Precision.HIGHEST, preferred_element_type=f32
    )


def cols(j):
    return pl.ds(j * CHUNK, CHUNK)


def centred(x):
    quotient = (x.astype(f32) * (1.0 / PRIME) + 0.5).astype(jnp.int32)
    return x - quotient * PRIME


def start_block(seed, first, columns):
    col = first + lax.broadcasted_iota(jnp.int32, (columns, RANK), 0)
    rank = lax.broadcasted_iota(jnp.int32, (columns, RANK), 1)
    hashed = centred(col * 131 + rank * 977 + seed)
    hashed = centred(hashed * hashed + rank * 17 + 7)
    hashed = centred(hashed * hashed + col)
    hashed = jnp.where(hashed < 0, hashed + PRIME, hashed)
    return (hashed.astype(f32) * (1.0 / PRIME) - 0.5) * unit_scale


def left_kernel(seed_ref, grad_hbm, feed_hbm, mine_ref, other_ref, sum_ref, grad_ref, start_ref, sems):
    steps = grad_ref.shape[2] // CHUNK
    seed = seed_ref[0]
    first = lax.axis_index("z") * grad_ref.shape[2]
    core = lax.axis_index("core")
    copies = []
    for j in range(steps):
        pair = (
            pltpu.make_async_copy(grad_hbm.at[:, :, cols(j)], grad_ref.at[:, :, cols(j)], sems.at[j, 0]),
            pltpu.make_async_copy(feed_hbm.at[:, :, cols(j)], sum_ref.at[:, :, cols(j)], sems.at[j, 1]),
        )
        for copy in pair:
            copy.start()
        copies.append(pair)
    for j in range(steps):
        high, low = split(start_block(seed, first + j * CHUNK, CHUNK))
        start_ref[cols(j), :RANK] = high
        start_ref[cols(j), RANK:] = low
    for j in range(steps):
        for copy in copies[j]:
            copy.wait()
        both = start_ref[cols(j), :]
        for slot, ref in enumerate((mine_ref, other_ref)):
            m = core ^ slot
            summed = grad_ref[m, :, cols(j)].astype(f32) + sum_ref[m, :, cols(j)]
            sum_ref[m, :, cols(j)] = summed
            s_high, s_low = split(summed)
            wide = dot(s_high, both)
            part = wide[:, :RANK] + wide[:, RANK:] + dot(s_low, both[:, :RANK])
            if j == 0:
                ref[...] = part
            else:
                ref[...] += part


def eliminate(gram):
    lane = lax.broadcasted_iota(jnp.int32, (1, RANK), 1)
    count = RANK // GROUP
    blocks = [gram[GROUP * b : GROUP * (b + 1), :] for b in range(count)]
    sub = lax.broadcasted_iota(jnp.int32, (GROUP, RANK), 0)
    pivots = []
    for b in range(count):
        start = GROUP * b
        panel = blocks[b]
        spread_cols = [jnp.broadcast_to(panel[:, start + t : start + t + 1], (GROUP, RANK)) for t in range(GROUP)]
        a = [[spread_cols[t][s : s + 1, :] for t in range(GROUP)] for s in range(GROUP)]
        factors = [[None] * GROUP for _ in range(GROUP)]
        inverses = []
        for t in range(GROUP):
            pivots.append(a[t][t])
            inverses.append(1.0 / a[t][t])
            for s in range(t + 1, GROUP):
                factors[s][t] = a[s][t] * inverses[t]
                for u in range(t + 1, GROUP):
                    a[s][u] = a[s][u] - factors[s][t] * a[t][u]
        rows, sources = [], []
        for s in range(GROUP):
            row = panel[s : s + 1, :]
            for t in range(s):
                row = jnp.where(lane == start + t, 0.0, row) - factors[s][t] * sources[t]
            rows.append(row)
            sources.append(jnp.where(lane == start + s, 1.0, row))
        for s in range(GROUP):
            panel = jnp.where(sub == s, rows[s], panel)
        blocks[b] = panel
        for later in range(b + 1, count):
            block = blocks[later]
            heads = [jnp.broadcast_to(block[:, start + t : start + t + 1], (GROUP, RANK)) for t in range(GROUP)]
            for t in range(GROUP):
                factor = heads[t] * inverses[t]
                for u in range(t + 1, GROUP):
                    heads[u] = heads[u] - factor * a[t][u]
                block = jnp.where(lane == start + t, 0.0, block) - factor * sources[t]
            blocks[later] = block
    return jnp.concatenate(blocks, axis=0), jnp.concatenate(pivots, axis=0)


def basis_kernel(mine_ref, other_ref, right_ref, basis_ref, inverse_ref):
    del right_ref
    core = lax.axis_index("core")
    i = lax.broadcasted_iota(jnp.int32, (RANK, RANK), 0)
    j = lax.broadcasted_iota(jnp.int32, (RANK, RANK), 1)
    for slot, ref in enumerate((mine_ref, other_ref)):
        left = ref[...] * (1.0 / 32)
        lower, pivots = eliminate(exact_dot(left, left, ((0,), (0,))))
        inverse = jnp.where(i > j, lower, jnp.where(i == j, 1.0, 0.0)) * lax.rsqrt(pivots)
        if slot == 0:
            inverse_ref[...] = inverse
        basis_ref[core ^ slot] = exact_dot(left, inverse, ((1,), (1,)))


def right_kernel(slot, left_ref, sum_ref, out_ref):
    m = lax.axis_index("core") ^ slot
    high, low = split(left_ref[...] * (1.0 / 32))
    first = jnp.concatenate([high, low], axis=1)
    second = jnp.concatenate([high, jnp.zeros_like(low)], axis=1)
    stack = jnp.concatenate([first, second], axis=0)
    for j in range(sum_ref.shape[2] // CHUNK):
        s_high, s_low = split(sum_ref[m, :, cols(j)])
        wide = dot(jnp.concatenate([s_high, s_low], axis=0), stack, ((0,), (0,)))
        out_ref[cols(j), :] = wide[:, :RANK] + wide[:, RANK:]


def finish_kernel(part_ref, inverse_ref, out_ref):
    total = part_ref[0]
    for i in range(1, part_ref.shape[0]):
        total = total + part_ref[i]
    done = exact_dot(total * (1.0 / 32), inverse_ref[...], ((1,), (1,)))
    for i in range(part_ref.shape[0]):
        out_ref[i] = done


def update_kernel(slot, basis_ref, right_ref, sum_ref, *rest):
    out_hbm, right_hbm, out_ref, sems = rest[2 * slot :]
    m = lax.axis_index("core") ^ slot
    copies = [pltpu.make_async_copy(right_ref, right_hbm.at[m], sems.at[0])]
    copies[0].start()
    high, low = split(basis_ref[m])
    wide = jnp.concatenate([high, low], axis=1)
    for j in range(right_ref.shape[0] // CHUNK):
        r_high, r_low = split(right_ref[cols(j), :])
        rebuilt = dot(wide, jnp.concatenate([r_high, r_high], axis=1), ((1,), (1,)))
        rebuilt = rebuilt + dot(high, r_low, ((1,), (1,)))
        out_ref[:, cols(j)] = sum_ref[m, :, cols(j)] - rebuilt
        copy = pltpu.make_async_copy(out_ref.at[:, cols(j)], out_hbm.at[m, :, cols(j)], sems.at[1 + j])
        copy.start()
        copies.append(copy)
    for copy in copies:
        copy.wait()


def params(mib):
    return pltpu.CompilerParams(vmem_limit_bytes=mib * MIB)


def right_part(slot, left, summed):
    _, rows, columns = summed.shape
    return pl.pallas_call(
        functools.partial(right_kernel, slot),
        in_specs=[vmem, vmem],
        out_specs=vmem,
        out_shape=pltpu.VMEM((columns, RANK), f32),
        cost_estimate=pl.CostEstimate(
            flops=6 * rows * columns * RANK, bytes_accessed=4 * rows * columns, transcendentals=0
        ),
        compiler_params=params(8),
        name=("right_mine", "right_other")[slot],
    )(left, summed)


def update(slot, basis, right, summed, previous=()):
    mats, rows, columns = summed.shape
    return pl.pallas_call(
        functools.partial(update_kernel, slot),
        in_specs=[vmem, vmem, vmem] + [hbm] * len(previous),
        out_specs=[hbm, hbm],
        out_shape=[
            jax.ShapeDtypeStruct((mats, rows, columns), f32),
            jax.ShapeDtypeStruct((mats, columns, RANK), f32),
        ],
        scratch_shapes=[
            pltpu.VMEM((rows, columns), f32),
            pltpu.SemaphoreType.DMA((1 + columns // CHUNK,)),
        ],
        input_output_aliases={3: 0, 4: 1} if previous else {},
        cost_estimate=pl.CostEstimate(
            flops=6 * rows * columns * RANK, bytes_accessed=8 * rows * columns, transcendentals=0
        ),
        compiler_params=params(8),
        name=("update_mine", "update_other")[slot],
    )(basis, right, summed, *previous)


def spread(x, axes, count):
    return lax.all_to_all(jnp.broadcast_to(x[None], (count,) + x.shape), axes, 0, 0)


def swap(x):
    return lax.ppermute(x, "core", [(0, 1), (1, 0)])


def on_device(gradients, feedback, seed_value):
    gradients, feedback = gradients[0], feedback[0]
    mats, rows, columns = gradients.shape
    chips = SIDE * SIDE
    depth = lax.axis_size("z")

    mine, other, summed = pl.pallas_call(
        left_kernel,
        in_specs=[smem, hbm, hbm],
        out_specs=[vmem, vmem, vmem],
        out_shape=[
            pltpu.VMEM((rows, RANK), f32),
            pltpu.VMEM((rows, RANK), f32),
            pltpu.VMEM((mats, rows, columns), f32),
        ],
        scratch_shapes=[
            pltpu.VMEM((mats, rows, columns), bf16),
            pltpu.VMEM((columns, 2 * RANK), bf16),
            pltpu.SemaphoreType.DMA((columns // CHUNK, 2)),
        ],
        compiler_params=params(12),
        name="left_part",
    )(
        seed_value,
        pltpu.with_memory_space_constraint(gradients, pltpu.HBM),
        pltpu.with_memory_space_constraint(feedback, pltpu.HBM),
    )

    left = mine + swap(other)
    left = lax.all_to_all(left.reshape(chips, rows // chips, RANK), ("x", "y"), 0, 0).sum(0)
    left = spread(left, "z", depth).sum(0)
    left_mine = spread(left, ("x", "y"), chips).reshape(rows, RANK)
    left_other = swap(left_mine)

    sent = swap(right_part(1, left_other, summed))
    right = right_part(0, left_mine, summed) + sent
    left_basis, inverse = pl.pallas_call(
        basis_kernel,
        in_specs=[vmem, vmem, pl.BlockSpec(memory_space=pl.ANY)],
        out_specs=[vmem, vmem],
        out_shape=[jax.ShapeDtypeStruct((mats, rows, RANK), f32), pltpu.VMEM((RANK, RANK), f32)],
        cost_estimate=pl.CostEstimate(flops=10_000_000_000, bytes_accessed=800_000, transcendentals=0),
        compiler_params=params(8),
        name="basis",
    )(left_mine, left_other, right)
    right = lax.all_to_all(right.reshape(chips, columns // chips, RANK), ("x", "y"), 0, 0)
    right = pl.pallas_call(
        finish_kernel,
        in_specs=[vmem, vmem],
        out_specs=vmem,
        out_shape=pltpu.VMEM(right.shape, f32),
        compiler_params=params(8),
        name="finish",
    )(right, inverse)
    right_mine = lax.all_to_all(right, ("x", "y"), 0, 0).reshape(columns, RANK)
    right_other = swap(right_mine)

    outs = update(0, left_basis, right_mine, summed)
    new_feedback, right_factor = update(1, left_basis, right_other, summed, outs)
    return new_feedback[None], left_basis, right_factor


def solution(mesh):
    fine = Mesh(mesh.devices.reshape(SIDE, SIDE, CORES, -1), ("x", "y", "core", "z"))
    dp = ("x", "y", "core")
    placed = (P(dp, None, None, "z"), P(dp, None, None, "z"), P())
    return jax.shard_map(
        on_device,
        mesh=fine,
        in_specs=placed,
        out_specs=(P(dp, None, None, "z"), P(), P(None, "z", None)),
        check_vma=False,
    )
```

time: 116 us -> 108 us (0.931)
  waiting for transfers between devices: 15 us -> 7.22 us
  other arithmetic: 3.34 us -> 1.08 us
  Pallas kernels: 18 us -> 19.6 us
    all_to_all x1, waiting for transfers between devices: 8.69 us -> 3.88 us  [on_device(): lax.all_to_all(right.reshape(chips, columns // chips, RANK), ('x', 'y'),...]
    ppermute x5 -> x4, waiting for transfers between devices: 6.36 us -> 3.34 us  [swap(): return lax.ppermute(x, 'core', [(0, 1), (1, 0)])]
    unnamed x12 -> x8, local copies, waits for them, and re-layouts: 6.08 us -> 7.71 us
    pallas_call x5 -> x6, Pallas kernels: 17.7 us -> 19.3 us  [the longest x1 10.3 us: on_device(): pl.pallas_call(basis_kernel, in_specs=[vmem, vmem, pl.BlockSpec(memory_sp...]
    another operation x3 -> x0, other arithmetic: 1.36 us -> none  [the longest x2 0.77 us: on_device(): left_basis = jnp.stack([mine_first, mine_last])]
    ppermute x5 -> x4, starting transfers between devices: 11.7 us -> 11.6 us  [swap(): return lax.ppermute(x, 'core', [(0, 1), (1, 0)])]
  transfers between devices with their start and end apart: 6 -> 5, of which waited for: 5 -> 4; matrix products, arithmetic and copies ran while one was open for 1% -> 0% of each run, Pallas kernels for 6% -> 12%
where the time goes in v3:
time: 108 us
  blocking collectives  55 us (51%)
  Pallas kernels  19.6 us (18%)
  starting transfers between devices  15.4 us (14%)
  local copies, waits for them, and re-layouts  7.76 us (7%)
  waiting for transfers between devices  7.22 us (7%)
  between operations  1.54 us (1%)
  other arithmetic  1.08 us (1%)
    all_to_all x2, blocking collectives, spread(): lax.all_to_all(jnp.broadcast_to(x[None], (count,) + x.shape), axes, 0, 0)  25.9 us
    all_to_all x1, blocking collectives, on_device(): right_mine = lax.all_to_all(right, ('x', 'y'), 0, 0).reshape(columns, RANK)  17.1 us
    all_to_all x1, blocking collectives, on_device(): lax.all_to_all(left.reshape(chips, rows // chips, RANK), ('x', 'y'), 0, 0)  11.9 us
    ppermute x4, starting transfers between devices, swap(): return lax.ppermute(x, 'core', [(0, 1), (1, 0)])  11.6 us
    pallas_call x1, Pallas kernels, on_device(): pl.pallas_call(basis_kernel, in_specs=[vmem, vmem, pl.BlockSpec(memory_sp...  10.3 us
    unnamed x8, local copies, waits for them, and re-layouts  7.71 us
    all_to_all x1, waiting for transfers between devices, on_device(): lax.all_to_all(right.reshape(chips, columns // chips, RANK), ('x', 'y'),...  3.88 us
    all_to_all x1, starting transfers between devices, on_device(): lax.all_to_all(right.reshape(chips, columns // chips, RANK), ('x', 'y'),...  3.82 us
  transfers between devices with their start and end apart: 5, of which 4 were waited for; matrix products, arithmetic and copies ran while one was open for 0% of the time, Pallas kernels for 12%

profile of v3, /device:TPU:1, one launch (start us, length us, event | category | flops | bytes accessed | tf_op | source)
XLA Modules:
  0.0 107.6 jit_solution(15253761343759199499)
XLA Ops:
  1.3 3.8 %left_part.1 = (f32[320,128]{1,0:T(8,128)S(1)}, f32[320,128]{1,0:T(8,128)S(1)}, f32[2,320,1792]{2,1,0:T(8,128)S(1)}) custom-call(s32[1]{0:T(128)S(6)} %copy.12.seed_ref, bf16[2,320,1792]{2,1,0:T(8,128)(2,1)} %bitcast.9, f32[2,320,1792]{2,1,0:T(8,128)} %bitcast.8), custom_call_target="tpu_custom_call" | custom-call | tf_op jit(solution)/shard_map/left_part/pallas_call | solution.py:248
  5.1 0.0 copy-start
  5.1 2.1 %copy-done = f32[2,320,1792]{2,1,0:T(8,128)} copy-done((f32[2,320,1792]{2,1,0:T(8,128)}, f32[2,320,1792]{2,1,0:T(8,128)S(1)}, u32[]{:S(2)}) %copy-start) | copy-done | bytes 4587544
  7.2 3.2 %collective-permute-start = (f32[320,128]{1,0:T(8,128)S(1)}, f32[320,128]{1,0:T(8,128)S(1)}, u32[]{:S(2)}, u32[]{:S(2)}) collective-permute-start(f32[320,128]{1,0:T(8,128)S(1)} %get-tuple-element.13), channel_id=1, source_target_pairs={{0,8},{8,0},{1,9},{9,1},{2,10},{10,2},{3,11},{11,3},{4,12},{12,4},... | collective-permute-start | bytes 491528 | tf_op jit(solution)/shard_map/ppermute | solution.py:239
  10.5 1.0 collective-permute-done
  11.5 11.9 %all_to_all.25 = f32[16,20,128]{2,1,0:T(8,128)S(1)} all-to-all(f32[16,20,128]{2,1,0:T(8,128)S(1)} %reshape.20), channel_id=1, replica_groups=mesh['x'=4,'y'=4,'core'=2,'z'=8] {'x','y'}, dimensions={0} | all-to-all | bytes 327680 | tf_op jit(solution)/shard_map/all_to_all | solution.py:271
  23.5 15.7 %all_to_all.26 = f32[8,20,128]{2,1,0:T(8,128)S(1)} all-to-all(f32[8,20,128]{2,1,0:T(8,128)S(1)} %broadcast_in_dim.6), channel_id=1, replica_groups=mesh['x'=4,'y'=4,'core'=2,'z'=8] {'z'}, dimensions={0} | all-to-all | bytes 163840 | tf_op jit(solution)/shard_map/all_to_all | solution.py:235
  39.2 10.3 %all_to_all.27 = f32[16,20,128]{2,1,0:T(8,128)S(1)} all-to-all(f32[16,20,128]{2,1,0:T(8,128)S(1)} %broadcast_in_dim.7), channel_id=1, replica_groups=mesh['x'=4,'y'=4,'core'=2,'z'=8] {'x','y'}, dimensions={0} | all-to-all | bytes 327680 | tf_op jit(solution)/shard_map/all_to_all | solution.py:235
  49.5 4.4 %collective-permute-start.1 = (f32[320,128]{1,0:T(8,128)S(1)}, f32[320,128]{1,0:T(8,128)S(1)}, u32[]{:S(2)}, u32[]{:S(2)}) collective-permute-start(f32[320,128]{1,0:T(8,128)S(1)} %reshape.21.left_ref.mine_ref), channel_id=1, source_target_pairs={{0,8},{8,0},{1,9},{9,1},{2,10},{10,2},{3,11},{11,3},{4,12},{12,4},... | collective-permute-start | bytes 491528 | tf_op jit(solution)/shard_map/ppermute | solution.py:239
  53.9 1.0 collective-permute-done.1.left_ref.other_ref
  54.9 0.0 copy-start.1
  54.9 2.3 %copy-done.1 = f32[2,320,1792]{2,1,0:T(8,128)S(1)} copy-done((f32[2,320,1792]{2,1,0:T(8,128)S(1)}, f32[2,320,1792]{2,1,0:T(8,128)}, u32[]{:S(2)}) %copy-start.1) | copy-done | bytes 4587544
  57.2 0.8 right_other.1
  58.0 0.5 collective-permute-start.2
  58.5 0.8 right_mine.1
  59.3 1.3 %collective-permute-done.2 = f32[1792,128]{1,0:T(8,128)S(1)} collective-permute-done((f32[1792,128]{1,0:T(8,128)S(1)}, f32[1792,128]{1,0:T(8,128)S(1)}, u32[]{:S(2)}, u32[]{:S(2)}) %collective-permute-start.2) | collective-permute-done | bytes 917536 | tf_op jit(solution)/shard_map/ppermute | solution.py:239
  60.6 1.0 add.7.right_ref
  61.6 3.8 %all-to-all-start.3 = ((f32[16,112,128]{2,1,0:T(8,128)}), f32[16,112,128]{2,1,0:T(8,128)S(1)}, u32[]{:S(2)}, u32[]{:S(2)}) async-start(f32[16,112,128]{2,1,0:T(8,128)} %bitcast.2), calls=%async_computation.3 | async-start | bytes 1835008 | tf_op jit(solution)/shard_map/all_to_all | solution.py:287
  65.4 10.3 %basis.1 = (f32[2,320,128]{2,1,0:T(8,128)}, f32[128,128]{1,0:T(8,128)S(1)}) custom-call(f32[320,128]{1,0:T(8,128)S(1)} %reshape.21.left_ref.mine_ref, f32[320,128]{1,0:T(8,128)S(1)} %collective-permute-done.1.left_ref.other_ref, f32[1792,128]{1,0:T(8,128)} %add.7.right_ref), custom_call_target="tpu_custom_call" | custom-call | flops 10000000000 | bytes 800000 | tf_op jit(solution)/shard_map/basis/pallas_call | solution.py:278
  75.7 3.9 %all-to-all-done.3.part_ref = f32[16,112,128]{2,1,0:T(8,128)S(1)} async-done(((f32[16,112,128]{2,1,0:T(8,128)}), f32[16,112,128]{2,1,0:T(8,128)S(1)}, u32[]{:S(2)}, u32[]{:S(2)}) %all-to-all-start.3) | async-done | bytes 917536 | tf_op jit(solution)/shard_map/all_to_all | solution.py:287
  79.6 0.3 finish.1
  79.9 17.1 %all_to_all.28 = f32[16,112,128]{2,1,0:T(8,128)S(1)} all-to-all(f32[16,112,128]{2,1,0:T(8,128)S(1)} %finish.1), channel_id=1, replica_groups=mesh['x'=4,'y'=4,'core'=2,'z'=8] {'x','y'}, dimensions={0} | all-to-all | bytes 1835008 | tf_op jit(solution)/shard_map/all_to_all | solution.py:296
  97.0 3.5 %collective-permute-start.3 = (f32[1792,128]{1,0:T(8,128)S(1)}, f32[1792,128]{1,0:T(8,128)S(1)}, u32[]{:S(2)}, u32[]{:S(2)}) collective-permute-start(f32[1792,128]{1,0:T(8,128)S(1)} %bitcast.5), channel_id=1, source_target_pairs={{0,8},{8,0},{1,9},{9,1},{2,10},{10,2},{3,11},{11,3},{4,12},{12,4},... | collective-permute-start | bytes 2752520 | tf_op jit(solution)/shard_map/ppermute | solution.py:239
  100.6 0.0 copy-start.2
  100.6 2.3 %copy-done.2 = f32[2,320,1792]{2,1,0:T(8,128)S(1)} copy-done((f32[2,320,1792]{2,1,0:T(8,128)S(1)}, f32[2,320,1792]{2,1,0:T(8,128)}, u32[]{:S(2)}) %copy-start.2) | copy-done | bytes 4587544
  102.9 0.0 copy-start.3
  102.9 1.0 copy-done.3
  103.8 1.8 %update_mine.1 = (f32[2,320,1792]{2,1,0:T(8,128)}, f32[2,1792,128]{2,1,0:T(8,128)}) custom-call(f32[2,320,128]{2,1,0:T(8,128)S(1)} %copy-done.3, f32[1792,128]{1,0:T(8,128)S(1)} %bitcast.6, f32[2,320,1792]{2,1,0:T(8,128)S(1)} %copy-done.2), custom_call_target="tpu_custom_call" | custom-call | flops 440401920 | bytes 4587520 | tf_op jit(solution)/shard_map/update_mine/pallas_call | solution.py:213
  105.6 0.0 collective-permute-done.3.right_ref
  105.6 1.8 %update_other.1 = (f32[2,320,1792]{2,1,0:T(8,128)}, f32[2,1792,128]{2,1,0:T(8,128)}) custom-call(f32[2,320,128]{2,1,0:T(8,128)S(1)} %copy-done.3, f32[1792,128]{1,0:T(8,128)S(1)} %collective-permute-done.3.right_ref, f32[2,320,1792]{2,1,0:T(8,128)S(1)} %copy-done.2, ...), custom_call_target="tpu_custom_call", output_to_operand_aliasing={{0}: (3, {}), {1}: (4, {})} | custom-call | flops 440401920 | bytes 4587520 | tf_op jit(solution)/shard_map/update_other/pallas_call | solution.py:213
  (7 shorter events, 0.1 us)
Async XLA Ops:
  5.1 2.1 %copy-start = (f32[2,320,1792]{2,1,0:T(8,128)}, f32[2,320,1792]{2,1,0:T(8,128)S(1)}, u32[]{:S(2)}) copy-start(f32[2,320,1792]{2,1,0:T(8,128)S(1)} %get-tuple-element.14.sum_ref) | copy-start | bytes 13762564
  7.2 4.3 %collective-permute-start = (f32[320,128]{1,0:T(8,128)S(1)}, f32[320,128]{1,0:T(8,128)S(1)}, u32[]{:S(2)}, u32[]{:S(2)}) collective-permute-start(f32[320,128]{1,0:T(8,128)S(1)} %get-tuple-element.13), channel_id=1, source_target_pairs={{0,8},{8,0},{1,9},{9,1},{2,10},{10,2},{3,11},{11,3},{4,12},{12,4},... | collective-permute-start | bytes 491528 | tf_op jit(solution)/shard_map/ppermute | solution.py:239
  49.5 5.4 %collective-permute-start.1 = (f32[320,128]{1,0:T(8,128)S(1)}, f32[320,128]{1,0:T(8,128)S(1)}, u32[]{:S(2)}, u32[]{:S(2)}) collective-permute-start(f32[320,128]{1,0:T(8,128)S(1)} %reshape.21.left_ref.mine_ref), channel_id=1, source_target_pairs={{0,8},{8,0},{1,9},{9,1},{2,10},{10,2},{3,11},{11,3},{4,12},{12,4},... | collective-permute-start | bytes 491528 | tf_op jit(solution)/shard_map/ppermute | solution.py:239
  54.9 2.3 %copy-start.1 = (f32[2,320,1792]{2,1,0:T(8,128)S(1)}, f32[2,320,1792]{2,1,0:T(8,128)}, u32[]{:S(2)}) copy-start(f32[2,320,1792]{2,1,0:T(8,128)} %copy-done) | copy-start | bytes 13762564
  58.0 2.6 %collective-permute-start.2 = (f32[1792,128]{1,0:T(8,128)S(1)}, f32[1792,128]{1,0:T(8,128)S(1)}, u32[]{:S(2)}, u32[]{:S(2)}) collective-permute-start(f32[1792,128]{1,0:T(8,128)S(1)} %right_other.1), channel_id=1, source_target_pairs={{0,8},{8,0},{1,9},{9,1},{2,10},{10,2},{3,11},{11,3},{4,12},{12,4},... | collective-permute-start | bytes 2752520 | tf_op jit(solution)/shard_map/ppermute | solution.py:239
  61.6 18.0 %all-to-all-start.3 = ((f32[16,112,128]{2,1,0:T(8,128)}), f32[16,112,128]{2,1,0:T(8,128)S(1)}, u32[]{:S(2)}, u32[]{:S(2)}) async-start(f32[16,112,128]{2,1,0:T(8,128)} %bitcast.2), calls=%async_computation.3 | async-start | bytes 1835008 | tf_op jit(solution)/shard_map/all_to_all | solution.py:287
  97.0 8.6 %collective-permute-start.3 = (f32[1792,128]{1,0:T(8,128)S(1)}, f32[1792,128]{1,0:T(8,128)S(1)}, u32[]{:S(2)}, u32[]{:S(2)}) collective-permute-start(f32[1792,128]{1,0:T(8,128)S(1)} %bitcast.5), channel_id=1, source_target_pairs={{0,8},{8,0},{1,9},{9,1},{2,10},{10,2},{3,11},{11,3},{4,12},{12,4},... | collective-permute-start | bytes 2752520 | tf_op jit(solution)/shard_map/ppermute | solution.py:239
  100.6 2.3 %copy-start.2 = (f32[2,320,1792]{2,1,0:T(8,128)S(1)}, f32[2,320,1792]{2,1,0:T(8,128)}, u32[]{:S(2)}) copy-start(f32[2,320,1792]{2,1,0:T(8,128)} %copy-done) | copy-start | bytes 13762564
  102.9 1.0 copy-start.3

commit v4 on v3

--- a/solution.py
+++ b/solution.py
@@ -13,6 +13,7 @@
 CORES = 2
 CHUNK = 256
 GROUP = 8
+TILE = 8
 MIB = 1024 * 1024
 
 unit_scale = 3.4641016
@@ -58,20 +59,24 @@
     return (hashed.astype(f32) * (1.0 / PRIME) - 0.5) * unit_scale
 
 
-def left_kernel(seed_ref, grad_hbm, feed_hbm, mine_ref, other_ref, sum_ref, grad_ref, start_ref, sems):
-    steps = grad_ref.shape[2] // CHUNK
-    seed = seed_ref[0]
-    first = lax.axis_index("z") * grad_ref.shape[2]
+def left_kernel(seed_ref, grad_hbm, feed_hbm, mine_ref, other_ref, mine_sum_ref, other_sum_ref, grad_ref, start_ref, sems):
+    _, rows, columns = grad_ref.shape
+    steps = columns // CHUNK
+    slots = ((mine_ref, mine_sum_ref), (other_ref, other_sum_ref))
+    first = lax.axis_index("z") * columns
     core = lax.axis_index("core")
     copies = []
     for j in range(steps):
-        pair = (
-            pltpu.make_async_copy(grad_hbm.at[:, :, cols(j)], grad_ref.at[:, :, cols(j)], sems.at[j, 0]),
-            pltpu.make_async_copy(feed_hbm.at[:, :, cols(j)], sum_ref.at[:, :, cols(j)], sems.at[j, 1]),
-        )
-        for copy in pair:
+        group = [pltpu.make_async_copy(grad_hbm.at[:, :, cols(j)], grad_ref.at[:, :, cols(j)], sems.at[j, 0])]
+        for slot, (_, sum_ref) in enumerate(slots):
+            source = feed_hbm.at[core ^ slot, :, cols(j)]
+            group.append(pltpu.make_async_copy(source, sum_ref.at[:, cols(j)], sems.at[j, 1 + slot]))
+        for copy in group:
             copy.start()
-        copies.append(pair)
+        copies.append(group)
+    for ref, _ in slots:
+        ref[rows:, :] = jnp.zeros((ref.shape[0] - rows, RANK), f32)
+    seed = seed_ref[0]
     for j in range(steps):
         high, low = split(start_block(seed, first + j * CHUNK, CHUNK))
         start_ref[cols(j), :RANK] = high
@@ -80,17 +85,16 @@
         for copy in copies[j]:
             copy.wait()
         both = start_ref[cols(j), :]
-        for slot, ref in enumerate((mine_ref, other_ref)):
-            m = core ^ slot
-            summed = grad_ref[m, :, cols(j)].astype(f32) + sum_ref[m, :, cols(j)]
-            sum_ref[m, :, cols(j)] = summed
+        for slot, (ref, sum_ref) in enumerate(slots):
+            summed = grad_ref[core ^ slot, :, cols(j)].astype(f32) + sum_ref[:, cols(j)]
+            sum_ref[:, cols(j)] = summed
             s_high, s_low = split(summed)
             wide = dot(s_high, both)
             part = wide[:, :RANK] + wide[:, RANK:] + dot(s_low, both[:, :RANK])
             if j == 0:
-                ref[...] = part
+                ref[:rows, :] = part
             else:
-                ref[...] += part
+                ref[:rows, :] += part
 
 
 def eliminate(gram):
@@ -141,7 +145,7 @@
     i = lax.broadcasted_iota(jnp.int32, (RANK, RANK), 0)
     j = lax.broadcasted_iota(jnp.int32, (RANK, RANK), 1)
     for slot, ref in enumerate((mine_ref, other_ref)):
-        left = ref[...] * (1.0 / 32)
+        left = ref[: basis_ref.shape[1], :] * (1.0 / 32)
         lower, pivots = eliminate(exact_dot(left, left, ((0,), (0,))))
         inverse = jnp.where(i > j, lower, jnp.where(i == j, 1.0, 0.0)) * lax.rsqrt(pivots)
         if slot == 0:
@@ -149,16 +153,29 @@
         basis_ref[core ^ slot] = exact_dot(left, inverse, ((1,), (1,)))
 
 
-def right_kernel(slot, left_ref, sum_ref, out_ref):
-    m = lax.axis_index("core") ^ slot
-    high, low = split(left_ref[...] * (1.0 / 32))
+def right_kernel(left_ref, *rest):
+    keeps = []
+    if len(rest) == 2:
+        sum_ref, out_ref = rest
+    else:
+        sum_ref, other_ref, out_ref, sum_hbm, other_hbm, sems = rest
+        keeps = [
+            pltpu.make_async_copy(sum_ref, sum_hbm, sems.at[0]),
+            pltpu.make_async_copy(other_ref, other_hbm, sems.at[1]),
+        ]
+    for keep in keeps:
+        keep.start()
+    rows, columns = sum_ref.shape
+    high, low = split(left_ref[:rows, :] * (1.0 / 32))
     first = jnp.concatenate([high, low], axis=1)
     second = jnp.concatenate([high, jnp.zeros_like(low)], axis=1)
     stack = jnp.concatenate([first, second], axis=0)
-    for j in range(sum_ref.shape[2] // CHUNK):
-        s_high, s_low = split(sum_ref[m, :, cols(j)])
+    for j in range(columns // CHUNK):
+        s_high, s_low = split(sum_ref[:, cols(j)])
         wide = dot(jnp.concatenate([s_high, s_low], axis=0), stack, ((0,), (0,)))
         out_ref[cols(j), :] = wide[:, :RANK] + wide[:, RANK:]
+    for keep in keeps:
+        keep.wait()
 
 
 def finish_kernel(part_ref, inverse_ref, out_ref):
@@ -181,7 +198,7 @@
         r_high, r_low = split(right_ref[cols(j), :])
         rebuilt = dot(wide, jnp.concatenate([r_high, r_high], axis=1), ((1,), (1,)))
         rebuilt = rebuilt + dot(high, r_low, ((1,), (1,)))
-        out_ref[:, cols(j)] = sum_ref[m, :, cols(j)] - rebuilt
+        out_ref[:, cols(j)] = sum_ref[:, cols(j)] - rebuilt
         copy = pltpu.make_async_copy(out_ref.at[:, cols(j)], out_hbm.at[m, :, cols(j)], sems.at[1 + j])
         copy.start()
         copies.append(copy)
@@ -193,23 +210,27 @@
     return pltpu.CompilerParams(vmem_limit_bytes=mib * MIB)
 
 
-def right_part(slot, left, summed):
-    _, rows, columns = summed.shape
-    return pl.pallas_call(
-        functools.partial(right_kernel, slot),
-        in_specs=[vmem, vmem],
-        out_specs=vmem,
-        out_shape=pltpu.VMEM((columns, RANK), f32),
+def right_part(name, left, *summed):
+    rows, columns = summed[0].shape
+    kept = len(summed) if len(summed) > 1 else 0
+    out = pl.pallas_call(
+        right_kernel,
+        in_specs=[vmem] * (1 + len(summed)),
+        out_specs=[vmem] + [hbm] * kept,
+        out_shape=[pltpu.VMEM((columns, RANK), f32)] + [pltpu.HBM((rows, columns), f32)] * kept,
+        scratch_shapes=[pltpu.SemaphoreType.DMA((kept,))] if kept else [],
         cost_estimate=pl.CostEstimate(
             flops=6 * rows * columns * RANK, bytes_accessed=4 * rows * columns, transcendentals=0
         ),
         compiler_params=params(8),
-        name=("right_mine", "right_other")[slot],
-    )(left, summed)
+        name=name,
+    )(left, *summed)
+    return out if kept else out[0]
 
 
 def update(slot, basis, right, summed, previous=()):
-    mats, rows, columns = summed.shape
+    mats = basis.shape[0]
+    rows, columns = summed.shape
     return pl.pallas_call(
         functools.partial(update_kernel, slot),
         in_specs=[vmem, vmem, vmem] + [hbm] * len(previous),
@@ -231,8 +252,23 @@
     )(basis, right, summed, *previous)
 
 
-def spread(x, axes, count):
-    return lax.all_to_all(jnp.broadcast_to(x[None], (count,) + x.shape), axes, 0, 0)
+def sum_kernel(part_ref, out_ref):
+    total = part_ref[0]
+    for i in range(1, part_ref.shape[0]):
+        total = total + part_ref[i]
+    for i in range(out_ref.shape[0]):
+        out_ref[i] = total
+
+
+def sum_spread(parts, count):
+    return pl.pallas_call(
+        sum_kernel,
+        in_specs=[vmem],
+        out_specs=vmem,
+        out_shape=pltpu.VMEM((count,) + parts.shape[1:], f32),
+        compiler_params=params(4),
+        name="sum_spread",
+    )(parts)
 
 
 def swap(x):
@@ -245,19 +281,23 @@
     chips = SIDE * SIDE
     depth = lax.axis_size("z")
 
-    mine, other, summed = pl.pallas_call(
+    share = -(-rows // (chips * TILE)) * TILE
+    padded = chips * share
+
+    mine, other, mine_sum, other_sum = pl.pallas_call(
         left_kernel,
         in_specs=[smem, hbm, hbm],
-        out_specs=[vmem, vmem, vmem],
+        out_specs=[vmem] * 4,
         out_shape=[
-            pltpu.VMEM((rows, RANK), f32),
-            pltpu.VMEM((rows, RANK), f32),
-            pltpu.VMEM((mats, rows, columns), f32),
+            pltpu.VMEM((padded, RANK), f32),
+            pltpu.VMEM((padded, RANK), f32),
+            pltpu.VMEM((rows, columns), f32),
+            pltpu.VMEM((rows, columns), f32),
         ],
         scratch_shapes=[
             pltpu.VMEM((mats, rows, columns), bf16),
             pltpu.VMEM((columns, 2 * RANK), bf16),
-            pltpu.SemaphoreType.DMA((columns // CHUNK, 2)),
+            pltpu.SemaphoreType.DMA((columns // CHUNK, 3)),
         ],
         compiler_params=params(12),
         name="left_part",
@@ -268,16 +308,17 @@
     )
 
     left = mine + swap(other)
-    left = lax.all_to_all(left.reshape(chips, rows // chips, RANK), ("x", "y"), 0, 0).sum(0)
-    left = spread(left, "z", depth).sum(0)
-    left_mine = spread(left, ("x", "y"), chips).reshape(rows, RANK)
+    left = lax.all_to_all(left.reshape(chips, share, RANK), ("x", "y"), 0, 0)
+    left = lax.all_to_all(sum_spread(left, depth), "z", 0, 0)
+    left_mine = lax.all_to_all(sum_spread(left, chips), ("x", "y"), 0, 0).reshape(padded, RANK)
     left_other = swap(left_mine)
 
-    sent = swap(right_part(1, left_other, summed))
-    right = right_part(0, left_mine, summed) + sent
+    sent = swap(right_part("right_other", left_other, other_sum))
+    right, mine_sum, other_sum = right_part("right_mine", left_mine, mine_sum, other_sum)
+    right = right + sent
     left_basis, inverse = pl.pallas_call(
         basis_kernel,
-        in_specs=[vmem, vmem, pl.BlockSpec(memory_space=pl.ANY)],
+        in_specs=[vmem, vmem, hbm],
         out_specs=[vmem, vmem],
         out_shape=[jax.ShapeDtypeStruct((mats, rows, RANK), f32), pltpu.VMEM((RANK, RANK), f32)],
         cost_estimate=pl.CostEstimate(flops=10_000_000_000, bytes_accessed=800_000, transcendentals=0),
@@ -296,8 +337,8 @@
     right_mine = lax.all_to_all(right, ("x", "y"), 0, 0).reshape(columns, RANK)
     right_other = swap(right_mine)
 
-    outs = update(0, left_basis, right_mine, summed)
-    new_feedback, right_factor = update(1, left_basis, right_other, summed, outs)
+    outs = update(0, left_basis, right_mine, mine_sum)
+    new_feedback, right_factor = update(1, left_basis, right_other, other_sum, outs)
     return new_feedback[None], left_basis, right_factor
 
 

time: 108 us -> 102 us (0.944)
  local copies, waits for them, and re-layouts: 7.76 us -> 1.47 us
  Pallas kernels: 19.6 us -> 21 us
  waiting for transfers between devices: 7.22 us -> 5.95 us
    unnamed x8 -> x10, local copies, waits for them, and re-layouts: 7.71 us -> 1.47 us
    pallas_call x4 -> x6, Pallas kernels: 15.7 us -> 17.2 us  [the longest x1 10.3 us: on_device(): pl.pallas_call(basis_kernel, in_specs=[vmem, vmem, hbm], out_specs=[vmem,...]
  transfers between devices with their start and end apart: 5 -> 5, of which waited for: 4 -> 4; matrix products, arithmetic and copies ran while one was open for 0% -> 0% of each run, Pallas kernels for 12% -> 14%
where the time goes in v4:
time: 102 us; the launch traced here: 101 us
  blocking collectives  55 us (54%)
  Pallas kernels  21 us (21%)
  starting transfers between devices  15.3 us (15%)
  waiting for transfers between devices  5.95 us (6%)
  between operations  1.52 us (1%)
  local copies, waits for them, and re-layouts  1.47 us (1%)
  other arithmetic  1.05 us (1%)
    all_to_all x1, blocking collectives, on_device(): right_mine = lax.all_to_all(right, ('x', 'y'), 0, 0).reshape(columns, RANK)  17.2 us
    all_to_all x1, blocking collectives, on_device(): left = lax.all_to_all(sum_spread(left, depth), 'z', 0, 0)  15.7 us
    all_to_all x1, blocking collectives, on_device(): left = lax.all_to_all(left.reshape(chips, share, RANK), ('x', 'y'), 0, 0)  11.9 us
    ppermute x4, starting transfers between devices, swap(): return lax.ppermute(x, 'core', [(0, 1), (1, 0)])  11.5 us
    pallas_call x1, Pallas kernels, on_device(): pl.pallas_call(basis_kernel, in_specs=[vmem, vmem, hbm], out_specs=[vmem,...  10.3 us
    all_to_all x1, blocking collectives, on_device(): lax.all_to_all(sum_spread(left, chips), ('x', 'y'), 0, 0)  10.3 us
    pallas_call x1, Pallas kernels, on_device(): pl.pallas_call(left_kernel, in_specs=[smem, hbm, hbm], out_specs=[vmem] *...  3.87 us
    all_to_all x1, starting transfers between devices, on_device(): lax.all_to_all(right.reshape(chips, columns // chips, RANK), ('x', 'y'),...  3.82 us
  transfers between devices with their start and end apart: 5, of which 4 were waited for; matrix products, arithmetic and copies ran while one was open for 0% of the time, Pallas kernels for 14%

profile of v4, /device:TPU:1, one launch (start us, length us, event | category | flops | bytes accessed | tf_op | source)
XLA Modules:
  0.0 101.4 jit_solution(17656145568630828691)
XLA Ops:
  1.3 3.9 %left_part.1 = (f32[384,128]{1,0:T(8,128)S(1)}, f32[384,128]{1,0:T(8,128)S(1)}, f32[320,1792]{1,0:T(8,128)S(1)}, f32[320,1792]{1,0:T(8,128)S(1)}) custom-call(s32[1]{0:T(128)S(6)} %copy.10.seed_ref, bf16[2,320,1792]{2,1,0:T(8,128)(2,1)} %bitcast.14, f32[2,320,1792]{2,1,0:T(8,128)} %bitcast.13), custom_call_target="tpu_custom_call" | custom-call | tf_op jit(solution)/shard_map/left_part/pallas_call | solution.py:287
  5.2 3.3 %collective-permute-start = (f32[384,128]{1,0:T(8,128)S(1)}, f32[384,128]{1,0:T(8,128)S(1)}, u32[]{:S(2)}, u32[]{:S(2)}) collective-permute-start(f32[384,128]{1,0:T(8,128)S(1)} %get-tuple-element.17), channel_id=1, source_target_pairs={{0,8},{8,0},{1,9},{9,1},{2,10},{10,2},{3,11},{11,3},{4,12},{12,4},... | collective-permute-start | bytes 589832 | tf_op jit(solution)/shard_map/ppermute | solution.py:275
  8.5 1.1 %collective-permute-done = f32[384,128]{1,0:T(8,128)S(1)} collective-permute-done((f32[384,128]{1,0:T(8,128)S(1)}, f32[384,128]{1,0:T(8,128)S(1)}, u32[]{:S(2)}, u32[]{:S(2)}) %collective-permute-start) | collective-permute-done | bytes 196640 | tf_op jit(solution)/shard_map/ppermute | solution.py:275
  9.6 11.9 %all_to_all.25.part_ref = f32[16,24,128]{2,1,0:T(8,128)S(1)} all-to-all(f32[16,24,128]{2,1,0:T(8,128)S(1)} %bitcast.15), channel_id=1, replica_groups=mesh['x'=4,'y'=4,'core'=2,'z'=8] {'x','y'}, dimensions={0} | all-to-all | bytes 393216 | tf_op jit(solution)/shard_map/all_to_all | solution.py:311
  21.5 15.7 %all_to_all.26.part_ref = f32[8,24,128]{2,1,0:T(8,128)S(1)} all-to-all(f32[8,24,128]{2,1,0:T(8,128)S(1)} %sum_spread.2), channel_id=1, replica_groups=mesh['x'=4,'y'=4,'core'=2,'z'=8] {'z'}, dimensions={0} | all-to-all | bytes 196608 | tf_op jit(solution)/shard_map/all_to_all | solution.py:312
  37.2 10.3 %all_to_all.27 = f32[16,24,128]{2,1,0:T(8,128)S(1)} all-to-all(f32[16,24,128]{2,1,0:T(8,128)S(1)} %sum_spread.3), channel_id=1, replica_groups=mesh['x'=4,'y'=4,'core'=2,'z'=8] {'x','y'}, dimensions={0} | all-to-all | bytes 393216 | tf_op jit(solution)/shard_map/all_to_all | solution.py:313
  47.5 4.3 %collective-permute-start.1 = (f32[384,128]{1,0:T(8,128)S(1)}, f32[384,128]{1,0:T(8,128)S(1)}, u32[]{:S(2)}, u32[]{:S(2)}) collective-permute-start(f32[384,128]{1,0:T(8,128)S(1)} %bitcast.9), channel_id=1, source_target_pairs={{0,8},{8,0},{1,9},{9,1},{2,10},{10,2},{3,11},{11,3},{4,12},{12,4},... | collective-permute-start | bytes 589832 | tf_op jit(solution)/shard_map/ppermute | solution.py:275
  51.8 1.1 %collective-permute-done.1.left_ref.other_ref = f32[384,128]{1,0:T(8,128)S(1)} collective-permute-done((f32[384,128]{1,0:T(8,128)S(1)}, f32[384,128]{1,0:T(8,128)S(1)}, u32[]{:S(2)}, u32[]{:S(2)}) %collective-permute-start.1) | collective-permute-done | bytes 196640 | tf_op jit(solution)/shard_map/ppermute | solution.py:275
  52.8 0.8 right_other.1
  53.7 0.5 collective-permute-start.2
  54.1 2.2 %right_mine.1 = (f32[1792,128]{1,0:T(8,128)S(1)}, f32[320,1792]{1,0:T(8,128)}, f32[320,1792]{1,0:T(8,128)}) custom-call(f32[384,128]{1,0:T(8,128)S(1)} %bitcast.10, f32[320,1792]{1,0:T(8,128)S(1)} %get-tuple-element.18.rest_0_, f32[320,1792]{1,0:T(8,128)S(1)} %get-tuple-element.19.rest_1_.rest_0_), custom_call_target="tpu_custom_call" | custom-call | flops 440401920 | bytes 2293760 | tf_op jit(solution)/shard_map/right_mine/pallas_call | solution.py:216
  56.3 0.0 collective-permute-done.2
  56.3 1.0 %add.7.right_ref = f32[1792,128]{1,0:T(8,128)} add(f32[1792,128]{1,0:T(8,128)S(1)} %get-tuple-element.20, f32[1792,128]{1,0:T(8,128)S(1)} %collective-permute-done.2) | non-fusion elementwise | flops 229376 | bytes 2752512 | tf_op jit(solution)/shard_map/add | solution.py:318
  57.3 3.8 %all-to-all-start.3 = ((f32[16,112,128]{2,1,0:T(8,128)}), f32[16,112,128]{2,1,0:T(8,128)S(1)}, u32[]{:S(2)}, u32[]{:S(2)}) async-start(f32[16,112,128]{2,1,0:T(8,128)} %bitcast.4), calls=%async_computation.3 | async-start | bytes 1835008 | tf_op jit(solution)/shard_map/all_to_all | solution.py:328
  61.1 10.3 %basis.1 = (f32[2,320,128]{2,1,0:T(8,128)}, f32[128,128]{1,0:T(8,128)S(1)}) custom-call(f32[384,128]{1,0:T(8,128)S(1)} %bitcast.11, f32[384,128]{1,0:T(8,128)S(1)} %collective-permute-done.1.left_ref.other_ref, f32[1792,128]{1,0:T(8,128)} %add.7.right_ref), custom_call_target="tpu_custom_call" | custom-call | flops 10000000000 | bytes 800000 | tf_op jit(solution)/shard_map/basis/pallas_call | solution.py:319
  71.4 0.0 copy-start.3
  71.4 0.6 copy-done.3
  72.0 0.0 copy-start.1
  72.0 0.0 copy-start.2
  72.0 3.5 %all-to-all-done.3.part_ref = f32[16,112,128]{2,1,0:T(8,128)S(1)} async-done(((f32[16,112,128]{2,1,0:T(8,128)}), f32[16,112,128]{2,1,0:T(8,128)S(1)}, u32[]{:S(2)}, u32[]{:S(2)}) %all-to-all-start.3) | async-done | bytes 917536 | tf_op jit(solution)/shard_map/all_to_all | solution.py:328
  75.6 0.0 copy-start.4
  75.6 0.8 copy-done.4
  76.4 0.3 finish.1
  76.7 0.0 copy-start
  76.7 17.2 %all_to_all.28 = f32[16,112,128]{2,1,0:T(8,128)S(1)} all-to-all(f32[16,112,128]{2,1,0:T(8,128)S(1)} %finish.1), channel_id=1, replica_groups=mesh['x'=4,'y'=4,'core'=2,'z'=8] {'x','y'}, dimensions={0} | all-to-all | bytes 1835008 | tf_op jit(solution)/shard_map/all_to_all | solution.py:337
  93.9 3.4 %collective-permute-start.3 = (f32[1792,128]{1,0:T(8,128)S(1)}, f32[1792,128]{1,0:T(8,128)S(1)}, u32[]{:S(2)}, u32[]{:S(2)}) collective-permute-start(f32[1792,128]{1,0:T(8,128)S(1)} %bitcast.7), channel_id=1, source_target_pairs={{0,8},{8,0},{1,9},{9,1},{2,10},{10,2},{3,11},{11,3},{4,12},{12,4},... | collective-permute-start | bytes 2752520 | tf_op jit(solution)/shard_map/ppermute | solution.py:275
  97.3 0.0 copy-done.1
  97.3 0.0 copy-done.2
  97.4 1.8 %update_mine.1 = (f32[2,320,1792]{2,1,0:T(8,128)}, f32[2,1792,128]{2,1,0:T(8,128)}) custom-call(f32[2,320,128]{2,1,0:T(8,128)S(1)} %copy-done.2, f32[1792,128]{1,0:T(8,128)S(1)} %bitcast.8, f32[320,1792]{1,0:T(8,128)S(1)} %copy-done.1), custom_call_target="tpu_custom_call" | custom-call | flops 440401920 | bytes 4587520 | tf_op jit(solution)/shard_map/update_mine/pallas_call | solution.py:234
  99.1 0.3 collective-permute-done.3.right_ref
  99.4 0.0 copy-done
  99.5 1.8 %update_other.1 = (f32[2,320,1792]{2,1,0:T(8,128)}, f32[2,1792,128]{2,1,0:T(8,128)}) custom-call(f32[2,320,128]{2,1,0:T(8,128)S(1)} %copy-done.2, f32[1792,128]{1,0:T(8,128)S(1)} %collective-permute-done.3.right_ref, f32[320,1792]{1,0:T(8,128)S(1)} %copy-done, ...), custom_call_target="tpu_custom_call", output_to_operand_aliasing={{0}: (3, {}), {1}: (4, {})} | custom-call | flops 440401920 | bytes 4587520 | tf_op jit(solution)/shard_map/update_other/pallas_call | solution.py:234
  (3 shorter events, 0.1 us)
Async XLA Ops:
  5.2 4.4 %collective-permute-start = (f32[384,128]{1,0:T(8,128)S(1)}, f32[384,128]{1,0:T(8,128)S(1)}, u32[]{:S(2)}, u32[]{:S(2)}) collective-permute-start(f32[384,128]{1,0:T(8,128)S(1)} %get-tuple-element.17), channel_id=1, source_target_pairs={{0,8},{8,0},{1,9},{9,1},{2,10},{10,2},{3,11},{11,3},{4,12},{12,4},... | collective-permute-start | bytes 589832 | tf_op jit(solution)/shard_map/ppermute | solution.py:275
  47.5 5.4 %collective-permute-start.1 = (f32[384,128]{1,0:T(8,128)S(1)}, f32[384,128]{1,0:T(8,128)S(1)}, u32[]{:S(2)}, u32[]{:S(2)}) collective-permute-start(f32[384,128]{1,0:T(8,128)S(1)} %bitcast.9), channel_id=1, source_target_pairs={{0,8},{8,0},{1,9},{9,1},{2,10},{10,2},{3,11},{11,3},{4,12},{12,4},... | collective-permute-start | bytes 589832 | tf_op jit(solution)/shard_map/ppermute | solution.py:275
  53.7 2.6 %collective-permute-start.2 = (f32[1792,128]{1,0:T(8,128)S(1)}, f32[1792,128]{1,0:T(8,128)S(1)}, u32[]{:S(2)}, u32[]{:S(2)}) collective-permute-start(f32[1792,128]{1,0:T(8,128)S(1)} %right_other.1), channel_id=1, source_target_pairs={{0,8},{8,0},{1,9},{9,1},{2,10},{10,2},{3,11},{11,3},{4,12},{12,4},... | collective-permute-start | bytes 2752520 | tf_op jit(solution)/shard_map/ppermute | solution.py:275
  57.3 18.2 %all-to-all-start.3 = ((f32[16,112,128]{2,1,0:T(8,128)}), f32[16,112,128]{2,1,0:T(8,128)S(1)}, u32[]{:S(2)}, u32[]{:S(2)}) async-start(f32[16,112,128]{2,1,0:T(8,128)} %bitcast.4), calls=%async_computation.3 | async-start | bytes 1835008 | tf_op jit(solution)/shard_map/all_to_all | solution.py:328
  71.4 0.6 copy-start.3
  72.0 25.3 %copy-start.1 = (f32[320,1792]{1,0:T(8,128)S(1)}, f32[320,1792]{1,0:T(8,128)}, u32[]{:S(2)}) copy-start(f32[320,1792]{1,0:T(8,128)} %get-tuple-element.24.sum_ref) | copy-start | bytes 6881284
  72.0 25.3 %copy-start.2 = (f32[2,320,128]{2,1,0:T(8,128)S(1)}, f32[2,320,128]{2,1,0:T(8,128)}, u32[]{:S(2)}) copy-start(f32[2,320,128]{2,1,0:T(8,128)} %get-tuple-element.14.basis_ref) | copy-start | bytes 983044
  75.6 0.8 copy-start.4
  76.7 22.8 %copy-start = (f32[320,1792]{1,0:T(8,128)S(1)}, f32[320,1792]{1,0:T(8,128)}, u32[]{:S(2)}) copy-start(f32[320,1792]{1,0:T(8,128)} %get-tuple-element.23.sum_ref) | copy-start | bytes 6881284
  93.9 5.5 %collective-permute-start.3 = (f32[1792,128]{1,0:T(8,128)S(1)}, f32[1792,128]{1,0:T(8,128)S(1)}, u32[]{:S(2)}, u32[]{:S(2)}) collective-permute-start(f32[1792,128]{1,0:T(8,128)S(1)} %bitcast.7), channel_id=1, source_target_pairs={{0,8},{8,0},{1,9},{9,1},{2,10},{10,2},{3,11},{11,3},{4,12},{12,4},... | collective-permute-start | bytes 2752520 | tf_op jit(solution)/shard_map/ppermute | solution.py:275

commit v5 on v2

v5 whole, which is shorter than its diff:
```python
import functools

import jax
import jax.numpy as jnp
from jax import lax
from jax.experimental import pallas as pl
from jax.experimental.pallas import tpu as pltpu
from jax.sharding import Mesh, PartitionSpec as P

RANK = 128
PRIME = 32749
CHIPS = 16
CHUNK = 256
LANES = 128
GROUP = 8
TILE = 8
MIB = 1024 * 1024

unit_scale = 3.4641016
f32 = jnp.float32
bf16 = jnp.bfloat16

smem = pl.BlockSpec(memory_space=pltpu.SMEM)
hbm = pl.BlockSpec(memory_space=pltpu.HBM)
vmem = pl.BlockSpec(memory_space=pltpu.VMEM)

PLANE = ("xh", "xl", "yh", "yl")


def split(x):
    high = x.astype(bf16)
    return high, (x - high.astype(f32)).astype(bf16)


def dot(a, b, contract=((1,), (0,))):
    return lax.dot_general(a, b, (contract, ((), ())), preferred_element_type=f32)


def exact_dot(a, b, contract):
    return lax.dot_general(
        a, b, (contract, ((), ())), precision=lax.Precision.HIGHEST, preferred_element_type=f32
    )


def cols(j):
    return pl.ds(j * CHUNK, CHUNK)


def params(mib):
    return pltpu.CompilerParams(vmem_limit_bytes=mib * MIB)


def centred(x):
    quotient = (x.astype(f32) * (1.0 / PRIME) + 0.5).astype(jnp.int32)
    return x - quotient * PRIME


def start_block(seed, first, columns):
    col = first + lax.broadcasted_iota(jnp.int32, (columns, RANK), 0)
    rank = lax.broadcasted_iota(jnp.int32, (columns, RANK), 1)
    hashed = centred(col * 131 + rank * 977 + seed)
    hashed = centred(hashed * hashed + rank * 17 + 7)
    hashed = centred(hashed * hashed + col)
    hashed = jnp.where(hashed < 0, hashed + PRIME, hashed)
    return (hashed.astype(f32) * (1.0 / PRIME) - 0.5) * unit_scale


def places(tile):
    xh, xl, yh, yl = tile >> 3, (tile >> 2) & 1, (tile >> 1) & 1, tile & 1
    rest = 2 * xh + yh
    far_x, far_y = xl ^ lax.axis_index("xl"), yl ^ lax.axis_index("yl")
    return 8 * far_x + 4 * far_y + rest, 8 * far_y + 4 * far_x + rest


def left_kernel(seed_ref, grad_hbm, feed_hbm, *refs):
    lefts, uppers, lowers, sums = (refs[n : n + 2] for n in range(0, 8, 2))
    grad_ref, feed_ref, start_ref, sems = refs[8:]
    _, rows, columns = grad_ref.shape
    half = rows // 2
    steps = columns // CHUNK
    seed = seed_ref[0]
    first = lax.axis_index("z") * columns
    core = lax.axis_index("core")
    copies = []
    for j in range(steps):
        pair = (
            pltpu.make_async_copy(grad_hbm.at[:, :, cols(j)], grad_ref.at[:, :, cols(j)], sems.at[j, 0]),
            pltpu.make_async_copy(feed_hbm.at[:, :, cols(j)], feed_ref.at[:, :, cols(j)], sems.at[j, 1]),
        )
        for copy in pair:
            copy.start()
        copies.append(pair)
    for left_ref in lefts:
        left_ref[rows:, :] = jnp.zeros((left_ref.shape[0] - rows, RANK), f32)
    for tile in range(columns // LANES, CHIPS):
        upper, lower = places(tile)
        for slot in range(2):
            uppers[slot][upper] = jnp.zeros((half, LANES), f32)
            lowers[slot][lower] = jnp.zeros((half, LANES), f32)
    for j in range(steps):
        high, low = split(start_block(seed, first + j * CHUNK, CHUNK))
        start_ref[cols(j), :RANK] = high
        start_ref[cols(j), RANK:] = low
    saves = []
    for j in range(steps):
        for copy in copies[j]:
            copy.wait()
        both = start_ref[cols(j), :]
        for slot in range(2):
            m = core ^ slot
            summed = grad_ref[m, :, cols(j)].astype(f32) + feed_ref[m, :, cols(j)]
            feed_ref[m, :, cols(j)] = summed
            save = pltpu.make_async_copy(feed_ref.at[m, :, cols(j)], sums[slot].at[:, cols(j)], sems.at[j, 2 + slot])
            save.start()
            saves.append(save)
            for part in range(CHUNK // LANES):
                upper, lower = places(j * (CHUNK // LANES) + part)
                span = slice(part * LANES, (part + 1) * LANES)
                uppers[slot][upper] = summed[:half, span]
                lowers[slot][lower] = summed[half:, span]
            s_high, s_low = split(summed)
            wide = dot(s_high, both)
            piece = wide[:, :RANK] + wide[:, RANK:] + dot(s_low, both[:, :RANK])
            if j == 0:
                lefts[slot][:rows, :] = piece
            else:
                lefts[slot][:rows, :] += piece
    for save in saves:
        save.wait()


def eliminate(gram):
    lane = lax.broadcasted_iota(jnp.int32, (1, RANK), 1)
    count = RANK // GROUP
    blocks = [gram[GROUP * b : GROUP * (b + 1), :] for b in range(count)]
    sub = lax.broadcasted_iota(jnp.int32, (GROUP, RANK), 0)
    pivots = []
    for b in range(count):
        start = GROUP * b
        panel = blocks[b]
        spread_cols = [jnp.broadcast_to(panel[:, start + t : start + t + 1], (GROUP, RANK)) for t in range(GROUP)]
        a = [[spread_cols[t][s : s + 1, :] for t in range(GROUP)] for s in range(GROUP)]
        factors = [[None] * GROUP for _ in range(GROUP)]
        inverses = []
        for t in range(GROUP):
            pivots.append(a[t][t])
            inverses.append(1.0 / a[t][t])
            for s in range(t + 1, GROUP):
                factors[s][t] = a[s][t] * inverses[t]
                for u in range(t + 1, GROUP):
                    a[s][u] = a[s][u] - factors[s][t] * a[t][u]
        rows, sources = [], []
        for s in range(GROUP):
            row = panel[s : s + 1, :]
            for t in range(s):
                row = jnp.where(lane == start + t, 0.0, row) - factors[s][t] * sources[t]
            rows.append(row)
            sources.append(jnp.where(lane == start + s, 1.0, row))
        for s in range(GROUP):
            panel = jnp.where(sub == s, rows[s], panel)
        blocks[b] = panel
        for later in range(b + 1, count):
            block = blocks[later]
            heads = [jnp.broadcast_to(block[:, start + t : start + t + 1], (GROUP, RANK)) for t in range(GROUP)]
            for t in range(GROUP):
                factor = heads[t] * inverses[t]
                for u in range(t + 1, GROUP):
                    heads[u] = heads[u] - factor * a[t][u]
                block = jnp.where(lane == start + t, 0.0, block) - factor * sources[t]
            blocks[later] = block
    return jnp.concatenate(blocks, axis=0), jnp.concatenate(pivots, axis=0)


def basis_kernel(left_ref, after_ref, basis_ref):
    del after_ref
    left = left_ref[: basis_ref.shape[0], :] * (1.0 / 32)
    lower, pivots = eliminate(exact_dot(left, left, ((0,), (0,))))
    i = lax.broadcasted_iota(jnp.int32, (RANK, RANK), 0)
    j = lax.broadcasted_iota(jnp.int32, (RANK, RANK), 1)
    inverse = jnp.where(i > j, lower, jnp.where(i == j, 1.0, 0.0)) * lax.rsqrt(pivots)
    basis_ref[...] = exact_dot(left, inverse, ((1,), (1,)))


def sum_kernel(part_ref, out_ref):
    total = part_ref[0]
    for i in range(1, part_ref.shape[0]):
        total = total + part_ref[i]
    for i in range(out_ref.shape[0]):
        out_ref[i] = total


def sum_spread(parts, count):
    return pl.pallas_call(
        sum_kernel,
        in_specs=[vmem],
        out_specs=vmem,
        out_shape=pltpu.VMEM((count,) + parts.shape[1:], f32),
        compiler_params=params(4),
        name="sum_spread",
    )(parts)


def halve_kernel(after_ref, *refs):
    del after_ref
    for side in range(2):
        kept_ref, got_ref = refs[2 * side : 2 * side + 2]
        keep_ref, send_ref = refs[4 + 2 * side : 6 + 2 * side]
        count = keep_ref.shape[0]
        for i in range(count):
            keep_ref[i] = kept_ref[i] + got_ref[i]
            send_ref[i] = kept_ref[count + i] + got_ref[count + i]


def halve(after, *blocks):
    shape = (blocks[0].shape[0] // 2,) + blocks[0].shape[1:]
    return pl.pallas_call(
        halve_kernel,
        in_specs=[hbm] + [vmem] * 4,
        out_specs=[vmem] * 4,
        out_shape=[pltpu.VMEM(shape, f32)] * 4,
        compiler_params=params(4),
        name="halve",
    )(after, *blocks)


def join_kernel(after_ref, upper_ref, upper_got_ref, lower_ref, lower_got_ref, out_ref):
    del after_ref
    half = upper_ref.shape[1]
    for i in range(out_ref.shape[0]):
        out_ref[i, :half, :] = upper_ref[i] + upper_got_ref[i]
        out_ref[i, half:, :] = lower_ref[i] + lower_got_ref[i]


def finish_kernel(part_ref, basis_ref, out_ref):
    total = part_ref[0]
    for i in range(1, part_ref.shape[0]):
        total = total + part_ref[i]
    right = exact_dot(total * (1.0 / 32), basis_ref[...], ((0,), (0,)))
    for i in range(out_ref.shape[0]):
        out_ref[i] = right


def update_kernel(slot, basis_ref, right_ref, sum_ref, *rest):
    out_hbm, right_hbm, basis_hbm, out_ref, sems = rest[3 * slot :]
    columns = sum_ref.shape[1]
    steps = columns // CHUNK
    m = lax.axis_index("core") ^ slot
    stores = [
        pltpu.make_async_copy(right_ref.at[:columns], right_hbm.at[m], sems.at[steps]),
        pltpu.make_async_copy(basis_ref, basis_hbm.at[m], sems.at[steps + 1]),
    ]
    for copy in stores:
        copy.start()
    high, low = split(basis_ref[...])
    wide = jnp.concatenate([high, low], axis=1)
    for j in range(steps):
        r_high, r_low = split(right_ref[cols(j), :])
        rebuilt = dot(wide, jnp.concatenate([r_high, r_high], axis=1), ((1,), (1,)))
        rebuilt = rebuilt + dot(high, r_low, ((1,), (1,)))
        out_ref[:, cols(j)] = sum_ref[:, cols(j)] - rebuilt
        copy = pltpu.make_async_copy(out_ref.at[:, cols(j)], out_hbm.at[m, :, cols(j)], sems.at[j])
        copy.start()
        stores.append(copy)
    for copy in stores:
        copy.wait()


def update(slot, basis, right, summed, previous=()):
    rows, columns = summed.shape
    return pl.pallas_call(
        functools.partial(update_kernel, slot),
        in_specs=[vmem] * 3 + [hbm] * len(previous),
        out_specs=[hbm] * 3,
        out_shape=[
            jax.ShapeDtypeStruct((2, rows, columns), f32),
            jax.ShapeDtypeStruct((2, columns, RANK), f32),
            jax.ShapeDtypeStruct((2, rows, RANK), f32),
        ],
        scratch_shapes=[
            pltpu.VMEM((rows, columns), f32),
            pltpu.SemaphoreType.DMA((2 + columns // CHUNK,)),
        ],
        input_output_aliases={3: 0, 4: 1, 5: 2} if previous else {},
        cost_estimate=pl.CostEstimate(
            flops=6 * rows * columns * RANK, bytes_accessed=8 * rows * columns, transcendentals=0
        ),
        compiler_params=params(8),
        name=("update_mine", "update_other")[slot],
    )(basis, right, summed, *previous)


def swap(x, axis="core"):
    return lax.ppermute(x, axis, [(0, 1), (1, 0)])


def exchange(x, axes=PLANE):
    return lax.all_to_all(x, axes, 0, 0)


def on_device(gradients, feedback, seed_value):
    gradients = pltpu.with_memory_space_constraint(gradients[0], pltpu.HBM)
    feedback = pltpu.with_memory_space_constraint(feedback[0], pltpu.HBM)
    mats, rows, columns = gradients.shape
    depth = lax.axis_size("z")
    share = -(-rows // (CHIPS * TILE)) * TILE
    padded = CHIPS * share

    mine, other, upper, upper_other, lower, lower_other, summed, summed_other = pl.pallas_call(
        left_kernel,
        in_specs=[smem, hbm, hbm],
        out_specs=[vmem] * 6 + [hbm] * 2,
        out_shape=[pltpu.VMEM((padded, RANK), f32)] * 2
        + [pltpu.VMEM((CHIPS, rows // 2, LANES), f32)] * 4
        + [pltpu.HBM((rows, columns), f32)] * 2,
        scratch_shapes=[
            pltpu.VMEM((mats, rows, columns), bf16),
            pltpu.VMEM((mats, rows, columns), f32),
            pltpu.VMEM((columns, 2 * RANK), bf16),
            pltpu.SemaphoreType.DMA((columns // CHUNK, 4)),
        ],
        compiler_params=params(20),
        name="left_part",
    )(seed_value, gradients, feedback)

    left = mine + swap(other)
    left, upper_other, lower_other = lax.optimization_barrier((left, upper_other, lower_other))
    upper_got, lower_got = swap(upper_other), swap(lower_other)
    left = exchange(left.reshape(CHIPS, share, RANK))
    upper, upper_send, lower, lower_send = halve(left, upper, upper_got, lower, lower_got)
    upper_got, lower_got = swap(upper_send, "xl"), swap(lower_send, "yl")
    left = exchange(sum_spread(left, depth), "z")
    upper, upper_send, lower, lower_send = halve(left, upper, upper_got, lower, lower_got)
    upper_got, lower_got = swap(upper_send, "yl"), swap(lower_send, "xl")
    left = exchange(sum_spread(left, CHIPS))

    quarter = pl.pallas_call(
        join_kernel,
        in_specs=[hbm] + [vmem] * 4,
        out_specs=vmem,
        out_shape=pltpu.VMEM((CHIPS // 4, rows, LANES), f32),
        compiler_params=params(4),
        name="join",
    )(left, upper, upper_got, lower, lower_got)
    basis = pl.pallas_call(
        basis_kernel,
        in_specs=[vmem, hbm],
        out_specs=vmem,
        out_shape=pltpu.VMEM((rows, RANK), f32),
        cost_estimate=pl.CostEstimate(flops=5_000_000_000, bytes_accessed=400_000, transcendentals=0),
        compiler_params=params(8),
        name="basis",
    )(left.reshape(padded, RANK), quarter)
    basis_other = swap(basis)
    right = pl.pallas_call(
        finish_kernel,
        in_specs=[vmem, vmem],
        out_specs=vmem,
        out_shape=pltpu.VMEM((CHIPS, LANES, RANK), f32),
        compiler_params=params(4),
        name="finish",
    )(exchange(quarter, ("xh", "yh")), basis)
    right = exchange(right).reshape(CHIPS * LANES, RANK)
    right_other = swap(right)

    outs = update(0, basis, right, summed)
    new_feedback, right_factor, left_basis = update(1, basis_other, right_other, summed_other, outs)
    return new_feedback[None], left_basis, right_factor


def solution(mesh):
    fine = Mesh(mesh.devices.reshape(2, 2, 2, 2, 2, -1), PLANE + ("core", "z"))
    dp = PLANE + ("core",)
    placed = (P(dp, None, None, "z"), P(dp, None, None, "z"), P())
    return jax.shard_map(
        on_device,
        mesh=fine,
        in_specs=placed,
        out_specs=(P(dp, None, None, "z"), P(), P(None, "z", None)),
        check_vma=False,
    )
```

time: 116 us -> 94.4 us (0.81)
  waiting for transfers between devices: 15 us -> 4.96 us
  local copies, waits for them, and re-layouts: 7.27 us -> 0.01 us
  other arithmetic: 3.34 us -> 0.02 us
  starting transfers between devices: 15.5 us -> 17.9 us
  Pallas kernels: 18 us -> 15.9 us
  blocking collectives: 55 us -> 53.8 us
    unnamed x12 -> x4, local copies, waits for them, and re-layouts: 6.08 us -> 0.01 us
    all_to_all x1, waiting for transfers between devices: 8.69 us -> 3.18 us  [exchange(): return lax.all_to_all(x, axes, 0, 0)]
    ppermute x5 -> x9, waiting for transfers between devices: 6.36 us -> 1.78 us  [swap(): return lax.ppermute(x, axis, [(0, 1), (1, 0)])]
    ppermute x5 -> x9, starting transfers between devices: 11.7 us -> 14.2 us  [swap(): return lax.ppermute(x, axis, [(0, 1), (1, 0)])]
    pallas_call x5 -> x9, Pallas kernels: 17.7 us -> 15.5 us  [the longest x1 5.61 us: on_device(): pl.pallas_call(left_kernel, in_specs=[smem, hbm, hbm], out_specs=[vmem] *...]
    add x2 -> x1, other arithmetic: 1.95 us -> 0.02 us  [on_device(): left = mine + swap(other)]
    another operation x3 -> x0, other arithmetic: 1.36 us -> none  [the longest x2 0.77 us: on_device(): left_basis = jnp.stack([mine_first, mine_last])]
    all_to_all x4, blocking collectives: 55 us -> 53.8 us  [exchange(): return lax.all_to_all(x, axes, 0, 0)]
  transfers between devices with their start and end apart: 6 -> 10, of which waited for: 5 -> 3; matrix products, arithmetic and copies ran while one was open for 1% -> 0% of each run, Pallas kernels for 6% -> 7%
where the time goes in v5:
time: 94.4 us; the launch traced here: 94.1 us
  blocking collectives  53.8 us (57%)
  starting transfers between devices  17.9 us (19%)
  Pallas kernels  15.9 us (17%)
  waiting for transfers between devices  4.96 us (5%)
  between operations  1.52 us (2%)
    all_to_all x4, blocking collectives, exchange(): return lax.all_to_all(x, axes, 0, 0)  53.8 us
    ppermute x9, starting transfers between devices, swap(): return lax.ppermute(x, axis, [(0, 1), (1, 0)])  14.2 us
    pallas_call x1, Pallas kernels, on_device(): pl.pallas_call(left_kernel, in_specs=[smem, hbm, hbm], out_specs=[vmem] *...  5.61 us
    pallas_call x1, Pallas kernels, on_device(): pl.pallas_call(basis_kernel, in_specs=[vmem, hbm], out_specs=vmem, out_sh...  4.87 us
    all_to_all x1, starting transfers between devices, exchange(): return lax.all_to_all(x, axes, 0, 0)  3.66 us
    pallas_call x2, Pallas kernels, update(): pl.pallas_call(functools.partial(update_kernel, slot), in_specs=[vmem] *...  3.63 us
    all_to_all x1, waiting for transfers between devices, exchange(): return lax.all_to_all(x, axes, 0, 0)  3.18 us
  transfers between devices with their start and end apart: 10, of which 3 were waited for; matrix products, arithmetic and copies ran while one was open for 0% of the time, Pallas kernels for 7%

profile of v5, /device:TPU:1, one launch (start us, length us, event | category | flops | bytes accessed | tf_op | source)
XLA Modules:
  0.0 94.1 jit_solution(5543406855553771860)
XLA Ops:
  1.3 5.6 %left_part.1 = (f32[384,128]{1,0:T(8,128)S(1)}, f32[384,128]{1,0:T(8,128)S(1)}, f32[16,160,128]{2,1,0:T(8,128)S(1)}, f32[16,160,128]{2,1,0:T(8,128)S(1)}, f32[16...) custom-call(s32[1]{0:T(128)S(6)} %copy.12.seed_ref, ...), custom_call_target="tpu_custom_call" | custom-call | tf_op jit(solution)/shard_map/left_part/pallas_call | solution.py:308
  6.9 3.3 %collective-permute-start = (f32[384,128]{1,0:T(8,128)S(1)}, f32[384,128]{1,0:T(8,128)S(1)}, u32[]{:S(2)}, u32[]{:S(2)}) collective-permute-start(f32[384,128]{1,0:T(8,128)S(1)} %get-tuple-element.29), channel_id=1, source_target_pairs={{0,8},{8,0},{1,9},{9,1},{2,10},{10,2},{3,11},{11,3},{4,12},{12,4},... | collective-permute-start | bytes 589832 | tf_op jit(solution)/shard_map/ppermute | solution.py:293
  10.2 1.1 %collective-permute-done = f32[384,128]{1,0:T(8,128)S(1)} collective-permute-done((f32[384,128]{1,0:T(8,128)S(1)}, f32[384,128]{1,0:T(8,128)S(1)}, u32[]{:S(2)}, u32[]{:S(2)}) %collective-permute-start) | collective-permute-done | bytes 196640 | tf_op jit(solution)/shard_map/ppermute | solution.py:293
  11.3 0.5 collective-permute-start.1
  11.8 0.1 collective-permute-start.2
  11.9 11.9 %all_to_all.25.part_ref.after_ref = f32[16,24,128]{2,1,0:T(8,128)S(1)} all-to-all(f32[16,24,128]{2,1,0:T(8,128)S(1)} %bitcast.12), channel_id=1, replica_groups=mesh['xh'=2,'xl'=2,'yh'=2,'yl'=2,'core'=2,'z'=8] {'xh','xl','yh','yl'}, dimensions={0} | all-to-all | bytes 393216 | tf_op jit(solution)/shard_map/all_to_all | solution.py:297
  23.8 0.0 collective-permute-done.1.refs_1_
  23.8 0.0 collective-permute-done.2.refs_3_
  23.8 0.3 halve.2
  24.1 0.2 collective-permute-start.3
  24.3 0.1 collective-permute-start.4
  24.4 15.6 %all_to_all.26.part_ref.after_ref = f32[8,24,128]{2,1,0:T(8,128)S(1)} all-to-all(f32[8,24,128]{2,1,0:T(8,128)S(1)} %sum_spread.2), channel_id=1, replica_groups=mesh['xh'=2,'xl'=2,'yh'=2,'yl'=2,'core'=2,'z'=8] {'z'}, dimensions={0} | all-to-all | bytes 196608 | tf_op jit(solution)/shard_map/all_to_all | solution.py:297
  39.9 0.0 collective-permute-done.3.refs_1_
  39.9 0.0 collective-permute-done.4.refs_3_
  39.9 0.1 halve.3
  40.1 1.5 %collective-permute-start.5 = (f32[4,160,128]{2,1,0:T(8,128)S(1)}, f32[4,160,128]{2,1,0:T(8,128)S(1)}, u32[]{:S(2)}, u32[]{:S(2)}) collective-permute-start(f32[4,160,128]{2,1,0:T(8,128)S(1)} %get-tuple-element.42), channel_id=1, source_target_pairs={{0,16},{16,0},{1,17},{17,1},{2,18},{18,2},{3,19},{19,3},{4,20},{20... | collective-permute-start | bytes 983048 | tf_op jit(solution)/shard_map/ppermute | solution.py:293
  41.6 1.3 %collective-permute-start.6 = (f32[4,160,128]{2,1,0:T(8,128)S(1)}, f32[4,160,128]{2,1,0:T(8,128)S(1)}, u32[]{:S(2)}, u32[]{:S(2)}) collective-permute-start(f32[4,160,128]{2,1,0:T(8,128)S(1)} %get-tuple-element.44), channel_id=1, source_target_pairs={{0,64},{64,0},{1,65},{65,1},{2,66},{66,2},{3,67},{67,3},{4,68},{68... | collective-permute-start | bytes 983048 | tf_op jit(solution)/shard_map/ppermute | solution.py:293
  42.9 11.1 %all_to_all.27.after_ref = f32[16,24,128]{2,1,0:T(8,128)S(1)} all-to-all(f32[16,24,128]{2,1,0:T(8,128)S(1)} %sum_spread.3), channel_id=1, replica_groups=mesh['xh'=2,'xl'=2,'yh'=2,'yl'=2,'core'=2,'z'=8] {'xh','xl','yh','yl'}, dimensions={0} | all-to-all | bytes 393216 | tf_op jit(solution)/shard_map/all_to_all | solution.py:297
  54.1 0.0 collective-permute-done.5.upper_got_ref
  54.1 0.0 collective-permute-done.6.lower_got_ref
  54.1 0.9 join.1.after_ref
  55.0 3.7 %all-to-all-start.3 = ((f32[4,320,128]{2,1,0:T(8,128)}), f32[4,320,128]{2,1,0:T(8,128)S(1)}, u32[]{:S(2)}, u32[]{:S(2)}) async-start(f32[4,320,128]{2,1,0:T(8,128)} %join.1.after_ref), calls=%async_computation.3 | async-start | bytes 1310720 | tf_op jit(solution)/shard_map/all_to_all | solution.py:297
  58.7 4.9 %basis.1.basis_ref = f32[320,128]{1,0:T(8,128)S(1)} custom-call(f32[384,128]{1,0:T(8,128)S(1)} %bitcast.8, f32[4,320,128]{2,1,0:T(8,128)} %join.1.after_ref), custom_call_target="tpu_custom_call" | custom-call | flops 5000000000 | bytes 400000 | tf_op jit(solution)/shard_map/basis/pallas_call | solution.py:344
  63.5 0.0 copy-start.1
  63.5 3.2 %all-to-all-done.3.part_ref = f32[4,320,128]{2,1,0:T(8,128)S(1)} async-done(((f32[4,320,128]{2,1,0:T(8,128)}), f32[4,320,128]{2,1,0:T(8,128)S(1)}, u32[]{:S(2)}, u32[]{:S(2)}) %all-to-all-start.3) | async-done | bytes 655392 | tf_op jit(solution)/shard_map/all_to_all | solution.py:297
  66.7 0.4 finish.1
  67.2 15.2 %all_to_all.28 = f32[16,128,128]{2,1,0:T(8,128)S(1)} all-to-all(f32[16,128,128]{2,1,0:T(8,128)S(1)} %finish.1), channel_id=1, replica_groups=mesh['xh'=2,'xl'=2,'yh'=2,'yl'=2,'core'=2,'z'=8] {'xh','xl','yh','yl'}, dimensions={0} | all-to-all | bytes 2097152 | tf_op jit(solution)/shard_map/all_to_all | solution.py:297
  82.4 0.0 copy-start
  82.4 7.2 %collective-permute-start.8 = (f32[2048,128]{1,0:T(8,128)S(1)}, f32[2048,128]{1,0:T(8,128)S(1)}, u32[]{:S(2)}, u32[]{:S(2)}) collective-permute-start(f32[2048,128]{1,0:T(8,128)S(1)} %bitcast.6), channel_id=1, source_target_pairs={{0,8},{8,0},{1,9},{9,1},{2,10},{10,2},{3,11},{11,3},{4,12},{12,4},... | collective-permute-start | bytes 3145736 | tf_op jit(solution)/shard_map/ppermute | solution.py:293
  89.6 0.0 collective-permute-start.7
  89.6 0.0 copy-done.1
  89.6 1.8 %update_mine.1 = (f32[2,320,1792]{2,1,0:T(8,128)}, f32[2,1792,128]{2,1,0:T(8,128)}, f32[2,320,128]{2,1,0:T(8,128)}) custom-call(f32[320,128]{1,0:T(8,128)S(1)} %basis.1.basis_ref, f32[2048,128]{1,0:T(8,128)S(1)} %bitcast.7, f32[320,1792]{1,0:T(8,128)S(1)} %copy-done.1), custom_call_target="tpu_custom_call" | custom-call | flops 440401920 | bytes 4587520 | tf_op jit(solution)/shard_map/update_mine/pallas_call | solution.py:270
  91.4 0.7 collective-permute-done.7.basis_ref
  92.1 0.0 collective-permute-done.8.right_ref
  92.1 0.0 copy-done
  92.1 1.8 %update_other.1 = (f32[2,320,1792]{2,1,0:T(8,128)}, f32[2,1792,128]{2,1,0:T(8,128)}, f32[2,320,128]{2,1,0:T(8,128)}) custom-call(f32[320,128]{1,0:T(8,128)S(1)} %collective-permute-done.7.basis_ref, f32[2048,128]{1,0:T(8,128)S(1)} %collective-permute-done.8.right_ref, ...), custom_call_target="tpu_custom_call", output_to_operand_aliasing={{0}: (3, {}), {1}: (4, {}), {2}: (5, {})} | custom-call | flops 440401920 | bytes 4587520 | tf_op jit(solution)/shard_map/update_other/pallas_call | solution.py:270
  (3 shorter events, 0.1 us)
Async XLA Ops:
  6.9 4.4 %collective-permute-start = (f32[384,128]{1,0:T(8,128)S(1)}, f32[384,128]{1,0:T(8,128)S(1)}, u32[]{:S(2)}, u32[]{:S(2)}) collective-permute-start(f32[384,128]{1,0:T(8,128)S(1)} %get-tuple-element.29), channel_id=1, source_target_pairs={{0,8},{8,0},{1,9},{9,1},{2,10},{10,2},{3,11},{11,3},{4,12},{12,4},... | collective-permute-start | bytes 589832 | tf_op jit(solution)/shard_map/ppermute | solution.py:293
  11.3 12.5 %collective-permute-start.1 = (f32[16,160,128]{2,1,0:T(8,128)S(1)}, f32[16,160,128]{2,1,0:T(8,128)S(1)}, u32[]{:S(2)}, u32[]{:S(2)}) collective-permute-start(f32[16,160,128]{2,1,0:T(8,128)S(1)} %get-tuple-element.34), channel_id=1, source_target_pairs={{0,8},{8,0},{1,9},{9,1},{2,10},{10,2},{3,11},{11,3},{4,12},{12,4},... | collective-permute-start | bytes 3932168 | tf_op jit(solution)/shard_map/ppermute | solution.py:293
  11.8 12.0 %collective-permute-start.2 = (f32[16,160,128]{2,1,0:T(8,128)S(1)}, f32[16,160,128]{2,1,0:T(8,128)S(1)}, u32[]{:S(2)}, u32[]{:S(2)}) collective-permute-start(f32[16,160,128]{2,1,0:T(8,128)S(1)} %get-tuple-element.36), channel_id=1, source_target_pairs={{0,8},{8,0},{1,9},{9,1},{2,10},{10,2},{3,11},{11,3},{4,12},{12,4},... | collective-permute-start | bytes 3932168 | tf_op jit(solution)/shard_map/ppermute | solution.py:293
  24.1 15.9 %collective-permute-start.3 = (f32[8,160,128]{2,1,0:T(8,128)S(1)}, f32[8,160,128]{2,1,0:T(8,128)S(1)}, u32[]{:S(2)}, u32[]{:S(2)}) collective-permute-start(f32[8,160,128]{2,1,0:T(8,128)S(1)} %get-tuple-element.38), channel_id=1, source_target_pairs={{0,64},{64,0},{1,65},{65,1},{2,66},{66,2},{3,67},{67,3},{4,68},{68... | collective-permute-start | bytes 1966088 | tf_op jit(solution)/shard_map/ppermute | solution.py:293
  24.3 15.7 %collective-permute-start.4 = (f32[8,160,128]{2,1,0:T(8,128)S(1)}, f32[8,160,128]{2,1,0:T(8,128)S(1)}, u32[]{:S(2)}, u32[]{:S(2)}) collective-permute-start(f32[8,160,128]{2,1,0:T(8,128)S(1)} %get-tuple-element.40), channel_id=1, source_target_pairs={{0,16},{16,0},{1,17},{17,1},{2,18},{18,2},{3,19},{19,3},{4,20},{20... | collective-permute-start | bytes 1966088 | tf_op jit(solution)/shard_map/ppermute | solution.py:293
  40.1 14.0 %collective-permute-start.5 = (f32[4,160,128]{2,1,0:T(8,128)S(1)}, f32[4,160,128]{2,1,0:T(8,128)S(1)}, u32[]{:S(2)}, u32[]{:S(2)}) collective-permute-start(f32[4,160,128]{2,1,0:T(8,128)S(1)} %get-tuple-element.42), channel_id=1, source_target_pairs={{0,16},{16,0},{1,17},{17,1},{2,18},{18,2},{3,19},{19,3},{4,20},{20... | collective-permute-start | bytes 983048 | tf_op jit(solution)/shard_map/ppermute | solution.py:293
  41.6 12.5 %collective-permute-start.6 = (f32[4,160,128]{2,1,0:T(8,128)S(1)}, f32[4,160,128]{2,1,0:T(8,128)S(1)}, u32[]{:S(2)}, u32[]{:S(2)}) collective-permute-start(f32[4,160,128]{2,1,0:T(8,128)S(1)} %get-tuple-element.44), channel_id=1, source_target_pairs={{0,64},{64,0},{1,65},{65,1},{2,66},{66,2},{3,67},{67,3},{4,68},{68... | collective-permute-start | bytes 983048 | tf_op jit(solution)/shard_map/ppermute | solution.py:293
  55.0 11.7 %all-to-all-start.3 = ((f32[4,320,128]{2,1,0:T(8,128)}), f32[4,320,128]{2,1,0:T(8,128)S(1)}, u32[]{:S(2)}, u32[]{:S(2)}) async-start(f32[4,320,128]{2,1,0:T(8,128)} %join.1.after_ref), calls=%async_computation.3 | async-start | bytes 1310720 | tf_op jit(solution)/shard_map/all_to_all | solution.py:297
  63.5 26.0 %copy-start.1 = (f32[320,1792]{1,0:T(8,128)S(1)}, f32[320,1792]{1,0:T(8,128)}, u32[]{:S(2)}) copy-start(f32[320,1792]{1,0:T(8,128)} %get-tuple-element.46.sum_ref) | copy-start | bytes 6881284
  82.4 9.7 %copy-start = (f32[320,1792]{1,0:T(8,128)S(1)}, f32[320,1792]{1,0:T(8,128)}, u32[]{:S(2)}) copy-start(f32[320,1792]{1,0:T(8,128)} %get-tuple-element.45.sum_ref) | copy-start | bytes 6881284
  82.4 9.7 %collective-permute-start.8 = (f32[2048,128]{1,0:T(8,128)S(1)}, f32[2048,128]{1,0:T(8,128)S(1)}, u32[]{:S(2)}, u32[]{:S(2)}) collective-permute-start(f32[2048,128]{1,0:T(8,128)S(1)} %bitcast.6), channel_id=1, source_target_pairs={{0,8},{8,0},{1,9},{9,1},{2,10},{10,2},{3,11},{11,3},{4,12},{12,4},... | collective-permute-start | bytes 3145736 | tf_op jit(solution)/shard_map/ppermute | solution.py:293
  89.6 2.5 %collective-permute-start.7 = (f32[320,128]{1,0:T(8,128)S(1)}, f32[320,128]{1,0:T(8,128)S(1)}, u32[]{:S(2)}, u32[]{:S(2)}) collective-permute-start(f32[320,128]{1,0:T(8,128)S(1)} %basis.1.basis_ref), channel_id=1, source_target_pairs={{0,8},{8,0},{1,9},{9,1},{2,10},{10,2},{3,11},{11,3},{4,12},{12,4},... | collective-permute-start | bytes 491528 | tf_op jit(solution)/shard_map/ppermute | solution.py:293

commit v6 on v5

--- a/solution.py
+++ b/solution.py
@@ -67,8 +67,8 @@
 
 def places(tile):
     xh, xl, yh, yl = tile >> 3, (tile >> 2) & 1, (tile >> 1) & 1, tile & 1
-    rest = 2 * xh + yh
-    far_x, far_y = xl ^ lax.axis_index("xl"), yl ^ lax.axis_index("yl")
+    rest = 2 * xl + yl
+    far_x, far_y = xh ^ lax.axis_index("xh"), yh ^ lax.axis_index("yh")
     return 8 * far_x + 4 * far_y + rest, 8 * far_y + 4 * far_x + rest
 
 
@@ -77,6 +77,7 @@
     grad_ref, feed_ref, start_ref, sems = refs[8:]
     _, rows, columns = grad_ref.shape
     half = rows // 2
+    width = columns // CHIPS
     steps = columns // CHUNK
     seed = seed_ref[0]
     first = lax.axis_index("z") * columns
@@ -92,11 +93,6 @@
         copies.append(pair)
     for left_ref in lefts:
         left_ref[rows:, :] = jnp.zeros((left_ref.shape[0] - rows, RANK), f32)
-    for tile in range(columns // LANES, CHIPS):
-        upper, lower = places(tile)
-        for slot in range(2):
-            uppers[slot][upper] = jnp.zeros((half, LANES), f32)
-            lowers[slot][lower] = jnp.zeros((half, LANES), f32)
     for j in range(steps):
         high, low = split(start_block(seed, first + j * CHUNK, CHUNK))
         start_ref[cols(j), :RANK] = high
@@ -109,15 +105,24 @@
         for slot in range(2):
             m = core ^ slot
             summed = grad_ref[m, :, cols(j)].astype(f32) + feed_ref[m, :, cols(j)]
-            feed_ref[m, :, cols(j)] = summed
-            save = pltpu.make_async_copy(feed_ref.at[m, :, cols(j)], sums[slot].at[:, cols(j)], sems.at[j, 2 + slot])
-            save.start()
-            saves.append(save)
-            for part in range(CHUNK // LANES):
-                upper, lower = places(j * (CHUNK // LANES) + part)
-                span = slice(part * LANES, (part + 1) * LANES)
-                uppers[slot][upper] = summed[:half, span]
-                lowers[slot][lower] = summed[half:, span]
+            if slot:
+                sums[slot][:, cols(j)] = summed
+            else:
+                feed_ref[m, :, cols(j)] = summed
+                save = pltpu.make_async_copy(feed_ref.at[m, :, cols(j)], sums[slot].at[:, cols(j)], sems.at[j, 2])
+                save.start()
+                saves.append(save)
+            for tile in range(CHIPS):
+                begin = tile * width
+                end = min(begin + LANES, columns)
+                if (end - 1) // CHUNK != j:
+                    continue
+                block = sums[slot][:, begin:end] if slot else feed_ref[m, :, begin:end]
+                if end - begin < LANES:
+                    block = jnp.concatenate([block, jnp.zeros((rows, LANES - end + begin), f32)], axis=1)
+                upper, lower = places(tile)
+                uppers[slot][upper] = block[:half]
+                lowers[slot][lower] = block[half:]
             s_high, s_low = split(summed)
             wide = dot(s_high, both)
             piece = wide[:, :RANK] + wide[:, RANK:] + dot(s_low, both[:, :RANK])
@@ -237,7 +242,7 @@
         total = total + part_ref[i]
     right = exact_dot(total * (1.0 / 32), basis_ref[...], ((0,), (0,)))
     for i in range(out_ref.shape[0]):
-        out_ref[i] = right
+        out_ref[i] = right[: out_ref.shape[1], :]
 
 
 def update_kernel(slot, basis_ref, right_ref, sum_ref, *rest):
@@ -246,7 +251,7 @@
     steps = columns // CHUNK
     m = lax.axis_index("core") ^ slot
     stores = [
-        pltpu.make_async_copy(right_ref.at[:columns], right_hbm.at[m], sems.at[steps]),
+        pltpu.make_async_copy(right_ref, right_hbm.at[m], sems.at[steps]),
         pltpu.make_async_copy(basis_ref, basis_hbm.at[m], sems.at[steps + 1]),
     ]
     for copy in stores:
@@ -289,8 +294,12 @@
     )(basis, right, summed, *previous)
 
 
-def swap(x, axis="core"):
-    return lax.ppermute(x, axis, [(0, 1), (1, 0)])
+def swap(x):
+    return lax.ppermute(x, "core", [(0, 1), (1, 0)])
+
+
+def cross(x, axis):
+    return lax.ppermute(x, (axis + "h", axis + "l"), [(i, 3 - i) for i in range(4)])
 
 
 def exchange(x, axes=PLANE):
@@ -308,10 +317,10 @@
     mine, other, upper, upper_other, lower, lower_other, summed, summed_other = pl.pallas_call(
         left_kernel,
         in_specs=[smem, hbm, hbm],
-        out_specs=[vmem] * 6 + [hbm] * 2,
+        out_specs=[vmem] * 6 + [hbm, vmem],
         out_shape=[pltpu.VMEM((padded, RANK), f32)] * 2
         + [pltpu.VMEM((CHIPS, rows // 2, LANES), f32)] * 4
-        + [pltpu.HBM((rows, columns), f32)] * 2,
+        + [pltpu.HBM((rows, columns), f32), pltpu.VMEM((rows, columns), f32)],
         scratch_shapes=[
             pltpu.VMEM((mats, rows, columns), bf16),
             pltpu.VMEM((mats, rows, columns), f32),
@@ -327,10 +336,10 @@
     upper_got, lower_got = swap(upper_other), swap(lower_other)
     left = exchange(left.reshape(CHIPS, share, RANK))
     upper, upper_send, lower, lower_send = halve(left, upper, upper_got, lower, lower_got)
-    upper_got, lower_got = swap(upper_send, "xl"), swap(lower_send, "yl")
+    upper_got, lower_got = cross(upper_send, "x"), cross(lower_send, "y")
     left = exchange(sum_spread(left, depth), "z")
     upper, upper_send, lower, lower_send = halve(left, upper, upper_got, lower, lower_got)
-    upper_got, lower_got = swap(upper_send, "yl"), swap(lower_send, "xl")
+    upper_got, lower_got = cross(upper_send, "y"), cross(lower_send, "x")
     left = exchange(sum_spread(left, CHIPS))
 
     quarter = pl.pallas_call(
@@ -355,11 +364,11 @@
         finish_kernel,
         in_specs=[vmem, vmem],
         out_specs=vmem,
-        out_shape=pltpu.VMEM((CHIPS, LANES, RANK), f32),
+        out_shape=pltpu.VMEM((CHIPS, columns // CHIPS, RANK), f32),
         compiler_params=params(4),
         name="finish",
-    )(exchange(quarter, ("xh", "yh")), basis)
-    right = exchange(right).reshape(CHIPS * LANES, RANK)
+    )(exchange(quarter, ("xl", "yl")), basis)
+    right = exchange(right).reshape(columns, RANK)
     right_other = swap(right)
 
     outs = update(0, basis, right, summed)

time: 94.4 us -> 92.3 us (0.978)
  starting transfers between devices: 17.9 us -> 21 us
  blocking collectives: 53.8 us -> 51.4 us
  waiting for transfers between devices: 4.96 us -> 2.68 us
    ppermute x9, starting transfers between devices: 14.2 us -> 17.4 us  [the longest x5 11.8 us: swap(): return lax.ppermute(x, 'core', [(0, 1), (1, 0)])]
    all_to_all x4, blocking collectives: 53.8 us -> 51.4 us  [exchange(): return lax.all_to_all(x, axes, 0, 0)]
    all_to_all x1, waiting for transfers between devices: 3.18 us -> 1.08 us  [exchange(): return lax.all_to_all(x, axes, 0, 0)]
where the time goes in v6:
time: 92.3 us; the launch traced here: 92 us
  blocking collectives  51.4 us (56%)
  starting transfers between devices  21 us (23%)
  Pallas kernels  15.4 us (17%)
  waiting for transfers between devices  2.68 us (3%)
  between operations  1.51 us (2%)
    all_to_all x4, blocking collectives, exchange(): return lax.all_to_all(x, axes, 0, 0)  51.4 us
    ppermute x5, starting transfers between devices, swap(): return lax.ppermute(x, 'core', [(0, 1), (1, 0)])  11.8 us
    ppermute x4, starting transfers between devices, cross(): lax.ppermute(x, (axis + 'h', axis + 'l'), [(i, 3 - i) for i in range(4)])  5.53 us
    pallas_call x1, Pallas kernels, on_device(): pl.pallas_call(left_kernel, in_specs=[smem, hbm, hbm], out_specs=[vmem] *...  5.15 us
    pallas_call x1, Pallas kernels, on_device(): pl.pallas_call(basis_kernel, in_specs=[vmem, hbm], out_specs=vmem, out_sh...  4.87 us
    all_to_all x1, starting transfers between devices, exchange(): return lax.all_to_all(x, axes, 0, 0)  3.66 us
    pallas_call x2, Pallas kernels, update(): pl.pallas_call(functools.partial(update_kernel, slot), in_specs=[vmem] *...  3.63 us
  transfers between devices with their start and end apart: 10, of which 3 were waited for; matrix products, arithmetic and copies ran while one was open for 0% of the time, Pallas kernels for 7%

profile of v6, /device:TPU:1, one launch (start us, length us, event | category | flops | bytes accessed | tf_op | source)
XLA Modules:
  0.0 92.0 jit_solution(3589321941421920884)
XLA Ops:
  1.3 5.2 %left_part.1 = (f32[384,128]{1,0:T(8,128)S(1)}, f32[384,128]{1,0:T(8,128)S(1)}, f32[16,160,128]{2,1,0:T(8,128)S(1)}, f32[16,160,128]{2,1,0:T(8,128)S(1)}, f32[16...) custom-call(s32[1]{0:T(128)S(6)} %copy.12.seed_ref, ...), custom_call_target="tpu_custom_call" | custom-call | tf_op jit(solution)/shard_map/left_part/pallas_call | solution.py:317
  6.4 3.3 %collective-permute-start = (f32[384,128]{1,0:T(8,128)S(1)}, f32[384,128]{1,0:T(8,128)S(1)}, u32[]{:S(2)}, u32[]{:S(2)}) collective-permute-start(f32[384,128]{1,0:T(8,128)S(1)} %get-tuple-element.29), channel_id=1, source_target_pairs={{0,8},{8,0},{1,9},{9,1},{2,10},{10,2},{3,11},{11,3},{4,12},{12,4},... | collective-permute-start | bytes 589832 | tf_op jit(solution)/shard_map/ppermute | solution.py:298
  9.8 1.1 %collective-permute-done = f32[384,128]{1,0:T(8,128)S(1)} collective-permute-done((f32[384,128]{1,0:T(8,128)S(1)}, f32[384,128]{1,0:T(8,128)S(1)}, u32[]{:S(2)}, u32[]{:S(2)}) %collective-permute-start) | collective-permute-done | bytes 196640 | tf_op jit(solution)/shard_map/ppermute | solution.py:298
  10.9 0.5 collective-permute-start.1
  11.3 0.1 collective-permute-start.2
  11.5 11.9 %all_to_all.25.part_ref.after_ref = f32[16,24,128]{2,1,0:T(8,128)S(1)} all-to-all(f32[16,24,128]{2,1,0:T(8,128)S(1)} %bitcast.12), channel_id=1, replica_groups=mesh['xh'=2,'xl'=2,'yh'=2,'yl'=2,'core'=2,'z'=8] {'xh','xl','yh','yl'}, dimensions={0} | all-to-all | bytes 393216 | tf_op jit(solution)/shard_map/all_to_all | solution.py:306
  23.3 0.0 collective-permute-done.1.refs_1_
  23.3 0.0 collective-permute-done.2.refs_3_
  23.3 0.3 halve.2
  23.6 1.1 %collective-permute-start.3 = (f32[8,160,128]{2,1,0:T(8,128)S(1)}, f32[8,160,128]{2,1,0:T(8,128)S(1)}, u32[]{:S(2)}, u32[]{:S(2)}) collective-permute-start(f32[8,160,128]{2,1,0:T(8,128)S(1)} %get-tuple-element.38), channel_id=1, source_target_pairs={{0,192},{64,128},{128,64},{192,0},{1,193},{65,129},{129,65},{193,1... | collective-permute-start | bytes 1966088 | tf_op jit(solution)/shard_map/ppermute | solution.py:302
  24.7 0.6 collective-permute-start.4
  25.3 15.6 %all_to_all.26.part_ref.after_ref = f32[8,24,128]{2,1,0:T(8,128)S(1)} all-to-all(f32[8,24,128]{2,1,0:T(8,128)S(1)} %sum_spread.2), channel_id=1, replica_groups=mesh['xh'=2,'xl'=2,'yh'=2,'yl'=2,'core'=2,'z'=8] {'z'}, dimensions={0} | all-to-all | bytes 196608 | tf_op jit(solution)/shard_map/all_to_all | solution.py:306
  40.9 0.0 collective-permute-done.3.refs_1_
  40.9 0.0 collective-permute-done.4.refs_3_
  40.9 0.1 halve.3
  41.0 2.1 %collective-permute-start.5 = (f32[4,160,128]{2,1,0:T(8,128)S(1)}, f32[4,160,128]{2,1,0:T(8,128)S(1)}, u32[]{:S(2)}, u32[]{:S(2)}) collective-permute-start(f32[4,160,128]{2,1,0:T(8,128)S(1)} %get-tuple-element.42), channel_id=1, source_target_pairs={{0,48},{16,32},{32,16},{48,0},{1,49},{17,33},{33,17},{49,1},{2,50}... | collective-permute-start | bytes 983048 | tf_op jit(solution)/shard_map/ppermute | solution.py:302
  43.2 1.7 %collective-permute-start.6 = (f32[4,160,128]{2,1,0:T(8,128)S(1)}, f32[4,160,128]{2,1,0:T(8,128)S(1)}, u32[]{:S(2)}, u32[]{:S(2)}) collective-permute-start(f32[4,160,128]{2,1,0:T(8,128)S(1)} %get-tuple-element.44), channel_id=1, source_target_pairs={{0,192},{64,128},{128,64},{192,0},{1,193},{65,129},{129,65},{193,1... | collective-permute-start | bytes 983048 | tf_op jit(solution)/shard_map/ppermute | solution.py:302
  44.9 10.4 %all_to_all.27.after_ref = f32[16,24,128]{2,1,0:T(8,128)S(1)} all-to-all(f32[16,24,128]{2,1,0:T(8,128)S(1)} %sum_spread.3), channel_id=1, replica_groups=mesh['xh'=2,'xl'=2,'yh'=2,'yl'=2,'core'=2,'z'=8] {'xh','xl','yh','yl'}, dimensions={0} | all-to-all | bytes 393216 | tf_op jit(solution)/shard_map/all_to_all | solution.py:306
  55.3 0.0 collective-permute-done.5.upper_got_ref
  55.3 0.0 collective-permute-done.6.lower_got_ref
  55.3 0.9 join.1.after_ref
  56.2 3.7 %all-to-all-start.3 = ((f32[4,320,128]{2,1,0:T(8,128)}), f32[4,320,128]{2,1,0:T(8,128)S(1)}, u32[]{:S(2)}, u32[]{:S(2)}) async-start(f32[4,320,128]{2,1,0:T(8,128)} %join.1.after_ref), calls=%async_computation.3 | async-start | bytes 1310720 | tf_op jit(solution)/shard_map/all_to_all | solution.py:306
  59.8 4.9 %basis.1.basis_ref = f32[320,128]{1,0:T(8,128)S(1)} custom-call(f32[384,128]{1,0:T(8,128)S(1)} %bitcast.8, f32[4,320,128]{2,1,0:T(8,128)} %join.1.after_ref), custom_call_target="tpu_custom_call" | custom-call | flops 5000000000 | bytes 400000 | tf_op jit(solution)/shard_map/basis/pallas_call | solution.py:353
  64.7 1.1 %all-to-all-done.3.part_ref = f32[4,320,128]{2,1,0:T(8,128)S(1)} async-done(((f32[4,320,128]{2,1,0:T(8,128)}), f32[4,320,128]{2,1,0:T(8,128)S(1)}, u32[]{:S(2)}, u32[]{:S(2)}) %all-to-all-start.3) | async-done | bytes 655392 | tf_op jit(solution)/shard_map/all_to_all | solution.py:306
  65.8 0.0 copy-start
  65.8 0.4 finish.1
  66.2 13.6 %all_to_all.28 = f32[16,112,128]{2,1,0:T(8,128)S(1)} all-to-all(f32[16,112,128]{2,1,0:T(8,128)S(1)} %finish.1), channel_id=1, replica_groups=mesh['xh'=2,'xl'=2,'yh'=2,'yl'=2,'core'=2,'z'=8] {'xh','xl','yh','yl'}, dimensions={0} | all-to-all | bytes 1835008 | tf_op jit(solution)/shard_map/all_to_all | solution.py:306
  79.8 7.9 %collective-permute-start.8 = (f32[1792,128]{1,0:T(8,128)S(1)}, f32[1792,128]{1,0:T(8,128)S(1)}, u32[]{:S(2)}, u32[]{:S(2)}) collective-permute-start(f32[1792,128]{1,0:T(8,128)S(1)} %bitcast.6), channel_id=1, source_target_pairs={{0,8},{8,0},{1,9},{9,1},{2,10},{10,2},{3,11},{11,3},{4,12},{12,4},... | collective-permute-start | bytes 2752520 | tf_op jit(solution)/shard_map/ppermute | solution.py:298
  87.7 0.0 collective-permute-start.7
  87.7 0.0 copy-done
  87.7 1.8 %update_mine.1 = (f32[2,320,1792]{2,1,0:T(8,128)}, f32[2,1792,128]{2,1,0:T(8,128)}, f32[2,320,128]{2,1,0:T(8,128)}) custom-call(f32[320,128]{1,0:T(8,128)S(1)} %basis.1.basis_ref, f32[1792,128]{1,0:T(8,128)S(1)} %bitcast.7, f32[320,1792]{1,0:T(8,128)S(1)} %copy-done), custom_call_target="tpu_custom_call" | custom-call | flops 440401920 | bytes 4587520 | tf_op jit(solution)/shard_map/update_mine/pallas_call | solution.py:275
  89.5 0.5 collective-permute-done.7.basis_ref
  90.0 0.0 collective-permute-done.8.right_ref
  90.1 1.8 %update_other.1 = (f32[2,320,1792]{2,1,0:T(8,128)}, f32[2,1792,128]{2,1,0:T(8,128)}, f32[2,320,128]{2,1,0:T(8,128)}) custom-call(f32[320,128]{1,0:T(8,128)S(1)} %collective-permute-done.7.basis_ref, f32[1792,128]{1,0:T(8,128)S(1)} %collective-permute-done.8.right_ref, ...), custom_call_target="tpu_custom_call", output_to_operand_aliasing={{0}: (3, {}), {1}: (4, {}), {2}: (5, {})} | custom-call | flops 440401920 | bytes 4587520 | tf_op jit(solution)/shard_map/update_other/pallas_call | solution.py:275
  (3 shorter events, 0.1 us)
Async XLA Ops:
  6.4 4.4 %collective-permute-start = (f32[384,128]{1,0:T(8,128)S(1)}, f32[384,128]{1,0:T(8,128)S(1)}, u32[]{:S(2)}, u32[]{:S(2)}) collective-permute-start(f32[384,128]{1,0:T(8,128)S(1)} %get-tuple-element.29), channel_id=1, source_target_pairs={{0,8},{8,0},{1,9},{9,1},{2,10},{10,2},{3,11},{11,3},{4,12},{12,4},... | collective-permute-start | bytes 589832 | tf_op jit(solution)/shard_map/ppermute | solution.py:298
  10.9 12.5 %collective-permute-start.1 = (f32[16,160,128]{2,1,0:T(8,128)S(1)}, f32[16,160,128]{2,1,0:T(8,128)S(1)}, u32[]{:S(2)}, u32[]{:S(2)}) collective-permute-start(f32[16,160,128]{2,1,0:T(8,128)S(1)} %get-tuple-element.34), channel_id=1, source_target_pairs={{0,8},{8,0},{1,9},{9,1},{2,10},{10,2},{3,11},{11,3},{4,12},{12,4},... | collective-permute-start | bytes 3932168 | tf_op jit(solution)/shard_map/ppermute | solution.py:298
  11.3 12.0 %collective-permute-start.2 = (f32[16,160,128]{2,1,0:T(8,128)S(1)}, f32[16,160,128]{2,1,0:T(8,128)S(1)}, u32[]{:S(2)}, u32[]{:S(2)}) collective-permute-start(f32[16,160,128]{2,1,0:T(8,128)S(1)} %get-tuple-element.36), channel_id=1, source_target_pairs={{0,8},{8,0},{1,9},{9,1},{2,10},{10,2},{3,11},{11,3},{4,12},{12,4},... | collective-permute-start | bytes 3932168 | tf_op jit(solution)/shard_map/ppermute | solution.py:298
  23.6 17.3 %collective-permute-start.3 = (f32[8,160,128]{2,1,0:T(8,128)S(1)}, f32[8,160,128]{2,1,0:T(8,128)S(1)}, u32[]{:S(2)}, u32[]{:S(2)}) collective-permute-start(f32[8,160,128]{2,1,0:T(8,128)S(1)} %get-tuple-element.38), channel_id=1, source_target_pairs={{0,192},{64,128},{128,64},{192,0},{1,193},{65,129},{129,65},{193,1... | collective-permute-start | bytes 1966088 | tf_op jit(solution)/shard_map/ppermute | solution.py:302
  24.7 16.2 %collective-permute-start.4 = (f32[8,160,128]{2,1,0:T(8,128)S(1)}, f32[8,160,128]{2,1,0:T(8,128)S(1)}, u32[]{:S(2)}, u32[]{:S(2)}) collective-permute-start(f32[8,160,128]{2,1,0:T(8,128)S(1)} %get-tuple-element.40), channel_id=1, source_target_pairs={{0,48},{16,32},{32,16},{48,0},{1,49},{17,33},{33,17},{49,1},{2,50}... | collective-permute-start | bytes 1966088 | tf_op jit(solution)/shard_map/ppermute | solution.py:302
  41.0 14.2 %collective-permute-start.5 = (f32[4,160,128]{2,1,0:T(8,128)S(1)}, f32[4,160,128]{2,1,0:T(8,128)S(1)}, u32[]{:S(2)}, u32[]{:S(2)}) collective-permute-start(f32[4,160,128]{2,1,0:T(8,128)S(1)} %get-tuple-element.42), channel_id=1, source_target_pairs={{0,48},{16,32},{32,16},{48,0},{1,49},{17,33},{33,17},{49,1},{2,50}... | collective-permute-start | bytes 983048 | tf_op jit(solution)/shard_map/ppermute | solution.py:302
  43.2 12.1 %collective-permute-start.6 = (f32[4,160,128]{2,1,0:T(8,128)S(1)}, f32[4,160,128]{2,1,0:T(8,128)S(1)}, u32[]{:S(2)}, u32[]{:S(2)}) collective-permute-start(f32[4,160,128]{2,1,0:T(8,128)S(1)} %get-tuple-element.44), channel_id=1, source_target_pairs={{0,192},{64,128},{128,64},{192,0},{1,193},{65,129},{129,65},{193,1... | collective-permute-start | bytes 983048 | tf_op jit(solution)/shard_map/ppermute | solution.py:302
  56.2 9.6 %all-to-all-start.3 = ((f32[4,320,128]{2,1,0:T(8,128)}), f32[4,320,128]{2,1,0:T(8,128)S(1)}, u32[]{:S(2)}, u32[]{:S(2)}) async-start(f32[4,320,128]{2,1,0:T(8,128)} %join.1.after_ref), calls=%async_computation.3 | async-start | bytes 1310720 | tf_op jit(solution)/shard_map/all_to_all | solution.py:306
  65.8 21.9 %copy-start = (f32[320,1792]{1,0:T(8,128)S(1)}, f32[320,1792]{1,0:T(8,128)}, u32[]{:S(2)}) copy-start(f32[320,1792]{1,0:T(8,128)} %get-tuple-element.46.sum_ref) | copy-start | bytes 6881284
  79.8 10.2 %collective-permute-start.8 = (f32[1792,128]{1,0:T(8,128)S(1)}, f32[1792,128]{1,0:T(8,128)S(1)}, u32[]{:S(2)}, u32[]{:S(2)}) collective-permute-start(f32[1792,128]{1,0:T(8,128)S(1)} %bitcast.6), channel_id=1, source_target_pairs={{0,8},{8,0},{1,9},{9,1},{2,10},{10,2},{3,11},{11,3},{4,12},{12,4},... | collective-permute-start | bytes 2752520 | tf_op jit(solution)/shard_map/ppermute | solution.py:298
  87.7 2.3 %collective-permute-start.7 = (f32[320,128]{1,0:T(8,128)S(1)}, f32[320,128]{1,0:T(8,128)S(1)}, u32[]{:S(2)}, u32[]{:S(2)}) collective-permute-start(f32[320,128]{1,0:T(8,128)S(1)} %basis.1.basis_ref), channel_id=1, source_target_pairs={{0,8},{8,0},{1,9},{9,1},{2,10},{10,2},{3,11},{11,3},{4,12},{12,4},... | collective-permute-start | bytes 491528 | tf_op jit(solution)/shard_map/ppermute | solution.py:298

commit v7 on v6

--- a/solution.py
+++ b/solution.py
@@ -55,14 +55,20 @@
     return x - quotient * PRIME
 
 
-def start_block(seed, first, columns):
+def first_hash(columns):
+    i = lax.broadcasted_iota(jnp.int32, (columns, RANK), 0)
+    rank = lax.broadcasted_iota(jnp.int32, (columns, RANK), 1)
+    return centred(i * 131 + rank * 977)
+
+
+def start_block(hashed, seed, first):
+    columns = hashed.shape[0]
     col = first + lax.broadcasted_iota(jnp.int32, (columns, RANK), 0)
-    rank = lax.broadcasted_iota(jnp.int32, (columns, RANK), 1)
-    hashed = centred(col * 131 + rank * 977 + seed)
-    hashed = centred(hashed * hashed + rank * 17 + 7)
+    rank = lax.broadcasted_iota(jnp.int32, (1, RANK), 1)
+    hashed = hashed + centred(first * 131 + seed)
+    hashed = centred(hashed * hashed + (rank * 17 + 7))
     hashed = centred(hashed * hashed + col)
-    hashed = jnp.where(hashed < 0, hashed + PRIME, hashed)
-    return (hashed.astype(f32) * (1.0 / PRIME) - 0.5) * unit_scale
+    return hashed.astype(f32) * (unit_scale / PRIME) + jnp.where(hashed < 0, 0.5 * unit_scale, -0.5 * unit_scale)
 
 
 def places(tile):
@@ -93,8 +99,9 @@
         copies.append(pair)
     for left_ref in lefts:
         left_ref[rows:, :] = jnp.zeros((left_ref.shape[0] - rows, RANK), f32)
+    hashed = first_hash(CHUNK)
     for j in range(steps):
-        high, low = split(start_block(seed, first + j * CHUNK, CHUNK))
+        high, low = split(start_block(hashed, seed, first + j * CHUNK))
         start_ref[cols(j), :RANK] = high
         start_ref[cols(j), RANK:] = low
     saves = []
@@ -228,19 +235,28 @@
     )(after, *blocks)
 
 
-def join_kernel(after_ref, upper_ref, upper_got_ref, lower_ref, lower_got_ref, out_ref):
+def join_kernel(after_ref, upper_ref, upper_got_ref, lower_ref, lower_got_ref, out_hbm, out_ref, sems):
     del after_ref
     half = upper_ref.shape[1]
+    copies = []
     for i in range(out_ref.shape[0]):
         out_ref[i, :half, :] = upper_ref[i] + upper_got_ref[i]
         out_ref[i, half:, :] = lower_ref[i] + lower_got_ref[i]
+        copies.append(pltpu.make_async_copy(out_ref.at[i], out_hbm.at[i], sems.at[i]))
+        copies[i].start()
+    for copy in copies:
+        copy.wait()
 
 
 def finish_kernel(part_ref, basis_ref, out_ref):
     total = part_ref[0]
     for i in range(1, part_ref.shape[0]):
         total = total + part_ref[i]
-    right = exact_dot(total * (1.0 / 32), basis_ref[...], ((0,), (0,)))
+    high, low = split(total * (1.0 / 32))
+    b_high, b_low = split(basis_ref[...])
+    rows = ((0,), (0,))
+    wide = dot(high, jnp.concatenate([b_high, b_low], axis=1), rows)
+    right = wide[:, :RANK] + wide[:, RANK:] + dot(low, b_high, rows)
     for i in range(out_ref.shape[0]):
         out_ref[i] = right[: out_ref.shape[1], :]
 
@@ -345,8 +361,9 @@
     quarter = pl.pallas_call(
         join_kernel,
         in_specs=[hbm] + [vmem] * 4,
-        out_specs=vmem,
-        out_shape=pltpu.VMEM((CHIPS // 4, rows, LANES), f32),
+        out_specs=hbm,
+        out_shape=pltpu.HBM((CHIPS // 4, rows, LANES), f32),
+        scratch_shapes=[pltpu.VMEM((CHIPS // 4, rows, LANES), f32), pltpu.SemaphoreType.DMA((CHIPS // 4,))],
         compiler_params=params(4),
         name="join",
     )(left, upper, upper_got, lower, lower_got)

time: 92.3 us -> 92.1 us (level)
  local copies, waits for them, and re-layouts: 0.01 us -> 1.11 us
  waiting for transfers between devices: 2.68 us -> 1.6 us
    unnamed x2 -> x4, local copies, waits for them, and re-layouts: 0.01 us -> 1.11 us
    all_to_all x1, waiting for transfers between devices: 1.08 us -> 0.01 us  [exchange(): return lax.all_to_all(x, axes, 0, 0)]
  transfers between devices with their start and end apart: 10 -> 10, of which waited for: 3 -> 2; matrix products, arithmetic and copies ran while one was open for 0% -> 0% of each run, Pallas kernels for 7% -> 7%
where the time goes in v7:
time: 92.1 us; the launch traced here: 91.8 us
  blocking collectives  52.1 us (57%)
  starting transfers between devices  20.3 us (22%)
  Pallas kernels  15.1 us (16%)
  waiting for transfers between devices  1.6 us (2%)
  between operations  1.54 us (2%)
  local copies, waits for them, and re-layouts  1.11 us (1%)
    all_to_all x4, blocking collectives, exchange(): return lax.all_to_all(x, axes, 0, 0)  52.1 us
    ppermute x5, starting transfers between devices, swap(): return lax.ppermute(x, 'core', [(0, 1), (1, 0)])  11.1 us
    ppermute x4, starting transfers between devices, cross(): lax.ppermute(x, (axis + 'h', axis + 'l'), [(i, 3 - i) for i in range(4)])  5.53 us
    pallas_call x1, Pallas kernels, on_device(): pl.pallas_call(left_kernel, in_specs=[smem, hbm, hbm], out_specs=[vmem] *...  5 us
    pallas_call x1, Pallas kernels, on_device(): pl.pallas_call(basis_kernel, in_specs=[vmem, hbm], out_specs=vmem, out_sh...  4.87 us
    all_to_all x1, starting transfers between devices, exchange(): return lax.all_to_all(x, axes, 0, 0)  3.68 us
    pallas_call x2, Pallas kernels, update(): pl.pallas_call(functools.partial(update_kernel, slot), in_specs=[vmem] *...  3.63 us
  transfers between devices with their start and end apart: 10, of which 2 were waited for; matrix products, arithmetic and copies ran while one was open for 0% of the time, Pallas kernels for 7%

profile of v7, /device:TPU:1, one launch (start us, length us, event | category | flops | bytes accessed | tf_op | source)
XLA Modules:
  0.0 91.8 jit_solution(14571979253768640532)
XLA Ops:
  1.3 5.0 %left_part.1 = (f32[384,128]{1,0:T(8,128)S(1)}, f32[384,128]{1,0:T(8,128)S(1)}, f32[16,160,128]{2,1,0:T(8,128)S(1)}, f32[16,160,128]{2,1,0:T(8,128)S(1)}, f32[16...) custom-call(s32[1]{0:T(128)S(6)} %copy.12.seed_ref, ...), custom_call_target="tpu_custom_call" | custom-call | tf_op jit(solution)/shard_map/left_part/pallas_call | solution.py:333
  6.3 3.3 %collective-permute-start = (f32[384,128]{1,0:T(8,128)S(1)}, f32[384,128]{1,0:T(8,128)S(1)}, u32[]{:S(2)}, u32[]{:S(2)}) collective-permute-start(f32[384,128]{1,0:T(8,128)S(1)} %get-tuple-element.29), channel_id=1, source_target_pairs={{0,8},{8,0},{1,9},{9,1},{2,10},{10,2},{3,11},{11,3},{4,12},{12,4},... | collective-permute-start | bytes 589832 | tf_op jit(solution)/shard_map/ppermute | solution.py:314
  9.6 1.1 %collective-permute-done = f32[384,128]{1,0:T(8,128)S(1)} collective-permute-done((f32[384,128]{1,0:T(8,128)S(1)}, f32[384,128]{1,0:T(8,128)S(1)}, u32[]{:S(2)}, u32[]{:S(2)}) %collective-permute-start) | collective-permute-done | bytes 196640 | tf_op jit(solution)/shard_map/ppermute | solution.py:314
  10.7 0.5 collective-permute-start.1
  11.2 0.1 collective-permute-start.2
  11.3 11.9 %all_to_all.25.part_ref.after_ref = f32[16,24,128]{2,1,0:T(8,128)S(1)} all-to-all(f32[16,24,128]{2,1,0:T(8,128)S(1)} %bitcast.12), channel_id=1, replica_groups=mesh['xh'=2,'xl'=2,'yh'=2,'yl'=2,'core'=2,'z'=8] {'xh','xl','yh','yl'}, dimensions={0} | all-to-all | bytes 393216 | tf_op jit(solution)/shard_map/all_to_all | solution.py:322
  23.2 0.0 collective-permute-done.1.refs_1_
  23.2 0.0 collective-permute-done.2.refs_3_
  23.2 0.3 halve.2
  23.5 1.1 %collective-permute-start.3 = (f32[8,160,128]{2,1,0:T(8,128)S(1)}, f32[8,160,128]{2,1,0:T(8,128)S(1)}, u32[]{:S(2)}, u32[]{:S(2)}) collective-permute-start(f32[8,160,128]{2,1,0:T(8,128)S(1)} %get-tuple-element.38), channel_id=1, source_target_pairs={{0,192},{64,128},{128,64},{192,0},{1,193},{65,129},{129,65},{193,1... | collective-permute-start | bytes 1966088 | tf_op jit(solution)/shard_map/ppermute | solution.py:318
  24.5 0.6 collective-permute-start.4
  25.2 15.6 %all_to_all.26.part_ref.after_ref = f32[8,24,128]{2,1,0:T(8,128)S(1)} all-to-all(f32[8,24,128]{2,1,0:T(8,128)S(1)} %sum_spread.2), channel_id=1, replica_groups=mesh['xh'=2,'xl'=2,'yh'=2,'yl'=2,'core'=2,'z'=8] {'z'}, dimensions={0} | all-to-all | bytes 196608 | tf_op jit(solution)/shard_map/all_to_all | solution.py:322
  40.8 0.0 collective-permute-done.3.refs_1_
  40.8 0.0 collective-permute-done.4.refs_3_
  40.8 0.1 halve.3
  40.9 2.1 %collective-permute-start.5 = (f32[4,160,128]{2,1,0:T(8,128)S(1)}, f32[4,160,128]{2,1,0:T(8,128)S(1)}, u32[]{:S(2)}, u32[]{:S(2)}) collective-permute-start(f32[4,160,128]{2,1,0:T(8,128)S(1)} %get-tuple-element.42), channel_id=1, source_target_pairs={{0,48},{16,32},{32,16},{48,0},{1,49},{17,33},{33,17},{49,1},{2,50}... | collective-permute-start | bytes 983048 | tf_op jit(solution)/shard_map/ppermute | solution.py:318
  43.0 1.7 %collective-permute-start.6 = (f32[4,160,128]{2,1,0:T(8,128)S(1)}, f32[4,160,128]{2,1,0:T(8,128)S(1)}, u32[]{:S(2)}, u32[]{:S(2)}) collective-permute-start(f32[4,160,128]{2,1,0:T(8,128)S(1)} %get-tuple-element.44), channel_id=1, source_target_pairs={{0,192},{64,128},{128,64},{192,0},{1,193},{65,129},{129,65},{193,1... | collective-permute-start | bytes 983048 | tf_op jit(solution)/shard_map/ppermute | solution.py:318
  44.7 10.4 %all_to_all.27.after_ref = f32[16,24,128]{2,1,0:T(8,128)S(1)} all-to-all(f32[16,24,128]{2,1,0:T(8,128)S(1)} %sum_spread.3), channel_id=1, replica_groups=mesh['xh'=2,'xl'=2,'yh'=2,'yl'=2,'core'=2,'z'=8] {'xh','xl','yh','yl'}, dimensions={0} | all-to-all | bytes 393216 | tf_op jit(solution)/shard_map/all_to_all | solution.py:322
  55.1 0.0 collective-permute-done.5.upper_got_ref
  55.1 0.0 collective-permute-done.6.lower_got_ref
  55.1 0.9 join.1.after_ref
  56.0 3.7 %all-to-all-start.3 = ((f32[4,320,128]{2,1,0:T(8,128)}), f32[4,320,128]{2,1,0:T(8,128)S(1)}, u32[]{:S(2)}, u32[]{:S(2)}) async-start(f32[4,320,128]{2,1,0:T(8,128)} %join.1.after_ref), calls=%async_computation.3 | async-start | bytes 1310720 | tf_op jit(solution)/shard_map/all_to_all | solution.py:322
  59.7 0.0 copy-start
  59.7 1.1 %copy-done = f32[4,320,128]{2,1,0:T(8,128)S(1)} copy-done((f32[4,320,128]{2,1,0:T(8,128)S(1)}, f32[4,320,128]{2,1,0:T(8,128)}, u32[]{:S(2)}) %copy-start) | copy-done | bytes 655384
  60.8 4.9 %basis.1.basis_ref = f32[320,128]{1,0:T(8,128)S(1)} custom-call(f32[384,128]{1,0:T(8,128)S(1)} %bitcast.8, f32[4,320,128]{2,1,0:T(8,128)S(1)} %copy-done), custom_call_target="tpu_custom_call" | custom-call | flops 5000000000 | bytes 400000 | tf_op jit(solution)/shard_map/basis/pallas_call | solution.py:370
  65.7 0.0 all-to-all-done.3.part_ref
  65.7 0.0 copy-start.1
  65.7 0.3 finish.1
  66.0 14.3 %all_to_all.28 = f32[16,112,128]{2,1,0:T(8,128)S(1)} all-to-all(f32[16,112,128]{2,1,0:T(8,128)S(1)} %finish.1), channel_id=1, replica_groups=mesh['xh'=2,'xl'=2,'yh'=2,'yl'=2,'core'=2,'z'=8] {'xh','xl','yh','yl'}, dimensions={0} | all-to-all | bytes 1835008 | tf_op jit(solution)/shard_map/all_to_all | solution.py:322
  80.3 7.2 %collective-permute-start.8 = (f32[1792,128]{1,0:T(8,128)S(1)}, f32[1792,128]{1,0:T(8,128)S(1)}, u32[]{:S(2)}, u32[]{:S(2)}) collective-permute-start(f32[1792,128]{1,0:T(8,128)S(1)} %bitcast.6), channel_id=1, source_target_pairs={{0,8},{8,0},{1,9},{9,1},{2,10},{10,2},{3,11},{11,3},{4,12},{12,4},... | collective-permute-start | bytes 2752520 | tf_op jit(solution)/shard_map/ppermute | solution.py:314
  87.5 0.0 collective-permute-start.7
  87.5 0.0 copy-done.1
  87.5 1.8 %update_mine.1 = (f32[2,320,1792]{2,1,0:T(8,128)}, f32[2,1792,128]{2,1,0:T(8,128)}, f32[2,320,128]{2,1,0:T(8,128)}) custom-call(f32[320,128]{1,0:T(8,128)S(1)} %basis.1.basis_ref, f32[1792,128]{1,0:T(8,128)S(1)} %bitcast.7, f32[320,1792]{1,0:T(8,128)S(1)} %copy-done.1), custom_call_target="tpu_custom_call" | custom-call | flops 440401920 | bytes 4587520 | tf_op jit(solution)/shard_map/update_mine/pallas_call | solution.py:291
  89.3 0.5 collective-permute-done.7.basis_ref
  89.8 0.0 collective-permute-done.8.right_ref
  89.8 1.8 %update_other.1 = (f32[2,320,1792]{2,1,0:T(8,128)}, f32[2,1792,128]{2,1,0:T(8,128)}, f32[2,320,128]{2,1,0:T(8,128)}) custom-call(f32[320,128]{1,0:T(8,128)S(1)} %collective-permute-done.7.basis_ref, f32[1792,128]{1,0:T(8,128)S(1)} %collective-permute-done.8.right_ref, ...), custom_call_target="tpu_custom_call", output_to_operand_aliasing={{0}: (3, {}), {1}: (4, {}), {2}: (5, {})} | custom-call | flops 440401920 | bytes 4587520 | tf_op jit(solution)/shard_map/update_other/pallas_call | solution.py:291
  (3 shorter events, 0.1 us)
Async XLA Ops:
  6.3 4.4 %collective-permute-start = (f32[384,128]{1,0:T(8,128)S(1)}, f32[384,128]{1,0:T(8,128)S(1)}, u32[]{:S(2)}, u32[]{:S(2)}) collective-permute-start(f32[384,128]{1,0:T(8,128)S(1)} %get-tuple-element.29), channel_id=1, source_target_pairs={{0,8},{8,0},{1,9},{9,1},{2,10},{10,2},{3,11},{11,3},{4,12},{12,4},... | collective-permute-start | bytes 589832 | tf_op jit(solution)/shard_map/ppermute | solution.py:314
  10.7 12.5 %collective-permute-start.1 = (f32[16,160,128]{2,1,0:T(8,128)S(1)}, f32[16,160,128]{2,1,0:T(8,128)S(1)}, u32[]{:S(2)}, u32[]{:S(2)}) collective-permute-start(f32[16,160,128]{2,1,0:T(8,128)S(1)} %get-tuple-element.34), channel_id=1, source_target_pairs={{0,8},{8,0},{1,9},{9,1},{2,10},{10,2},{3,11},{11,3},{4,12},{12,4},... | collective-permute-start | bytes 3932168 | tf_op jit(solution)/shard_map/ppermute | solution.py:314
  11.2 12.0 %collective-permute-start.2 = (f32[16,160,128]{2,1,0:T(8,128)S(1)}, f32[16,160,128]{2,1,0:T(8,128)S(1)}, u32[]{:S(2)}, u32[]{:S(2)}) collective-permute-start(f32[16,160,128]{2,1,0:T(8,128)S(1)} %get-tuple-element.36), channel_id=1, source_target_pairs={{0,8},{8,0},{1,9},{9,1},{2,10},{10,2},{3,11},{11,3},{4,12},{12,4},... | collective-permute-start | bytes 3932168 | tf_op jit(solution)/shard_map/ppermute | solution.py:314
  23.5 17.3 %collective-permute-start.3 = (f32[8,160,128]{2,1,0:T(8,128)S(1)}, f32[8,160,128]{2,1,0:T(8,128)S(1)}, u32[]{:S(2)}, u32[]{:S(2)}) collective-permute-start(f32[8,160,128]{2,1,0:T(8,128)S(1)} %get-tuple-element.38), channel_id=1, source_target_pairs={{0,192},{64,128},{128,64},{192,0},{1,193},{65,129},{129,65},{193,1... | collective-permute-start | bytes 1966088 | tf_op jit(solution)/shard_map/ppermute | solution.py:318
  24.5 16.2 %collective-permute-start.4 = (f32[8,160,128]{2,1,0:T(8,128)S(1)}, f32[8,160,128]{2,1,0:T(8,128)S(1)}, u32[]{:S(2)}, u32[]{:S(2)}) collective-permute-start(f32[8,160,128]{2,1,0:T(8,128)S(1)} %get-tuple-element.40), channel_id=1, source_target_pairs={{0,48},{16,32},{32,16},{48,0},{1,49},{17,33},{33,17},{49,1},{2,50}... | collective-permute-start | bytes 1966088 | tf_op jit(solution)/shard_map/ppermute | solution.py:318
  40.9 14.2 %collective-permute-start.5 = (f32[4,160,128]{2,1,0:T(8,128)S(1)}, f32[4,160,128]{2,1,0:T(8,128)S(1)}, u32[]{:S(2)}, u32[]{:S(2)}) collective-permute-start(f32[4,160,128]{2,1,0:T(8,128)S(1)} %get-tuple-element.42), channel_id=1, source_target_pairs={{0,48},{16,32},{32,16},{48,0},{1,49},{17,33},{33,17},{49,1},{2,50}... | collective-permute-start | bytes 983048 | tf_op jit(solution)/shard_map/ppermute | solution.py:318
  43.0 12.1 %collective-permute-start.6 = (f32[4,160,128]{2,1,0:T(8,128)S(1)}, f32[4,160,128]{2,1,0:T(8,128)S(1)}, u32[]{:S(2)}, u32[]{:S(2)}) collective-permute-start(f32[4,160,128]{2,1,0:T(8,128)S(1)} %get-tuple-element.44), channel_id=1, source_target_pairs={{0,192},{64,128},{128,64},{192,0},{1,193},{65,129},{129,65},{193,1... | collective-permute-start | bytes 983048 | tf_op jit(solution)/shard_map/ppermute | solution.py:318
  56.0 9.7 %all-to-all-start.3 = ((f32[4,320,128]{2,1,0:T(8,128)}), f32[4,320,128]{2,1,0:T(8,128)S(1)}, u32[]{:S(2)}, u32[]{:S(2)}) async-start(f32[4,320,128]{2,1,0:T(8,128)} %join.1.after_ref), calls=%async_computation.3 | async-start | bytes 1310720 | tf_op jit(solution)/shard_map/all_to_all | solution.py:322
  59.7 1.1 %copy-start = (f32[4,320,128]{2,1,0:T(8,128)S(1)}, f32[4,320,128]{2,1,0:T(8,128)}, u32[]{:S(2)}) copy-start(f32[4,320,128]{2,1,0:T(8,128)} %join.1.after_ref) | copy-start | bytes 1966084
  65.7 21.8 %copy-start.1 = (f32[320,1792]{1,0:T(8,128)S(1)}, f32[320,1792]{1,0:T(8,128)}, u32[]{:S(2)}) copy-start(f32[320,1792]{1,0:T(8,128)} %get-tuple-element.46.sum_ref) | copy-start | bytes 6881284
  80.3 9.5 %collective-permute-start.8 = (f32[1792,128]{1,0:T(8,128)S(1)}, f32[1792,128]{1,0:T(8,128)S(1)}, u32[]{:S(2)}, u32[]{:S(2)}) collective-permute-start(f32[1792,128]{1,0:T(8,128)S(1)} %bitcast.6), channel_id=1, source_target_pairs={{0,8},{8,0},{1,9},{9,1},{2,10},{10,2},{3,11},{11,3},{4,12},{12,4},... | collective-permute-start | bytes 2752520 | tf_op jit(solution)/shard_map/ppermute | solution.py:314
  87.5 2.3 %collective-permute-start.7 = (f32[320,128]{1,0:T(8,128)S(1)}, f32[320,128]{1,0:T(8,128)S(1)}, u32[]{:S(2)}, u32[]{:S(2)}) collective-permute-start(f32[320,128]{1,0:T(8,128)S(1)} %basis.1.basis_ref), channel_id=1, source_target_pairs={{0,8},{8,0},{1,9},{9,1},{2,10},{10,2},{3,11},{11,3},{4,12},{12,4},... | collective-permute-start | bytes 491528 | tf_op jit(solution)/shard_map/ppermute | solution.py:314

commit v8 on v7

--- a/solution.py
+++ b/solution.py
@@ -79,8 +79,8 @@
 
 
 def left_kernel(seed_ref, grad_hbm, feed_hbm, *refs):
-    lefts, uppers, lowers, sums = (refs[n : n + 2] for n in range(0, 8, 2))
-    grad_ref, feed_ref, start_ref, sems = refs[8:]
+    lefts, (upper_ref, lower_ref, tiles_ref), sums = refs[:2], refs[2:5], refs[5:7]
+    grad_ref, feed_ref, start_ref, sems = refs[7:]
     _, rows, columns = grad_ref.shape
     half = rows // 2
     width = columns // CHIPS
@@ -128,8 +128,12 @@
                 if end - begin < LANES:
                     block = jnp.concatenate([block, jnp.zeros((rows, LANES - end + begin), f32)], axis=1)
                 upper, lower = places(tile)
-                uppers[slot][upper] = block[:half]
-                lowers[slot][lower] = block[half:]
+                if slot:
+                    tiles_ref[upper, :half, :] = block[:half]
+                    tiles_ref[lower, half:, :] = block[half:]
+                else:
+                    upper_ref[upper] = block[:half]
+                    lower_ref[lower] = block[half:]
             s_high, s_low = split(summed)
             wide = dot(s_high, both)
             piece = wide[:, :RANK] + wide[:, RANK:] + dot(s_low, both[:, :RANK])
@@ -223,11 +227,17 @@
             send_ref[i] = kept_ref[count + i] + got_ref[count + i]
 
 
+def first_halve_kernel(after_ref, upper_ref, lower_ref, got_ref, *outs):
+    half = upper_ref.shape[1]
+    got = got_ref.at[:, :half, :], got_ref.at[:, half:, :]
+    halve_kernel(after_ref, upper_ref, got[0], lower_ref, got[1], *outs)
+
+
 def halve(after, *blocks):
     shape = (blocks[0].shape[0] // 2,) + blocks[0].shape[1:]
     return pl.pallas_call(
-        halve_kernel,
-        in_specs=[hbm] + [vmem] * 4,
+        halve_kernel if len(blocks) == 4 else first_halve_kernel,
+        in_specs=[hbm] + [vmem] * len(blocks),
         out_specs=[vmem] * 4,
         out_shape=[pltpu.VMEM(shape, f32)] * 4,
         compiler_params=params(4),
@@ -330,12 +340,13 @@
     share = -(-rows // (CHIPS * TILE)) * TILE
     padded = CHIPS * share
 
-    mine, other, upper, upper_other, lower, lower_other, summed, summed_other = pl.pallas_call(
+    mine, other, upper, lower, tiles_other, summed, summed_other = pl.pallas_call(
         left_kernel,
         in_specs=[smem, hbm, hbm],
-        out_specs=[vmem] * 6 + [hbm, vmem],
+        out_specs=[vmem] * 5 + [hbm, vmem],
         out_shape=[pltpu.VMEM((padded, RANK), f32)] * 2
-        + [pltpu.VMEM((CHIPS, rows // 2, LANES), f32)] * 4
+        + [pltpu.VMEM((CHIPS, rows // 2, LANES), f32)] * 2
+        + [pltpu.VMEM((CHIPS, rows, LANES), f32)]
         + [pltpu.HBM((rows, columns), f32), pltpu.VMEM((rows, columns), f32)],
         scratch_shapes=[
             pltpu.VMEM((mats, rows, columns), bf16),
@@ -348,10 +359,10 @@
     )(seed_value, gradients, feedback)
 
     left = mine + swap(other)
-    left, upper_other, lower_other = lax.optimization_barrier((left, upper_other, lower_other))
-    upper_got, lower_got = swap(upper_other), swap(lower_other)
+    left, tiles_other = lax.optimization_barrier((left, tiles_other))
+    tiles_got = swap(tiles_other)
     left = exchange(left.reshape(CHIPS, share, RANK))
-    upper, upper_send, lower, lower_send = halve(left, upper, upper_got, lower, lower_got)
+    upper, upper_send, lower, lower_send = halve(left, upper, lower, tiles_got)
     upper_got, lower_got = cross(upper_send, "x"), cross(lower_send, "y")
     left = exchange(sum_spread(left, depth), "z")
     upper, upper_send, lower, lower_send = halve(left, upper, upper_got, lower, lower_got)

time: 92.1 us -> 91.9 us (level)
    ppermute x5 -> x4, starting transfers between devices: 11.1 us -> 11 us  [swap(): return lax.ppermute(x, 'core', [(0, 1), (1, 0)])]
  transfers between devices with their start and end apart: 10 -> 9, of which waited for: 2 -> 2; matrix products, arithmetic and copies ran while one was open for 0% -> 0% of each run, Pallas kernels for 7% -> 7%
where the time goes in v8:
time: 91.9 us; the launch traced here: 91.6 us
  blocking collectives  52 us (57%)
  starting transfers between devices  20.2 us (22%)
  Pallas kernels  15.1 us (16%)
  waiting for transfers between devices  1.6 us (2%)
  between operations  1.54 us (2%)
  local copies, waits for them, and re-layouts  1.11 us (1%)
    all_to_all x4, blocking collectives, exchange(): return lax.all_to_all(x, axes, 0, 0)  52 us
    ppermute x4, starting transfers between devices, swap(): return lax.ppermute(x, 'core', [(0, 1), (1, 0)])  11 us
    ppermute x4, starting transfers between devices, cross(): lax.ppermute(x, (axis + 'h', axis + 'l'), [(i, 3 - i) for i in range(4)])  5.53 us
    pallas_call x1, Pallas kernels, on_device(): pl.pallas_call(left_kernel, in_specs=[smem, hbm, hbm], out_specs=[vmem] *...  5 us
    pallas_call x1, Pallas kernels, on_device(): pl.pallas_call(basis_kernel, in_specs=[vmem, hbm], out_specs=vmem, out_sh...  4.87 us
    all_to_all x1, starting transfers between devices, exchange(): return lax.all_to_all(x, axes, 0, 0)  3.68 us
    pallas_call x2, Pallas kernels, update(): pl.pallas_call(functools.partial(update_kernel, slot), in_specs=[vmem] *...  3.63 us
  transfers between devices with their start and end apart: 9, of which 2 were waited for; matrix products, arithmetic and copies ran while one was open for 0% of the time, Pallas kernels for 7%

profile of v8, /device:TPU:1, one launch (start us, length us, event | category | flops | bytes accessed | tf_op | source)
XLA Modules:
  0.0 91.6 jit_solution(354231034264668671)
XLA Ops:
  1.3 5.0 %left_part.1 = (f32[384,128]{1,0:T(8,128)S(1)}, f32[384,128]{1,0:T(8,128)S(1)}, f32[16,160,128]{2,1,0:T(8,128)S(1)}, f32[16,160,128]{2,1,0:T(8,128)S(1)}, f32[16...) custom-call(s32[1]{0:T(128)S(6)} %copy.12.seed_ref, bf16[2,320,1792]{2,1,0:T(8,128)(2,1)} %bitcast.11, ...), custom_call_target="tpu_custom_call" | custom-call | tf_op jit(solution)/shard_map/left_part/pallas_call | solution.py:343
  6.3 3.3 %collective-permute-start = (f32[384,128]{1,0:T(8,128)S(1)}, f32[384,128]{1,0:T(8,128)S(1)}, u32[]{:S(2)}, u32[]{:S(2)}) collective-permute-start(f32[384,128]{1,0:T(8,128)S(1)} %get-tuple-element.27), channel_id=1, source_target_pairs={{0,8},{8,0},{1,9},{9,1},{2,10},{10,2},{3,11},{11,3},{4,12},{12,4},... | collective-permute-start | bytes 589832 | tf_op jit(solution)/shard_map/ppermute | solution.py:324
  9.6 1.1 %collective-permute-done = f32[384,128]{1,0:T(8,128)S(1)} collective-permute-done((f32[384,128]{1,0:T(8,128)S(1)}, f32[384,128]{1,0:T(8,128)S(1)}, u32[]{:S(2)}, u32[]{:S(2)}) %collective-permute-start) | collective-permute-done | bytes 196640 | tf_op jit(solution)/shard_map/ppermute | solution.py:324
  10.7 0.5 collective-permute-start.1
  11.2 11.8 %all_to_all.25.part_ref.after_ref = f32[16,24,128]{2,1,0:T(8,128)S(1)} all-to-all(f32[16,24,128]{2,1,0:T(8,128)S(1)} %bitcast.12), channel_id=1, replica_groups=mesh['xh'=2,'xl'=2,'yh'=2,'yl'=2,'core'=2,'z'=8] {'xh','xl','yh','yl'}, dimensions={0} | all-to-all | bytes 393216 | tf_op jit(solution)/shard_map/all_to_all | solution.py:332
  23.0 0.0 collective-permute-done.1.got_ref
  23.0 0.3 halve.2
  23.3 1.3 %collective-permute-start.2 = (f32[8,160,128]{2,1,0:T(8,128)S(1)}, f32[8,160,128]{2,1,0:T(8,128)S(1)}, u32[]{:S(2)}, u32[]{:S(2)}) collective-permute-start(f32[8,160,128]{2,1,0:T(8,128)S(1)} %get-tuple-element.34), channel_id=1, source_target_pairs={{0,192},{64,128},{128,64},{192,0},{1,193},{65,129},{129,65},{193,1... | collective-permute-start | bytes 1966088 | tf_op jit(solution)/shard_map/ppermute | solution.py:328
  24.6 0.5 collective-permute-start.3
  25.1 15.6 %all_to_all.26.part_ref.after_ref = f32[8,24,128]{2,1,0:T(8,128)S(1)} all-to-all(f32[8,24,128]{2,1,0:T(8,128)S(1)} %sum_spread.2), channel_id=1, replica_groups=mesh['xh'=2,'xl'=2,'yh'=2,'yl'=2,'core'=2,'z'=8] {'z'}, dimensions={0} | all-to-all | bytes 196608 | tf_op jit(solution)/shard_map/all_to_all | solution.py:332
  40.6 0.0 collective-permute-done.2.refs_1_
  40.7 0.0 collective-permute-done.3.refs_3_
  40.7 0.1 halve.3
  40.8 2.4 %collective-permute-start.4 = (f32[4,160,128]{2,1,0:T(8,128)S(1)}, f32[4,160,128]{2,1,0:T(8,128)S(1)}, u32[]{:S(2)}, u32[]{:S(2)}) collective-permute-start(f32[4,160,128]{2,1,0:T(8,128)S(1)} %get-tuple-element.38), channel_id=1, source_target_pairs={{0,48},{16,32},{32,16},{48,0},{1,49},{17,33},{33,17},{49,1},{2,50}... | collective-permute-start | bytes 983048 | tf_op jit(solution)/shard_map/ppermute | solution.py:328
  43.2 1.3 %collective-permute-start.5 = (f32[4,160,128]{2,1,0:T(8,128)S(1)}, f32[4,160,128]{2,1,0:T(8,128)S(1)}, u32[]{:S(2)}, u32[]{:S(2)}) collective-permute-start(f32[4,160,128]{2,1,0:T(8,128)S(1)} %get-tuple-element.40), channel_id=1, source_target_pairs={{0,192},{64,128},{128,64},{192,0},{1,193},{65,129},{129,65},{193,1... | collective-permute-start | bytes 983048 | tf_op jit(solution)/shard_map/ppermute | solution.py:328
  44.5 10.4 %all_to_all.27.after_ref = f32[16,24,128]{2,1,0:T(8,128)S(1)} all-to-all(f32[16,24,128]{2,1,0:T(8,128)S(1)} %sum_spread.3), channel_id=1, replica_groups=mesh['xh'=2,'xl'=2,'yh'=2,'yl'=2,'core'=2,'z'=8] {'xh','xl','yh','yl'}, dimensions={0} | all-to-all | bytes 393216 | tf_op jit(solution)/shard_map/all_to_all | solution.py:332
  54.9 0.0 collective-permute-done.4.upper_got_ref
  54.9 0.0 collective-permute-done.5.lower_got_ref
  54.9 0.9 join.1.after_ref
  55.8 3.7 %all-to-all-start.3 = ((f32[4,320,128]{2,1,0:T(8,128)}), f32[4,320,128]{2,1,0:T(8,128)S(1)}, u32[]{:S(2)}, u32[]{:S(2)}) async-start(f32[4,320,128]{2,1,0:T(8,128)} %join.1.after_ref), calls=%async_computation.3 | async-start | bytes 1310720 | tf_op jit(solution)/shard_map/all_to_all | solution.py:332
  59.5 0.0 copy-start
  59.5 1.1 %copy-done = f32[4,320,128]{2,1,0:T(8,128)S(1)} copy-done((f32[4,320,128]{2,1,0:T(8,128)S(1)}, f32[4,320,128]{2,1,0:T(8,128)}, u32[]{:S(2)}) %copy-start) | copy-done | bytes 655384
  60.6 4.9 %basis.1.basis_ref = f32[320,128]{1,0:T(8,128)S(1)} custom-call(f32[384,128]{1,0:T(8,128)S(1)} %bitcast.8, f32[4,320,128]{2,1,0:T(8,128)S(1)} %copy-done), custom_call_target="tpu_custom_call" | custom-call | flops 5000000000 | bytes 400000 | tf_op jit(solution)/shard_map/basis/pallas_call | solution.py:381
  65.5 0.0 all-to-all-done.3.part_ref
  65.5 0.0 copy-start.1
  65.5 0.3 finish.1
  65.8 14.3 %all_to_all.28 = f32[16,112,128]{2,1,0:T(8,128)S(1)} all-to-all(f32[16,112,128]{2,1,0:T(8,128)S(1)} %finish.1), channel_id=1, replica_groups=mesh['xh'=2,'xl'=2,'yh'=2,'yl'=2,'core'=2,'z'=8] {'xh','xl','yh','yl'}, dimensions={0} | all-to-all | bytes 1835008 | tf_op jit(solution)/shard_map/all_to_all | solution.py:332
  80.1 7.2 %collective-permute-start.7 = (f32[1792,128]{1,0:T(8,128)S(1)}, f32[1792,128]{1,0:T(8,128)S(1)}, u32[]{:S(2)}, u32[]{:S(2)}) collective-permute-start(f32[1792,128]{1,0:T(8,128)S(1)} %bitcast.6), channel_id=1, source_target_pairs={{0,8},{8,0},{1,9},{9,1},{2,10},{10,2},{3,11},{11,3},{4,12},{12,4},... | collective-permute-start | bytes 2752520 | tf_op jit(solution)/shard_map/ppermute | solution.py:324
  87.3 0.0 collective-permute-start.6
  87.3 0.0 copy-done.1
  87.3 1.8 %update_mine.1 = (f32[2,320,1792]{2,1,0:T(8,128)}, f32[2,1792,128]{2,1,0:T(8,128)}, f32[2,320,128]{2,1,0:T(8,128)}) custom-call(f32[320,128]{1,0:T(8,128)S(1)} %basis.1.basis_ref, f32[1792,128]{1,0:T(8,128)S(1)} %bitcast.7, f32[320,1792]{1,0:T(8,128)S(1)} %copy-done.1), custom_call_target="tpu_custom_call" | custom-call | flops 440401920 | bytes 4587520 | tf_op jit(solution)/shard_map/update_mine/pallas_call | solution.py:301
  89.1 0.5 collective-permute-done.6.basis_ref
  89.6 0.0 collective-permute-done.7.right_ref
  89.6 1.8 %update_other.1 = (f32[2,320,1792]{2,1,0:T(8,128)}, f32[2,1792,128]{2,1,0:T(8,128)}, f32[2,320,128]{2,1,0:T(8,128)}) custom-call(f32[320,128]{1,0:T(8,128)S(1)} %collective-permute-done.6.basis_ref, f32[1792,128]{1,0:T(8,128)S(1)} %collective-permute-done.7.right_ref, ...), custom_call_target="tpu_custom_call", output_to_operand_aliasing={{0}: (3, {}), {1}: (4, {}), {2}: (5, {})} | custom-call | flops 440401920 | bytes 4587520 | tf_op jit(solution)/shard_map/update_other/pallas_call | solution.py:301
  (3 shorter events, 0.1 us)
Async XLA Ops:
  6.3 4.4 %collective-permute-start = (f32[384,128]{1,0:T(8,128)S(1)}, f32[384,128]{1,0:T(8,128)S(1)}, u32[]{:S(2)}, u32[]{:S(2)}) collective-permute-start(f32[384,128]{1,0:T(8,128)S(1)} %get-tuple-element.27), channel_id=1, source_target_pairs={{0,8},{8,0},{1,9},{9,1},{2,10},{10,2},{3,11},{11,3},{4,12},{12,4},... | collective-permute-start | bytes 589832 | tf_op jit(solution)/shard_map/ppermute | solution.py:324
  10.7 12.3 %collective-permute-start.1 = (f32[16,320,128]{2,1,0:T(8,128)S(1)}, f32[16,320,128]{2,1,0:T(8,128)S(1)}, u32[]{:S(2)}, u32[]{:S(2)}) collective-permute-start(f32[16,320,128]{2,1,0:T(8,128)S(1)} %get-tuple-element.32), channel_id=1, source_target_pairs={{0,8},{8,0},{1,9},{9,1},{2,10},{10,2},{3,11},{11,3},{4,12},{12,4},... | collective-permute-start | bytes 7864328 | tf_op jit(solution)/shard_map/ppermute | solution.py:324
  23.3 17.4 %collective-permute-start.2 = (f32[8,160,128]{2,1,0:T(8,128)S(1)}, f32[8,160,128]{2,1,0:T(8,128)S(1)}, u32[]{:S(2)}, u32[]{:S(2)}) collective-permute-start(f32[8,160,128]{2,1,0:T(8,128)S(1)} %get-tuple-element.34), channel_id=1, source_target_pairs={{0,192},{64,128},{128,64},{192,0},{1,193},{65,129},{129,65},{193,1... | collective-permute-start | bytes 1966088 | tf_op jit(solution)/shard_map/ppermute | solution.py:328
  24.6 16.1 %collective-permute-start.3 = (f32[8,160,128]{2,1,0:T(8,128)S(1)}, f32[8,160,128]{2,1,0:T(8,128)S(1)}, u32[]{:S(2)}, u32[]{:S(2)}) collective-permute-start(f32[8,160,128]{2,1,0:T(8,128)S(1)} %get-tuple-element.36), channel_id=1, source_target_pairs={{0,48},{16,32},{32,16},{48,0},{1,49},{17,33},{33,17},{49,1},{2,50}... | collective-permute-start | bytes 1966088 | tf_op jit(solution)/shard_map/ppermute | solution.py:328
  40.8 14.1 %collective-permute-start.4 = (f32[4,160,128]{2,1,0:T(8,128)S(1)}, f32[4,160,128]{2,1,0:T(8,128)S(1)}, u32[]{:S(2)}, u32[]{:S(2)}) collective-permute-start(f32[4,160,128]{2,1,0:T(8,128)S(1)} %get-tuple-element.38), channel_id=1, source_target_pairs={{0,48},{16,32},{32,16},{48,0},{1,49},{17,33},{33,17},{49,1},{2,50}... | collective-permute-start | bytes 983048 | tf_op jit(solution)/shard_map/ppermute | solution.py:328
  43.2 11.8 %collective-permute-start.5 = (f32[4,160,128]{2,1,0:T(8,128)S(1)}, f32[4,160,128]{2,1,0:T(8,128)S(1)}, u32[]{:S(2)}, u32[]{:S(2)}) collective-permute-start(f32[4,160,128]{2,1,0:T(8,128)S(1)} %get-tuple-element.40), channel_id=1, source_target_pairs={{0,192},{64,128},{128,64},{192,0},{1,193},{65,129},{129,65},{193,1... | collective-permute-start | bytes 983048 | tf_op jit(solution)/shard_map/ppermute | solution.py:328
  55.8 9.7 %all-to-all-start.3 = ((f32[4,320,128]{2,1,0:T(8,128)}), f32[4,320,128]{2,1,0:T(8,128)S(1)}, u32[]{:S(2)}, u32[]{:S(2)}) async-start(f32[4,320,128]{2,1,0:T(8,128)} %join.1.after_ref), calls=%async_computation.3 | async-start | bytes 1310720 | tf_op jit(solution)/shard_map/all_to_all | solution.py:332
  59.5 1.1 %copy-start = (f32[4,320,128]{2,1,0:T(8,128)S(1)}, f32[4,320,128]{2,1,0:T(8,128)}, u32[]{:S(2)}) copy-start(f32[4,320,128]{2,1,0:T(8,128)} %join.1.after_ref) | copy-start | bytes 1966084
  65.5 21.8 %copy-start.1 = (f32[320,1792]{1,0:T(8,128)S(1)}, f32[320,1792]{1,0:T(8,128)}, u32[]{:S(2)}) copy-start(f32[320,1792]{1,0:T(8,128)} %get-tuple-element.42.sum_ref) | copy-start | bytes 6881284
  80.1 9.5 %collective-permute-start.7 = (f32[1792,128]{1,0:T(8,128)S(1)}, f32[1792,128]{1,0:T(8,128)S(1)}, u32[]{:S(2)}, u32[]{:S(2)}) collective-permute-start(f32[1792,128]{1,0:T(8,128)S(1)} %bitcast.6), channel_id=1, source_target_pairs={{0,8},{8,0},{1,9},{9,1},{2,10},{10,2},{3,11},{11,3},{4,12},{12,4},... | collective-permute-start | bytes 2752520 | tf_op jit(solution)/shard_map/ppermute | solution.py:324
  87.3 2.3 %collective-permute-start.6 = (f32[320,128]{1,0:T(8,128)S(1)}, f32[320,128]{1,0:T(8,128)S(1)}, u32[]{:S(2)}, u32[]{:S(2)}) collective-permute-start(f32[320,128]{1,0:T(8,128)S(1)} %basis.1.basis_ref), channel_id=1, source_target_pairs={{0,8},{8,0},{1,9},{9,1},{2,10},{10,2},{3,11},{11,3},{4,12},{12,4},... | collective-permute-start | bytes 491528 | tf_op jit(solution)/shard_map/ppermute | solution.py:324
